TPU v7x, 32 devices: a whole 2x2x4 slice. The times are simulated.
32 devices in a mesh: ctx: 4 (over z), row: 2 (over x), col: 4 (over y, core).
Axes of the slice: x: 2, y: 2, z: 4, core: 2. Of those that a mesh axis runs over, the one named last changes fastest.
Arguments:
- tokens: bfloat16 [1024, 8192], P('ctx', 'row'), may hold values from -6 to 6
- proj_x: bfloat16 [8192, 8192], P('row', 'col'), may hold values from -0.09375 to 0.09375
- proj_z: bfloat16 [8192, 8192], P('row', 'col'), may hold values from -0.0625 to 0.0625
- proj_bc: bfloat16 [8192, 256], P('row'), may hold values from -0.015625 to 0.015625
- proj_dt: bfloat16 [8192, 128], P('row', 'col'), may hold values from -0.0625 to 0.0625
- dt_bias: float32 [128], P('col'), may hold values from -1.5 to 0.5
- decay_rate: float32 [128], P('col'), may hold values from 0.00048828125 to 0.2
- skip_gain: float32 [128], P('col'), may hold values from 0.5 to 1.5
- conv_x: float32 [8192, 4], P('col'), may hold values from -3 to 3
- conv_bc: float32 [256, 4], replicated, may hold values from -3 to 3
- norm_gain: float32 [8192], P('col'), may hold values from 0.1 to 1.9
- proj_out: bfloat16 [8192, 8192], P('col', 'row'), may hold values from -0.09375 to 0.09375
Outputs:
- layer_out: bfloat16 [1024, 8192], P('ctx', ('row', 'col'))
All inputs are finite; a program needn't handle non-finite values.
Results may differ from a plain program's by a relative error of at most 0.03.
Values may be sent and summed in bfloat16 or wider, within the bound.
No kernel may reach another device: no remote copies, remote signals or barrier semaphores. Data moves between devices by JAX's collectives and lax.ppermute only.
A program may use at most 128 MiB of HBM per device.

v0:
```python
import jax
import jax.numpy as jnp
from jax import lax
from jax.sharding import PartitionSpec as P

Q = 256


highest_mode = lax.Precision.HIGHEST


def shifted(shard, axis, by):
    devices = lax.axis_size(axis)
    pairs = [(i, i + by) for i in range(devices) if 0 <= i + by < devices]
    return lax.ppermute(shard, axis, pairs)


def local(
    tokens,
    proj_x,
    proj_z,
    proj_bc,
    proj_dt,
    dt_bias,
    decay_rate,
    skip_gain,
    conv_x,
    conv_bc,
    norm_gain,
    proj_out,
):
    tok_count = tokens.shape[0]
    col_heads = proj_dt.shape[1]
    head_dim = proj_x.shape[1] // col_heads
    state_dim = proj_bc.shape[1] // 2
    tap_count = conv_bc.shape[1]
    group_count = tok_count // Q
    bc_term = jnp.einsum("dc,td->ct", proj_bc, tokens, preferred_element_type=jnp.float32)
    local_heads = col_heads // lax.axis_size("row")
    first_head = lax.axis_index("row") * local_heads
    x_part = jnp.einsum("dc,td->ct", proj_x, tokens, preferred_element_type=jnp.float32).reshape(
        local_heads * lax.axis_size("row"), head_dim, tok_count
    )
    z_part = jnp.einsum("dc,td->ct", proj_z, tokens, preferred_element_type=jnp.float32).reshape(
        local_heads * lax.axis_size("row"), head_dim, tok_count
    )
    dt_part = jnp.einsum("dc,td->ct", proj_dt, tokens, preferred_element_type=jnp.float32).reshape(
        local_heads * lax.axis_size("row"), 1, tok_count
    )
    head_sum = lax.psum_scatter(
        jnp.concatenate([x_part, z_part, dt_part], axis=1).astype(jnp.bfloat16),
        "row",
        scatter_dimension=0,
        tiled=True,
    )
    bc_sum = lax.psum(bc_term.astype(jnp.bfloat16), "row")
    channels = local_heads * head_dim
    z_in = head_sum[:, head_dim : 2 * head_dim]
    dt_in = head_sum[:, 2 * head_dim]
    flat_in = jnp.concatenate([head_sum[:, :head_dim].reshape(channels, tok_count), bc_sum], axis=0)
    prior = shifted(flat_in[:, tok_count - tap_count + 1 :], "ctx", 1)
    padded = jnp.concatenate([prior, flat_in], axis=1).astype(jnp.float32)
    kernel = jnp.concatenate(
        [lax.dynamic_slice_in_dim(conv_x, first_head * head_dim, channels, 0), conv_bc], axis=0
    )
    running = jnp.zeros(flat_in.shape, jnp.float32)
    for tap_index in range(tap_count):
        running = (
            running
            + kernel[:, tap_index : tap_index + 1] * padded[:, tap_index : tap_index + tok_count]
        )
    conv_out = jax.nn.silu(running)
    x_conv = conv_out[:channels].reshape(local_heads, head_dim, tok_count)
    b_blocks = conv_out[channels : channels + state_dim].reshape(state_dim, group_count, Q)
    c_blocks = conv_out[channels + state_dim :].reshape(state_dim, group_count, Q)
    bias_now = lax.dynamic_slice_in_dim(dt_bias, first_head, local_heads, 0)
    decay_now = lax.dynamic_slice_in_dim(decay_rate, first_head, local_heads, 0)
    skip_now = lax.dynamic_slice_in_dim(skip_gain, first_head, local_heads, 0)
    gain_now = lax.dynamic_slice_in_dim(norm_gain, first_head * head_dim, channels, 0).reshape(
        local_heads, head_dim, 1
    )
    dt_full = jax.nn.softplus(dt_in.astype(jnp.float32) + bias_now[:, None])
    log_decay = -decay_now[:, None] * dt_full
    x_scaled = x_conv * dt_full[:, None, :]
    cum_decay = jnp.cumsum(log_decay.reshape(local_heads, group_count, Q), axis=2)
    x_blocks = x_scaled.reshape(local_heads, head_dim, group_count, Q)
    scores = jnp.einsum("nci,ncj->cij", c_blocks, b_blocks, precision=highest_mode)
    lower_mask = jnp.arange(Q)[:, None] >= jnp.arange(Q)[None, :]
    log_gap = cum_decay[:, :, :, None] - cum_decay[:, :, None, :]
    weights = jnp.where(lower_mask, jnp.exp(jnp.where(lower_mask, log_gap, 0.0)), 0.0)
    inner_out = jnp.einsum(
        "hcij,hpcj->hpci", scores[None] * weights, x_blocks, precision=highest_mode
    )
    tail_weight = jnp.exp(cum_decay[:, :, -1:] - cum_decay)
    group_states = jnp.einsum(
        "hcj,hpcj,ncj->chpn", tail_weight, x_blocks, b_blocks, precision=highest_mode
    )
    group_logs = cum_decay[:, :, -1].T

    def group_step(carried, step_inputs):
        group_log, group_state = step_inputs
        return (jnp.exp(group_log)[:, None, None] * carried + group_state, carried)

    start_state = jnp.zeros((local_heads, head_dim, state_dim), jnp.float32)
    final_state, local_enter = lax.scan(group_step, start_state, (group_logs, group_states))
    device_log = jnp.sum(group_logs, axis=0)
    before_logs = jnp.cumsum(group_logs, axis=0) - group_logs
    log_all, state_all = (
        lax.all_gather(device_log[None].astype(jnp.bfloat16), "ctx", axis=0, tiled=True).astype(
            jnp.float32
        ),
        lax.all_gather(final_state[None].astype(jnp.bfloat16), "ctx", axis=0, tiled=True).astype(
            jnp.float32
        ),
    )
    my_index = lax.axis_index("ctx")
    earlier_mask = (jnp.arange(log_all.shape[0], dtype=jnp.int32) < my_index)[:, None]
    log_prefix = jnp.cumsum(log_all, axis=0)
    up_to_me = jnp.sum(jnp.where(earlier_mask, log_all, 0.0), axis=0)
    reach_weight = jnp.where(
        earlier_mask, jnp.exp(jnp.where(earlier_mask, up_to_me - log_prefix, 0.0)), 0.0
    )
    device_state = jnp.einsum("jh,jhpn->hpn", reach_weight, state_all, precision=highest_mode)
    enter_state = jnp.exp(before_logs)[:, :, None, None] * device_state[None] + local_enter
    outer_out = jnp.exp(cum_decay)[:, None] * jnp.einsum(
        "nci,chpn->hpci", c_blocks, enter_state, precision=highest_mode
    )
    ssm_out = (inner_out + outer_out).reshape(local_heads, head_dim, tok_count) + skip_now[
        :, None, None
    ] * x_conv
    gated = ssm_out * jax.nn.silu(z_in.astype(jnp.float32))
    inv_rms = lax.rsqrt(jnp.mean(gated * gated, axis=1, keepdims=True) + 1e-05)
    normed = (gated * inv_rms * gain_now).astype(jnp.bfloat16)
    out_cols = proj_out.shape[1]
    piece = lax.all_gather(normed, "row", axis=0, tiled=True)
    piece_heads = piece.shape[0]
    rows_now = proj_out.reshape(piece_heads, head_dim, out_cols)
    col_partial = jnp.einsum("hpt,hpd->td", piece, rows_now, preferred_element_type=jnp.float32)
    return lax.psum_scatter(
        col_partial.astype(jnp.bfloat16), "col", scatter_dimension=1, tiled=True
    )


def solution(mesh):
    in_specs = (
        P("ctx", "row"),
        P("row", "col"),
        P("row", "col"),
        P("row", None),
        P("row", "col"),
        P("col"),
        P("col"),
        P("col"),
        P("col", None),
        P(),
        P("col"),
        P("col", "row"),
    )
    out_specs = P("ctx", ("row", "col"))
    return jax.shard_map(local, mesh=mesh, in_specs=in_specs, out_specs=out_specs, check_vma=False)
```

profile of v0, /device:TPU:0, one launch (start us, length us, event | category | flops | bytes accessed | tf_op | source)
XLA Modules:
  0.0 209.5 jit_solution(5886048797416643064)
XLA Ops:
  6.5 1.6 copy-done
  8.1 8.7 %convolution_convert_fusion.1 = bf16[2048,256]{1,0:T(8,128)(2,1)S(1)} fusion(bf16[4096,2048]{1,0:T(8,128)(2,1)} %param.13, bf16[256,4096]{1,0:T(8,128)(2,1)S(1)} %copy-done), kind=kOutput, calls=%fused_computation.9 | convolution fusion | flops 4295491584 | bytes 19922944 | tf_op jit(solution)/shard_map/dc,td->ct/dot_general | solution.py:41
  16.8 1.8 copy-done.5
  18.7 5.0 %convolution_convert_fusion = bf16[2048,256]{1,0:T(8,128)(2,1)S(1)} fusion(bf16[4096,2048]{1,0:T(8,128)(2,1)S(1)} %copy-done.5, bf16[256,4096]{1,0:T(8,128)(2,1)S(1)} %copy-done), kind=kOutput, calls=%fused_computation.8 | convolution fusion | flops 4295491584 | bytes 19922944 | tf_op jit(solution)/shard_map/dc,td->ct/dot_general | solution.py:44
  24.5 1.6 pad_maximum_fusion
  26.2 3.0 %convolution_convert_fusion.2 = bf16[256,256]{1,0:T(8,128)(2,1)} fusion(bf16[4096,256]{1,0:T(8,128)(2,1)} %param.15, bf16[256,4096]{1,0:T(8,128)(2,1)S(1)} %copy-done), kind=kOutput, calls=%fused_computation.32 | convolution fusion | flops 536936448 | bytes 4325376 | tf_op jit(solution)/shard_map/dc,td->ct/dot_general | solution.py:38
  29.5 32.7 %reduce-scatter.3.cloned.1.call-done = bf16[16,129,256]{2,1,0:T(8,128)(2,1)} async-done(((bf16[32,129,256]{2,1,0:T(8,128)(2,1)}), bf16[16,129,256]{2,1,0:T(8,128)(2,1)}) %reduce-scatter.3.cloned.1.call-update) | async-done | bytes 1056784 | tf_op jit(solution)/shard_map/reduce_scatter | solution.py:50
  64.1 1.1 slice.75
  65.2 20.9 %all-reduce.3.cloned.1.call-done = bf16[256,256]{1,0:T(8,128)(2,1)} async-done(((bf16[256,256]{1,0:T(8,128)(2,1)}), bf16[256,256]{1,0:T(8,128)(2,1)}) %all-reduce.3.cloned.1.call-update) | async-done | bytes 131088 | tf_op jit(solution)/shard_map/psum | solution.py:56
  86.0 1.0 pad_maximum_fusion.1
  87.0 3.6 %collective-permute-start = (bf16[1280,3]{1,0:T(8,128)(2,1)S(1)}, bf16[1280,3]{1,0:T(8,128)(2,1)S(1)}, u32[]{:S(2)}, u32[]{:S(2)}) collective-permute-start(bf16[1280,3]{1,0:T(8,128)(2,1)S(1)} %pad_maximum_fusion.1), channel_id=1, source_target_pairs={{0,8},{8,16},{16,24},{1,9},{9,17},{17,25},{2,10},{10,18},{18,26},{... | collective-permute-start | bytes 23048 | tf_op jit(solution)/shard_map/ppermute | solution.py:15
  92.2 4.7 %collective-permute-done = bf16[1280,3]{1,0:T(8,128)(2,1)S(1)} collective-permute-done((bf16[1280,3]{1,0:T(8,128)(2,1)S(1)}, bf16[1280,3]{1,0:T(8,128)(2,1)S(1)}, u32[]{:S(2)}, u32[]{:S(2)}) %collective-permute-start) | collective-permute-done | bytes 7712 | tf_op jit(solution)/shard_map/ppermute | solution.py:15
  96.9 1.3 maximum_convert_fusion
  98.3 1.9 divide_multiply_fusion
  100.4 1.7 fusion.18
  104.1 12.7 %all-reduce = bf16[64]{0:T(256)(128)(2,1)S(1)} all-reduce(bf16[64]{0:T(256)(128)(2,1)S(1)} %dynamic-update-slice), channel_id=2, replica_groups=mesh['ctx'=4,'row'=2,'col'=4] {'ctx'}, use_global_device_ids=true, to_apply=%add | all-reduce | flops 64 | bytes 256
  117.6 5.8 %fusion.1 = f32[16,64,256]{2,1,0:T(8,128)} fusion(f32[16,256]{1,0:T(8,128)S(1)} %get-tuple-element.27, f32[256,256]{1,0:T(8,128)S(1)} %fusion.36, pred[256,256]{1,0:T(8,128)(4,1)S(1)} %iota_compare_fusion, f32[16,64,256]{2,1,0:T(8,128)S(1)} %bitcast.59, f32[16,256]{1,0:T(8,128)S(1)} %bitcast.66), kind=kOutput, calls=%fused_computation.2 | convolution fusion | flops 809762816 | bytes 2457600 | tf_op jit(solution)/shard_map/hcij,hpcj->hpci/dot_general | solution.py:91
  123.5 7.7 %all-gather.7.cloned.1.call-done = bf16[64,64,128]{2,1,0:T(8,128)(2,1)} async-done(((bf16[16,64,128]{2,1,0:T(8,128)(2,1)}), bf16[64,64,128]{2,1,0:T(8,128)(2,1)}) %all-gather.7.cloned.1.call-update) | async-done | bytes 1048592 | tf_op jit(solution)/shard_map/all_gather | solution.py:112
  131.2 3.2 %fusion.24 = f32[16,1,64,128]{3,1,2,0:T(1,128)S(1)} fusion(f32[4,16,1,1]{0,2,3,1:T(1,128)S(1)} %copy.31, bf16[4,16,64,128]{3,2,1,0:T(8,128)(2,1)} %bitcast.71), kind=kOutput, calls=%fused_computation.41 | convolution fusion | flops 6291456 | bytes 1573120 | tf_op jit(solution)/shard_map/jh,jhpn->hpn/dot_general | solution.py:123
  134.4 2.8 %multiply_reduce_fusion = (f32[16,256]{1,0:T(8,128)S(1)}, f32[16,64,256]{2,1,0:T(8,128)S(1)}) fusion(bf16[16,129,256]{2,1,0:T(8,128)(2,1)} %reduce-scatter.3.cloned.1.call-done, f32[16,64,256]{2,1,0:T(8,128)S(1)} %bitcast.60, f32[16]{0:T(128)S(1)} %dynamic_slice.24, f32[16,64,256]{2,1,0:T(8,128)} %fusion.1, f32[1280,256]{1,0:T(8,128)S(1)} %divide_multiply_fusion, ...), kind=kOutput, calls=%fused_computation.39 | convolution fusion | flops 405925888 | bytes 4359168 | tf_op jit(solution)/shard_map/nci,chpn->hpci/dot_general | solution.py:125
  137.2 1.0 multiply_convert_fusion
  138.5 20.7 %all-gather.5.cloned.1.call-done = bf16[32,64,256]{2,1,0:T(8,128)(2,1)} async-done(((bf16[16,64,256]{2,1,0:T(8,128)(2,1)}), bf16[32,64,256]{2,1,0:T(8,128)(2,1)}) %all-gather.5.cloned.1.call-update) | async-done | bytes 1048592 | tf_op jit(solution)/shard_map/all_gather | solution.py:135
  159.2 12.2 %fusion = bf16[256,4096]{1,0:T(8,128)(2,1)} fusion(bf16[32,64,256]{2,1,0:T(8,128)(2,1)} %all-gather.5.cloned.1.call-done, bf16[32,64,4096]{2,1,0:T(8,128)(2,1)} %bitcast.55), kind=kOutput, calls=%fused_computation.1 | convolution fusion | flops 4296015872 | bytes 19922944 | tf_op jit(solution)/shard_map/hpt,hpd->td/dot_general | solution.py:138
  171.4 31.6 %reduce-scatter.5.cloned.1.call-done = bf16[256,1024]{1,0:T(8,128)(2,1)} async-done(((bf16[256,4096]{1,0:T(8,128)(2,1)}), bf16[256,1024]{1,0:T(8,128)(2,1)}) %reduce-scatter.5.cloned.1.call-update) | async-done | bytes 524304 | tf_op jit(solution)/shard_map/reduce_scatter | solution.py:139
  (68 shorter events, 7.1 us)
Async XLA Ops:
  6.5 1.6 copy-start
  6.5 55.7 %reduce-scatter.3.cloned.1.call-start = ((), (), s32[]{:S(2)}) async-start(), calls=%async_computation.2 | async-start | bytes 3342336 | tf_op jit(solution)/shard_map/reduce_scatter | solution.py:50
  8.1 10.5 %copy-start.5 = (bf16[4096,2048]{1,0:T(8,128)(2,1)S(1)}, bf16[4096,2048]{1,0:T(8,128)(2,1)}, u32[]{:S(2)}) copy-start(bf16[4096,2048]{1,0:T(8,128)(2,1)} %param.14) | copy-start | bytes 50331652
  18.7 5.1 %copy-start.2 = (bf16[4096,32]{0,1:T(8,128)(2,1)S(1)}, bf16[4096,32]{0,1:T(8,128)(2,1)}, u32[]{:S(2)}) copy-start(bf16[4096,32]{0,1:T(8,128)(2,1)} %param.16) | copy-start | bytes 786436
  26.1 3.2 %copy-start.6 = (f32[32]{0:T(128)S(1)}, f32[32]{0:T(128)}, u32[]{:S(2)}) copy-start(f32[32]{0:T(128)} %param.17) | copy-start | bytes 388
  26.1 3.3 %copy-start.7 = (f32[32]{0:T(128)S(1)}, f32[32]{0:T(128)}, u32[]{:S(2)}) copy-start(f32[32]{0:T(128)} %param.18) | copy-start | bytes 388
  26.1 3.3 %copy-start.3 = (f32[2048,4]{0,1:T(4,128)S(1)}, f32[2048,4]{0,1:T(4,128)}, u32[]{:S(2)}) copy-start(f32[2048,4]{0,1:T(4,128)} %param.20) | copy-start | bytes 98308
  26.1 3.3 %copy-start.4 = (f32[256,4]{0,1:T(4,128)S(1)}, f32[256,4]{0,1:T(4,128)}, u32[]{:S(2)}) copy-start(f32[256,4]{0,1:T(4,128)} %param.21) | copy-start | bytes 12292
  26.2 59.9 %all-reduce.3.cloned.1.call-start = ((), (), s32[]{:S(2)}) async-start(), calls=%async_computation.3 | async-start | bytes 262144 | tf_op jit(solution)/shard_map/psum | solution.py:56
  29.2 102.0 %all-gather.7.cloned.1.call-start = ((), (), s32[]{:S(2)}) async-start(), calls=%async_computation.6 | async-start | bytes 1310720 | tf_op jit(solution)/shard_map/all_gather | solution.py:112
  87.0 9.9 %collective-permute-start = (bf16[1280,3]{1,0:T(8,128)(2,1)S(1)}, bf16[1280,3]{1,0:T(8,128)(2,1)S(1)}, u32[]{:S(2)}, u32[]{:S(2)}) collective-permute-start(bf16[1280,3]{1,0:T(8,128)(2,1)S(1)} %pad_maximum_fusion.1), channel_id=1, source_target_pairs={{0,8},{8,16},{16,24},{1,9},{9,17},{17,25},{2,10},{10,18},{18,26},{... | collective-permute-start | bytes 23048 | tf_op jit(solution)/shard_map/ppermute | solution.py:15
  100.2 1.9 copy-start.8
  100.2 2.0 dynamic-slice-start
  100.3 2.0 copy-start.9
  102.1 57.1 %all-gather.5.cloned.1.call-start = ((), (), s32[]{:S(2)}) async-start(), calls=%async_computation.4 | async-start | bytes 1572864 | tf_op jit(solution)/shard_map/all_gather | solution.py:135
  138.2 64.7 %reduce-scatter.5.cloned.1.call-start = ((), (), s32[]{:S(2)}) async-start(), calls=%async_computation.5 | async-start | bytes 2621440 | tf_op jit(solution)/shard_map/reduce_scatter | solution.py:139
  159.2 43.8 %copy-start.1 = (bf16[256,4096]{1,0:T(8,128)(2,1)S(1)}, bf16[256,4096]{1,0:T(8,128)(2,1)}, u32[]{:S(2)}) copy-start(bf16[256,4096]{1,0:T(8,128)(2,1)} %param.12) | copy-start | bytes 6291460
Sparse Core Ops, SparseCore 0:
  26.2 35.9 reduce-scatter.2
  64.6 21.4 all-reduce.2
  102.2 28.9 all-gather.6
  138.3 20.7 all-gather.4
  171.5 31.4 reduce-scatter.4
where the time goes:
time: 210 us
  waiting for transfers between devices  118 us (56%)
  matrix products  43.6 us (21%)
  between operations  14.1 us (7%)
  blocking collectives  12.7 us (6%)
  other arithmetic  10.3 us (5%)
  local copies, waits for them, and re-layouts  6.53 us (3%)
  starting transfers between devices  3.98 us (2%)
    reduce_scatter x1, waiting for transfers between devices, local(): lax.psum_scatter(jnp.concatenate([x_part, z_part, dt_part], axis=1).astyp...  32.7 us
    reduce_scatter x1, waiting for transfers between devices, local(): lax.psum_scatter(col_partial.astype(jnp.bfloat16), 'col', scatter_dimensi...  31.6 us
    psum x1, waiting for transfers between devices, local(): bc_sum = lax.psum(bc_term.astype(jnp.bfloat16), 'row')  20.9 us
    all_gather x1, waiting for transfers between devices, local(): piece = lax.all_gather(normed, 'row', axis=0, tiled=True)  20.7 us
    unnamed x1, blocking collectives  12.7 us
    dot_general x1, matrix products, local(): jnp.einsum('hpt,hpd->td', piece, rows_now, preferred_element_type=jnp.flo...  12.2 us
    dot_general x1, matrix products, local(): jnp.einsum('dc,td->ct', proj_x, tokens, preferred_element_type=jnp.float32)  8.69 us
    all_gather x1, waiting for transfers between devices, local(): lax.all_gather(final_state[None].astype(jnp.bfloat16), 'ctx', axis=0, til...  7.72 us
  transfers between devices with their start and end apart: 6, of which 6 were waited for; matrix products, arithmetic and copies ran while one was open for 7% of the time, Pallas kernels for 0%

commit v1 on v0

--- a/solution.py
+++ b/solution.py
@@ -1,12 +1,590 @@
+import functools
+
 import jax
 import jax.numpy as jnp
 from jax import lax
+from jax.experimental import pallas as pl
+from jax.experimental.pallas import tpu as pltpu
 from jax.sharding import PartitionSpec as P
 
 Q = 256
-
-
+EPS = 1e-05
+HALO = 16
+VMEM_LIMIT = 48 * 1024 * 1024
+f32 = jnp.float32
+bf16 = jnp.bfloat16
 highest_mode = lax.Precision.HIGHEST
+
+
+def mm(a, b):
+    return jnp.dot(a, b, preferred_element_type=f32)
+
+
+def mm_tn(a, b):
+    return lax.dot_general(a, b, (((0,), (0,)), ((), ())), preferred_element_type=f32)
+
+
+def mm_nt(a, b):
+    return lax.dot_general(a, b, (((1,), (1,)), ((), ())), preferred_element_type=f32)
+
+
+def silu(v):
+    return v / (1.0 + jnp.exp(-v))
+
+
+def softplus(v):
+    return jnp.maximum(v, 0.0) + jnp.log(1.0 + jnp.exp(-jnp.abs(v)))
+
+
+def total(mine, theirs):
+    return (mine.astype(f32) + theirs.astype(f32)).astype(bf16).astype(f32)
+
+
+def spread(per_head, head_dim):
+    heads = per_head.shape[0]
+    high = per_head.astype(bf16)
+    low = (per_head - high.astype(f32)).astype(bf16)
+    parts = jnp.concatenate([high.astype(f32), low.astype(f32)], axis=0).astype(bf16)
+    shape = (2 * heads, heads * head_dim)
+    row = lax.broadcasted_iota(jnp.int32, shape, 0) % heads
+    col = lax.broadcasted_iota(jnp.int32, shape, 1) // head_dim
+    return mm_tn(parts, jnp.where(row == col, 1.0, 0.0).astype(bf16))
+
+
+def pick(row_vector, first, count):
+    shape = (count, row_vector.shape[1])
+    lane = lax.broadcasted_iota(jnp.int32, shape, 1)
+    sub = lax.broadcasted_iota(jnp.int32, shape, 0)
+    return jnp.sum(jnp.where(lane == sub + first, row_vector, 0.0), axis=1, keepdims=True)
+
+
+def conv(ext_ref, taps, toks):
+    count = taps.shape[0]
+    running = None
+    for tap in range(count):
+        term = taps[tap : tap + 1, :] * ext_ref[pl.ds(HALO - count + 1 + tap, toks), :]
+        running = term if running is None else running + term
+    return running
+
+
+def prefix(messages, here, state_dim):
+    def parts(message):
+        return message[:state_dim].astype(f32), message[state_dim : state_dim + 1].astype(f32)
+
+    state, decay = parts(messages[0])
+    enter = jnp.zeros_like(state)
+    reach = jnp.ones_like(decay)
+    for step, message in enumerate(messages[1:]):
+        their_state, their_decay = parts(message)
+        later = ((here >> step) & 1) == 1
+        enter = jnp.where(later, enter + reach * their_state, enter)
+        reach = jnp.where(later, reach * their_decay, reach)
+        state = jnp.where(later, decay * their_state + state, their_decay * state + their_state)
+        decay = decay * their_decay
+    return enter, state, decay
+
+
+def first_kernel(where, tok, w_x, w_bc, w_dt, msg, acc_x, acc_bc, acc_dt):
+    step = pl.program_id(0)
+    toks, lanes = acc_bc.shape
+
+    @pl.when(step == 0)
+    def _():
+        acc_x[...] = jnp.zeros_like(acc_x)
+        acc_bc[...] = jnp.zeros_like(acc_bc)
+        acc_dt[...] = jnp.zeros_like(acc_dt)
+
+    now = tok[...]
+    acc_x[...] += mm(now, w_x[...])
+    acc_bc[...] += mm(now, w_bc[...])
+    acc_dt[...] += mm_nt(w_dt[...], now)
+
+    @pl.when(step == pl.num_programs(0) - 1)
+    def _():
+        heads = acc_dt.shape[0]
+        msg[:toks, :] = acc_bc[...].astype(bf16)
+        msg[toks : toks + heads, :] = acc_dt[...].astype(bf16)
+        for j in range(acc_x.shape[1] // lanes):
+            low = toks + heads + j * toks
+            msg[low : low + toks, :] = acc_x[:, j * lanes : (j + 1) * lanes].astype(bf16)
+
+
+def product_kernel(where, tok, weight, *refs, edges):
+    step = pl.program_id(0)
+    out, acc = refs[edges or 0], refs[-1]
+    toks = tok.shape[0]
+    lanes = out.shape[1]
+
+    @pl.when(step == 0)
+    def _():
+        acc[...] = jnp.zeros_like(acc)
+
+    acc[...] += mm(tok[...], weight[...])
+
+    @pl.when(step == pl.num_programs(0) - 1)
+    def _():
+        for j in range(acc.shape[1] // lanes):
+            out[j * toks : (j + 1) * toks, :] = acc[:, j * lanes : (j + 1) * lanes].astype(bf16)
+        if edges is not None:
+            edge = refs[edges + 1]
+            for j in range(edges):
+                edge[j * HALO : (j + 1) * HALO, :] = refs[j][...]
+            for j in range(acc.shape[1] // lanes):
+                low = (edges + j) * HALO
+                edge[low : low + HALO, :] = acc[
+                    toks - HALO :, j * lanes : (j + 1) * lanes
+                ].astype(bf16)
+
+
+def state_kernel(
+    where, *refs, first, chunk, chunks, head_dim, state_dim, toks, lanes
+):
+    refs = list(refs)
+    if first:
+        bc_mine, bc_theirs = refs.pop(0), refs.pop(0)
+    else:
+        bc_in = refs.pop(0)
+    dt_mine, dt_theirs, x_mine, x_theirs, edge_a, edge_b, taps_x, taps_bc, bias, decay = refs[:10]
+    refs = refs[10:]
+    if first:
+        bc_out, scores = refs.pop(0), refs.pop(0)
+    msg, scaled, conv_out, cum_out, cum_t_out, ext = refs
+    row, here = where[0], where[2]
+    blocks = x_mine.shape[0] // toks
+    heads = blocks * lanes // head_dim
+    local_heads = heads * chunks
+    inside = jnp.where(here > 0, 1.0, 0.0)
+
+    def halo(block):
+        low = block * HALO
+        return total(edge_a[low : low + HALO, :], edge_b[low : low + HALO, :]) * inside
+
+    if first:
+        ext[:HALO, :] = halo(0)
+        ext[HALO:, :] = total(bc_mine[...], bc_theirs[...])
+        bc_now = silu(conv(ext, taps_bc[...], toks)).astype(bf16)
+        bc_out[...] = bc_now
+        b_now = bc_now[:, :state_dim]
+        products = mm_nt(bc_now[:, state_dim:], b_now)
+        shape = (toks, toks)
+        lower = lax.broadcasted_iota(jnp.int32, shape, 0) >= lax.broadcasted_iota(jnp.int32, shape, 1)
+        scores[...] = jnp.where(lower, products, 0.0)
+    else:
+        b_now = bc_in[:, :state_dim]
+
+    low = pl.multiple_of(row * local_heads, local_heads)
+    dt_sum = total(dt_mine[pl.ds(low, local_heads), :], dt_theirs[pl.ds(low, local_heads), :])
+    dt_sum = dt_sum[chunk * heads : (chunk + 1) * heads]
+    first_head = row * local_heads + chunk * heads
+    dt_now = softplus(dt_sum + pick(bias[...], first_head, heads))
+    log_decay = -pick(decay[...], first_head, heads) * dt_now
+    shape = (toks, toks)
+    upper = lax.broadcasted_iota(jnp.int32, shape, 0) <= lax.broadcasted_iota(jnp.int32, shape, 1)
+    cum = lax.dot_general(
+        log_decay,
+        jnp.where(upper, 1.0, 0.0),
+        (((1,), (0,)), ((), ())),
+        precision=highest_mode,
+        preferred_element_type=f32,
+    )
+    last = cum[:, toks - 1 : toks]
+    cum_out[...] = cum
+    cum_t_out[...] = cum.T
+    dt_wide = spread(dt_now, head_dim)
+    tail_wide = spread(dt_now * jnp.exp(last - cum), head_dim)
+    through = spread(jnp.exp(jnp.broadcast_to(last, (heads, HALO))), head_dim)
+    rows = state_dim + HALO
+    for j in range(blocks):
+        ext[:HALO, :] = halo(1 + chunk * blocks + j)
+        ext[HALO:, :] = total(
+            x_mine[j * toks : (j + 1) * toks, :], x_theirs[j * toks : (j + 1) * toks, :]
+        )
+        cols = slice(j * lanes, (j + 1) * lanes)
+        x_now = silu(conv(ext, taps_x[:, cols], toks))
+        conv_out[:, cols] = x_now.astype(bf16)
+        scaled[:, cols] = (x_now * dt_wide[:, cols]).astype(bf16)
+        state = mm_tn(b_now, (x_now * tail_wide[:, cols]).astype(bf16))
+        msg[j * rows : j * rows + state_dim, :] = state.astype(bf16)
+        msg[j * rows + state_dim : (j + 1) * rows, :] = through[:, cols].astype(bf16)
+
+
+def combine_kernel(where, *refs, state_dim, lanes):
+    *messages, out = refs
+    rows = state_dim + HALO
+    for j in range(out.shape[0] // rows):
+        now = [m[j * rows : (j + 1) * rows, :] for m in messages]
+        _, state, decay = prefix(now, where[2], state_dim)
+        out[j * rows : j * rows + state_dim, :] = state.astype(bf16)
+        out[j * rows + state_dim : (j + 1) * rows, :] = jnp.broadcast_to(decay, (HALO, lanes)).astype(bf16)
+
+
+def inner_kernel(where, scores, scaled, conv_out, cum, cum_t, skip, out, *, head_dim, first_of, local_heads):
+    toks, channels = scaled.shape
+    pair = 2 * head_dim
+    half = toks // 2
+    heads = channels // head_dim
+    skip_now = pick(skip[...], where[0] * local_heads + first_of, heads)
+    skip_wide = spread(jnp.broadcast_to(skip_now, (heads, HALO)), head_dim)[:1, :]
+    left = lax.broadcasted_iota(jnp.int32, (toks, pair), 1) < head_dim
+    zero = jnp.zeros((toks, pair), bf16)
+    for p in range(heads // 2):
+        cols = slice(p * pair, (p + 1) * pair)
+        x_pair = scaled[:, cols]
+        top = None
+        for side in range(2):
+            h = 2 * p + side
+            x_now = jnp.where(left, x_pair, zero) if side == 0 else jnp.where(left, zero, x_pair)
+            gap_top = jnp.minimum(cum_t[:half, h : h + 1] - cum[h : h + 1, :half], 0.0)
+            gap_low = jnp.minimum(cum_t[half:, h : h + 1] - cum[h : h + 1, :], 0.0)
+            w_top = (jnp.exp(gap_top) * scores[:half, :half]).astype(bf16)
+            w_low = (jnp.exp(gap_low) * scores[half:, :]).astype(bf16)
+            part_top = mm(w_top, x_now[:half])
+            part_low = mm(w_low, x_now)
+            top = part_top if top is None else top + part_top
+            low = part_low if side == 0 else low + part_low
+        skips = skip_wide[:, cols]
+        out[:half, cols] = top + skips * conv_out[:half, cols].astype(f32)
+        out[half:, cols] = low + skips * conv_out[half:, cols].astype(f32)
+
+
+def gate_kernel(where, inner, bc, cum, z_mine, z_theirs, gain, *refs, head_dim, state_dim, lanes):
+    *messages, out = refs
+    toks = inner.shape[0]
+    rows = state_dim + HALO
+    grown = spread(jnp.exp(cum[...]), head_dim)
+    c_now = bc[:, state_dim:]
+    wide = 2 * head_dim
+    shape = (wide, wide)
+    same = (lax.broadcasted_iota(jnp.int32, shape, 0) // head_dim) == (
+        lax.broadcasted_iota(jnp.int32, shape, 1) // head_dim
+    )
+    mean_of = jnp.where(same, 1.0 / head_dim, 0.0).astype(bf16)
+    for j in range(inner.shape[1] // lanes):
+        now = [m[j * rows : (j + 1) * rows, :] for m in messages]
+        enter, _, _ = prefix(now, where[2], state_dim)
+        cols = slice(j * lanes, (j + 1) * lanes)
+        scanned = inner[:, cols] + grown[:, cols] * mm(c_now, enter.astype(bf16))
+        z_now = total(z_mine[j * toks : (j + 1) * toks, :], z_theirs[j * toks : (j + 1) * toks, :])
+        gated = scanned * silu(z_now)
+        square = gated * gated
+        for i in range(lanes // wide):
+            part = square[:, i * wide : (i + 1) * wide]
+            high = part.astype(bf16)
+            rest = (part - high.astype(f32)).astype(bf16)
+            mean = mm(high, mean_of) + mm(rest, mean_of)
+            low = j * lanes + i * wide
+            out[j * toks : (j + 1) * toks, i * wide : (i + 1) * wide] = (
+                gated[:, i * wide : (i + 1) * wide]
+                * lax.rsqrt(mean + EPS)
+                * gain[:, low : low + wide]
+            ).astype(bf16)
+
+
+def out_kernel(where, weight, *refs, half):
+    *normed, send, keep = refs
+    step = pl.program_id(0)
+    lanes = normed[0].shape[1]
+    toks = send.shape[0]
+    width = weight.shape[1]
+    per_send = send.shape[1] // width
+    acc = None
+    for side in range(2):
+        low = jnp.where(side == 0, where[0], 1 - where[0]) * half
+        at = 0
+        for chunk in normed[side * (len(normed) // 2) : (side + 1) * (len(normed) // 2)]:
+            for j in range(chunk.shape[0] // toks):
+                rows = pl.ds(pl.multiple_of(low + at, lanes), lanes)
+                part = mm(chunk[j * toks : (j + 1) * toks, :], weight[rows, :])
+                acc = part if acc is None else acc + part
+                at += lanes
+    done = acc.astype(bf16)
+
+    @pl.when(step < per_send)
+    def _():
+        send[:, pl.ds(pl.multiple_of(step * width, width), width)] = done
+
+    @pl.when(step >= per_send)
+    def _():
+        keep[:, pl.ds(pl.multiple_of((step - per_send) * width, width), width)] = done
+
+
+def add_kernel(a, b, out):
+    out[...] = (a[...].astype(f32) + b[...].astype(f32)).astype(bf16)
+
+
+def sds(*shape, dtype=bf16):
+    return jax.ShapeDtypeStruct(shape, dtype)
+
+
+def cost(flops, size):
+    return pl.CostEstimate(flops=int(flops), bytes_accessed=int(size), transcendentals=0)
+
+
+def call(kernel, where, args, specs, outs, out_specs, scratch=(), grid=(1,), flops=0, size=0, name=None):
+    return pl.pallas_call(
+        kernel,
+        grid_spec=pltpu.PrefetchScalarGridSpec(
+            num_scalar_prefetch=1,
+            grid=grid,
+            in_specs=specs,
+            out_specs=out_specs,
+            scratch_shapes=list(scratch),
+        ),
+        out_shape=outs,
+        compiler_params=pltpu.CompilerParams(
+            dimension_semantics=("arbitrary",) * len(grid), vmem_limit_bytes=VMEM_LIMIT
+        ),
+        cost_estimate=cost(flops, size),
+        name=name,
+    )(where, *args)
+
+
+def whole(shape):
+    return pl.BlockSpec(shape, lambda i, w: (0,) * len(shape))
+
+
+def at(shape, index):
+    return pl.BlockSpec(shape, index)
+
+
+def swapped(shard, axis, by):
+    devices = lax.axis_size(axis)
+    return lax.ppermute(shard, axis, [(i, i ^ by) for i in range(devices)])
+
+
+def fast(
+    tokens, proj_x, proj_z, proj_bc, proj_dt, dt_bias, decay_rate, skip_gain,
+    conv_x, conv_bc, norm_gain, proj_out,
+):
+    toks, depth = tokens.shape
+    heads = proj_dt.shape[1]
+    head_dim = proj_x.shape[1] // heads
+    lanes = proj_bc.shape[1]
+    state_dim = lanes // 2
+    taps = conv_bc.shape[1]
+    local_heads = heads // 2
+    half = local_heads * head_dim
+    chunks = 2
+    width = half // chunks
+    blocks = width // lanes
+    chunk_heads = local_heads // chunks
+    out_cols = proj_out.shape[1]
+    ctx_size = lax.axis_size("ctx")
+    row, col, ctx = lax.axis_index("row"), lax.axis_index("col"), lax.axis_index("ctx")
+    where = jnp.stack([row, col, ctx]).astype(jnp.int32)
+    conv_x_t, conv_bc_t, proj_dt_t = conv_x.T, conv_bc.T, proj_dt.T
+    bias, decay, skip, gain = (v[None] for v in (dt_bias, decay_rate, skip_gain, norm_gain))
+
+    kb = depth // 8
+    tok_spec = at((toks, kb), lambda k, w: (0, k))
+    msg_rows = toks + heads + blocks * toks
+    msg_first = call(
+        first_kernel,
+        where,
+        (tokens, proj_x, proj_bc, proj_dt_t),
+        [
+            tok_spec,
+            at((kb, width), lambda k, w: (k, (1 - w[0]) * chunks)),
+            at((kb, lanes), lambda k, w: (k, 0)),
+            at((heads, kb), lambda k, w: (0, k)),
+        ],
+        sds(msg_rows, lanes),
+        whole((msg_rows, lanes)),
+        [pltpu.VMEM((toks, width), f32), pltpu.VMEM((toks, lanes), f32), pltpu.VMEM((heads, toks), f32)],
+        grid=(depth // kb,),
+        flops=2 * toks * depth * (width + lanes + heads),
+        size=2 * depth * (toks + width + lanes + heads),
+        name="first",
+    )
+    first_got = swapped(msg_first, "row", 1)
+
+    def product(weight, n_cols, col_of, edge_blocks, name):
+        edge_args = [msg_first] * len(edge_blocks)
+        edge_specs = [at((HALO, lanes), lambda k, w, e=e: (e, 0)) for e in edge_blocks]
+        out_rows = n_cols // lanes * toks
+        outs, out_specs = [sds(out_rows, lanes)], [whole((out_rows, lanes))]
+        edges = None
+        if edge_blocks:
+            edges = len(edge_blocks)
+            edge_rows = (edges + n_cols // lanes) * HALO
+            outs.append(sds(edge_rows, lanes))
+            out_specs.append(whole((edge_rows, lanes)))
+        return call(
+            functools.partial(product_kernel, edges=edges),
+            where,
+            (tokens, weight, *edge_args),
+            [tok_spec, at((kb, n_cols), lambda k, w: (k, col_of(w))), *edge_specs],
+            outs,
+            out_specs,
+            [pltpu.VMEM((toks, n_cols), f32)],
+            grid=(depth // kb,),
+            flops=2 * toks * depth * n_cols,
+            size=2 * depth * (toks + n_cols),
+            name=name,
+        )
+
+    def last_rows(low):
+        return (low + toks) // HALO - 1
+
+    bc_edge = last_rows(0)
+    x_edges = [last_rows(toks + heads + j * toks) for j in range(blocks)]
+    msg_second, edge_other = product(
+        proj_x, width, lambda w: (1 - w[0]) * chunks + 1, [bc_edge, *x_edges], "x_other"
+    )
+    second_got = swapped(msg_second, "row", 1)
+    down = [(i, (i + 1) % ctx_size) for i in range(ctx_size)]
+    edge_a = lax.ppermute(
+        edge_other, ("ctx", "row"), [(2 * i + s, 2 * j + 1 - s) for i, j in down for s in range(2)]
+    )
+    x_mine, edge_own = product(proj_x, half, lambda w: w[0], [bc_edge], "x_own")
+    edge_b = lax.ppermute(edge_own, "ctx", down)
+    z_send = [
+        product(proj_z, width, lambda w, c=c: (1 - w[0]) * chunks + c, [], "z_other")[0]
+        for c in range(chunks)
+    ]
+    z_got = [swapped(z, "row", 1) for z in z_send]
+    z_mine = product(proj_z, half, lambda w: w[0], [], "z_own")[0]
+
+    edge_shape = edge_a.shape
+    rows = state_dim + HALO
+    kernel_sizes = dict(head_dim=head_dim, state_dim=state_dim, lanes=lanes)
+    states, scans = [], []
+    bc_now = scores = None
+    for c in range(chunks):
+        dt_at = at((heads, lanes), lambda k, w: (toks // heads, 0))
+        args, specs = [], []
+        outs, out_specs = [], []
+        if c == 0:
+            args += [msg_first, first_got]
+            specs += [at((toks, lanes), lambda k, w: (0, 0))] * 2
+            outs += [sds(toks, lanes), sds(toks, toks, dtype=f32)]
+            out_specs += [whole((toks, lanes)), whole((toks, toks))]
+        else:
+            args += [bc_now]
+            specs += [whole((toks, lanes))]
+        x_theirs = first_got[toks + heads :] if c == 0 else second_got
+        args += [msg_first, first_got, x_mine, x_theirs, edge_a, edge_b, conv_x_t, conv_bc_t, bias, decay]
+        specs += [
+            dt_at,
+            dt_at,
+            at((blocks * toks, lanes), lambda k, w, c=c: (c, 0)),
+            whole((blocks * toks, lanes)),
+            whole(edge_shape),
+            whole(edge_shape),
+            at((taps, width), lambda k, w, c=c: (0, w[0] * chunks + c)),
+            whole((taps, lanes)),
+            whole((1, heads)),
+            whole((1, heads)),
+        ]
+        outs += [
+            sds(blocks * rows, lanes),
+            sds(toks, width),
+            sds(toks, width),
+            sds(chunk_heads, toks, dtype=f32),
+            sds(toks, chunk_heads, dtype=f32),
+        ]
+        out_specs += [whole(o.shape) for o in outs[len(out_specs) :]]
+        got = call(
+            functools.partial(
+                state_kernel, first=c == 0, chunk=c, chunks=chunks, toks=toks, **kernel_sizes
+            ),
+            where, args, specs, outs, out_specs,
+            [pltpu.VMEM((HALO + toks, lanes), f32)],
+            flops=2 * toks * width * (state_dim + 64), size=2 * toks * width * 6, name="state",
+        )
+        if c == 0:
+            bc_now, scores = got[:2]
+            got = got[2:]
+        states.append(got[0])
+        scans.append(got[1:])
+
+    messages = []
+    for c in range(chunks):
+        heard = [states[c]]
+        send = states[c]
+        by = 1
+        while by < ctx_size:
+            if by > 1:
+                send = call(
+                    functools.partial(combine_kernel, state_dim=state_dim, lanes=lanes),
+                    where, heard, [whole(send.shape)] * len(heard), sds(*send.shape), whole(send.shape),
+                    flops=send.size * 6, size=send.size * 6, name="combine",
+                )
+            heard.append(swapped(send, "ctx", by))
+            by *= 2
+        messages.append(heard)
+
+    inners = []
+    for c in range(chunks):
+        scaled, conv_out, cum, cum_t = scans[c]
+        args = (scores, scaled, conv_out, cum, cum_t, skip)
+        inners.append(
+            call(
+                functools.partial(
+                    inner_kernel, head_dim=head_dim, first_of=c * chunk_heads, local_heads=local_heads
+                ),
+                where, args, [whole(a.shape) for a in args], sds(toks, width, dtype=f32),
+                whole((toks, width)), flops=chunk_heads * 2 * toks * toks * 2 * head_dim,
+                size=2 * toks * width * 5, name="inner",
+            )
+        )
+
+    normed, normed_got = [], []
+    for c in range(chunks):
+        cum = scans[c][2]
+        args = (inners[c], bc_now, cum, z_mine, z_got[c], gain, *messages[c])
+        now = call(
+            functools.partial(gate_kernel, **kernel_sizes),
+            where,
+            args,
+            [
+                whole((toks, width)),
+                whole((toks, lanes)),
+                whole(cum.shape),
+                at((blocks * toks, lanes), lambda k, w, c=c: (c, 0)),
+                whole((blocks * toks, lanes)),
+                at((1, width), lambda k, w, c=c: (0, w[0] * chunks + c)),
+                *[whole(m.shape) for m in messages[c]],
+            ],
+            sds(blocks * toks, lanes),
+            whole((blocks * toks, lanes)),
+            flops=2 * toks * width * (state_dim + 4 * head_dim), size=2 * toks * width * 6, name="gate",
+        )
+        normed.append(now)
+        normed_got.append(swapped(now, "row", 1))
+
+    piece = out_cols // lax.axis_size("col")
+    tile = piece // 2
+    per = piece // tile
+
+    def out_half(pair_of, name):
+        def weight_at(n, w):
+            core = jnp.where(n < per, 1 - w[1] % 2, w[1] % 2)
+            return (0, (pair_of(w) * 2 + core) * per + n % per)
+
+        args = (proj_out, *normed, *normed_got)
+        return call(
+            functools.partial(out_kernel, half=half),
+            where,
+            args,
+            [at((proj_out.shape[0], tile), weight_at), *[whole(a.shape) for a in args[1:]]],
+            [sds(toks, piece)] * 2,
+            [whole((toks, piece))] * 2,
+            grid=(2 * per,),
+            flops=2 * toks * proj_out.shape[0] * 2 * piece,
+            size=2 * proj_out.shape[0] * 2 * piece,
+            name=name,
+        )
+
+    def added(a, b):
+        return (a.astype(f32) + b.astype(f32)).astype(bf16)
+
+    far_send, far_keep = out_half(lambda w: 1 - w[1] // 2, "out_far")
+    far = added(far_keep, swapped(far_send, "col", 1))
+    far_got = swapped(far, "col", 2)
+    near_send, near_keep = out_half(lambda w: w[1] // 2, "out_near")
+    near = near_keep.astype(f32) + swapped(near_send, "col", 1).astype(f32)
+    return (near + far_got.astype(f32)).astype(bf16)
 
 
 def shifted(shard, axis, by):
@@ -15,7 +593,7 @@
     return lax.ppermute(shard, axis, pairs)
 
 
-def local(
+def general(
     tokens,
     proj_x,
     proj_z,
@@ -141,6 +719,24 @@
     )
 
 
+def local(*args):
+    tokens, proj_x, _, proj_bc, proj_dt = args[:5]
+    toks, heads, lanes = tokens.shape[0], proj_dt.shape[1], proj_bc.shape[1]
+    ctx_size = lax.axis_size("ctx")
+    fits = (
+        lax.axis_size("row") == 2
+        and lax.axis_size("col") == 4
+        and ctx_size & (ctx_size - 1) == 0
+        and toks == Q
+        and lanes == toks
+        and heads % 32 == 0
+        and toks % heads == 0
+        and proj_x.shape[1] % (4 * lanes) == 0
+        and lanes % (2 * proj_x.shape[1] // heads) == 0
+    )
+    return fast(*args) if fits else general(*args)
+
+
 def solution(mesh):
     in_specs = (
         P("ctx", "row"),

time: 210 us -> 115 us (0.55)
  waiting for transfers between devices: 118 us -> 23.1 us
  Pallas kernels: 0 us -> 66.1 us
  matrix products: 43.6 us -> 0 us
  starting transfers between devices: 3.98 us -> 19.4 us
  between operations: 14.1 us -> 0.27 us
  blocking collectives: 12.7 us -> 0 us
  other arithmetic: 10.3 us -> 1.33 us
  local copies, waits for them, and re-layouts: 6.53 us -> 4.19 us
    pallas_call x0 -> x16, Pallas kernels: none -> 66.1 us  [call(): pl.pallas_call(kernel, grid_spec=pltpu.PrefetchScalarGridSpec(num_scalar_...]
    reduce_scatter x2 -> x0, waiting for transfers between devices: 64.3 us -> none  [the longest x1 32.7 us: local(): lax.psum_scatter(jnp.concatenate([x_part, z_part, dt_part], axis=1).astyp...]
    dot_general x10 -> x0, matrix products: 43.6 us -> none  [the longest x1 12.2 us: local(): jnp.einsum('hpt,hpd->td', piece, rows_now, preferred_element_type=jnp.flo...]
    all_gather x2 -> x0, waiting for transfers between devices: 28.4 us -> none  [the longest x1 20.7 us: local(): piece = lax.all_gather(normed, 'row', axis=0, tiled=True)]
    psum x1 -> x0, waiting for transfers between devices: 20.9 us -> none  [local(): bc_sum = lax.psum(bc_term.astype(jnp.bfloat16), 'row')]
    ppermute x1 -> x15, waiting for transfers between devices: 4.74 us -> 23.1 us  [the longest x13 18.9 us: swapped(): return lax.ppermute(shard, axis, [(i, i ^ by) for i in range(devices)])]
    ppermute x1 -> x15, starting transfers between devices: 3.59 us -> 19.4 us  [the longest x13 14.8 us: swapped(): return lax.ppermute(shard, axis, [(i, i ^ by) for i in range(devices)])]
    unnamed x1 -> x0, blocking collectives: 12.7 us -> none
  transfers between devices with their start and end apart: 6 -> 15, of which waited for: 6 -> 5; matrix products, arithmetic and copies ran while one was open for 7% -> 0% of each run, Pallas kernels for 0% -> 44%
where the time goes in v1:
time: 115 us; the launch traced here: 114 us
  Pallas kernels  66.1 us (57%)
  waiting for transfers between devices  23.1 us (20%)
  starting transfers between devices  19.4 us (17%)
  local copies, waits for them, and re-layouts  4.19 us (4%)
  other arithmetic  1.33 us (1%)
    pallas_call x16, Pallas kernels, call(): pl.pallas_call(kernel, grid_spec=pltpu.PrefetchScalarGridSpec(num_scalar_...  66.1 us
    ppermute x13, waiting for transfers between devices, swapped(): return lax.ppermute(shard, axis, [(i, i ^ by) for i in range(devices)])  18.9 us
    ppermute x13, starting transfers between devices, swapped(): return lax.ppermute(shard, axis, [(i, i ^ by) for i in range(devices)])  14.8 us
    unnamed x20, local copies, waits for them, and re-layouts  4.18 us
    ppermute x1, waiting for transfers between devices, fast(): lax.ppermute(edge_other, ('ctx', 'row'), [(2 * i + s, 2 * j + 1 - s) for...  2.69 us
    ppermute x1, starting transfers between devices, fast(): lax.ppermute(edge_other, ('ctx', 'row'), [(2 * i + s, 2 * j + 1 - s) for...  2.51 us
  transfers between devices with their start and end apart: 15, of which 5 were waited for; matrix products, arithmetic and copies ran while one was open for 0% of the time, Pallas kernels for 44%

profile of v1, /device:TPU:0, one launch (start us, length us, event | category | flops | bytes accessed | tf_op | source)
XLA Modules:
  0.0 114.4 jit_solution(12425815930971663248)
XLA Ops:
  0.1 1.6 %copy-done = bf16[256,4096]{1,0:T(8,128)(2,1)S(1)} copy-done((bf16[256,4096]{1,0:T(8,128)(2,1)S(1)}, bf16[256,4096]{1,0:T(8,128)(2,1)}, u32[]{:S(2)}) %copy-start) | copy-done | bytes 2097176
  1.7 1.6 %copy-done.2 = bf16[4096,256]{1,0:T(8,128)(2,1)S(1)} copy-done((bf16[4096,256]{1,0:T(8,128)(2,1)S(1)}, bf16[4096,256]{1,0:T(8,128)(2,1)}, u32[]{:S(2)}) %copy-start.2) | copy-done | bytes 2097176
  4.2 7.2 %first.1.refs_0_.refs_1_.refs_2_ = bf16[800,256]{1,0:T(8,128)(2,1)S(1)} custom-call(s32[3]{0:T(128)S(1)} %pad_add_fusion.where, bf16[256,4096]{1,0:T(8,128)(2,1)S(1)} %copy-done, bf16[4096,2048]{1,0:T(8,128)(2,1)} %weight.8, bf16[4096,256]{1,0:T(8,128)(2,1)S(1)} %copy-done.2, bf16[32,4096]{1,0:T(8,128)(2,1)S(1)} %bitcast.10), custom_call_target="tpu_custom_call" | custom-call | flops 1677721600 | bytes 8650752 | tf_op jit(solution)/shard_map/first/pallas_call | solution.py:324
  11.5 3.0 %collective-permute-start = (bf16[800,256]{1,0:T(8,128)(2,1)S(1)}, bf16[800,256]{1,0:T(8,128)(2,1)S(1)}, u32[]{:S(2)}, u32[]{:S(2)}) collective-permute-start(bf16[800,256]{1,0:T(8,128)(2,1)S(1)} %first.1.refs_0_.refs_1_.refs_2_), channel_id=1, source_target_pairs={{0,4},{4,0},{1,5},{5,1},{2,6},{6,2},{3,7},{7,3},{8,12},{12,8},{9,1... | collective-permute-start | bytes 1228808 | tf_op jit(solution)/shard_map/ppermute | solution.py:352
  14.5 6.6 %x_other.1 = (bf16[512,256]{1,0:T(8,128)(2,1)S(1)}, bf16[80,256]{1,0:T(8,128)(2,1)S(1)}) custom-call(s32[3]{0:T(128)S(1)} %pad_add_fusion.where, bf16[256,4096]{1,0:T(8,128)(2,1)S(1)} %copy-done, bf16[4096,2048]{1,0:T(8,128)(2,1)} %weight.8, bf16[800,256]{1,0:T(8,128)(2,1)S(1)} %first.1.refs_0_.refs_1_.refs_2_, ...), custom_call_target="tpu_custom_call" | custom-call | flops 1073741824 | bytes 6291456 | tf_op jit(solution)/shard_map/x_other/pallas_call | solution.py:324
  21.2 8.2 %x_own.1 = (bf16[1024,256]{1,0:T(8,128)(2,1)S(1)}, bf16[80,256]{1,0:T(8,128)(2,1)S(1)}) custom-call(s32[3]{0:T(128)S(1)} %pad_add_fusion.where, bf16[256,4096]{1,0:T(8,128)(2,1)S(1)} %copy-done, bf16[4096,2048]{1,0:T(8,128)(2,1)} %weight.8, bf16[800,256]{1,0:T(8,128)(2,1)S(1)} %first.1.refs_0_.refs_1_.refs_2_), custom_call_target="tpu_custom_call" | custom-call | flops 2147483648 | bytes 10485760 | tf_op jit(solution)/shard_map/x_own/pallas_call | solution.py:324
  29.4 2.1 %collective-permute-start.2 = (bf16[80,256]{1,0:T(8,128)(2,1)S(1)}, bf16[80,256]{1,0:T(8,128)(2,1)S(1)}, u32[]{:S(2)}, u32[]{:S(2)}) collective-permute-start(bf16[80,256]{1,0:T(8,128)(2,1)S(1)} %get-tuple-element.27), channel_id=1, source_target_pairs={{0,8},{8,16},{16,24},{24,0},{1,9},{9,17},{17,25},{25,1},{2,10},{10... | collective-permute-start | bytes 122888 | tf_op jit(solution)/shard_map/ppermute | solution.py:440
  31.5 2.5 %collective-permute-start.1 = (bf16[80,256]{1,0:T(8,128)(2,1)S(1)}, bf16[80,256]{1,0:T(8,128)(2,1)S(1)}, u32[]{:S(2)}, u32[]{:S(2)}) collective-permute-start(bf16[80,256]{1,0:T(8,128)(2,1)S(1)} %get-tuple-element.26), channel_id=1, source_target_pairs={{0,12},{4,8},{8,20},{12,16},{16,28},{20,24},{24,4},{28,0},{1,13},{... | collective-permute-start | bytes 122888 | tf_op jit(solution)/shard_map/ppermute | solution.py:436
  35.5 2.7 %collective-permute-done.1.refs_6_.refs_5_ = bf16[80,256]{1,0:T(8,128)(2,1)S(1)} collective-permute-done((bf16[80,256]{1,0:T(8,128)(2,1)S(1)}, bf16[80,256]{1,0:T(8,128)(2,1)S(1)}, u32[]{:S(2)}, u32[]{:S(2)}) %collective-permute-start.1) | collective-permute-done | bytes 40992 | tf_op jit(solution)/shard_map/ppermute | solution.py:436
  38.2 2.1 %state.2 = (bf16[256,256]{1,0:T(8,128)(2,1)S(1)}, f32[256,256]{1,0:T(8,128)S(1)}, bf16[288,256]{1,0:T(8,128)(2,1)S(1)}, bf16[256,512]{1,0:T(8,128)(2,1)S(1)}, bf...) custom-call(s32[3]{0:T(128)S(1)} %pad_add_fusion.where, ...), custom_call_target="tpu_custom_call" | custom-call | flops 50331648 | bytes 1572864 | tf_op jit(solution)/shard_map/state/pallas_call | solution.py:324
  40.4 1.9 %state.3 = (bf16[288,256]{1,0:T(8,128)(2,1)S(1)}, bf16[256,512]{1,0:T(8,128)(2,1)S(1)}, bf16[256,512]{1,0:T(8,128)(2,1)S(1)}, f32[8,256]{1,0:T(8,128)S(1)}, f32[256,8]{1,0:T(8,128)S(1)}) custom-call(s32[3]{0:T(128)S(1)} %pad_add_fusion.where, bf16[256,256]{1,0:T(8,128)(2,1)S(1)} %get-tuple-element.33.bc.refs_0_, ...), custom_call_target="tpu_custom_call" | custom-call | flops 50331648 | bytes 1572864 | tf_op jit(solution)/shard_map/state/pallas_call | solution.py:324
  42.4 2.0 %collective-permute-start.4 = (bf16[288,256]{1,0:T(8,128)(2,1)S(1)}, bf16[288,256]{1,0:T(8,128)(2,1)S(1)}, u32[]{:S(2)}, u32[]{:S(2)}) collective-permute-start(bf16[288,256]{1,0:T(8,128)(2,1)S(1)} %get-tuple-element.34.refs_0_), channel_id=1, source_target_pairs={{0,8},{8,0},{16,24},{24,16},{1,9},{9,1},{17,25},{25,17},{2,10},{10... | collective-permute-start | bytes 442376 | tf_op jit(solution)/shard_map/ppermute | solution.py:352
  44.4 6.6 %z_other.3 = bf16[512,256]{1,0:T(8,128)(2,1)S(1)} custom-call(s32[3]{0:T(128)S(1)} %pad_add_fusion.where, bf16[256,4096]{1,0:T(8,128)(2,1)S(1)} %copy-done.1, bf16[4096,2048]{1,0:T(8,128)(2,1)} %weight.11), custom_call_target="tpu_custom_call" | custom-call | flops 1073741824 | bytes 6291456 | tf_op jit(solution)/shard_map/z_other/pallas_call | solution.py:324
  51.0 1.6 %collective-permute-start.7 = (bf16[512,256]{1,0:T(8,128)(2,1)S(1)}, bf16[512,256]{1,0:T(8,128)(2,1)S(1)}, u32[]{:S(2)}, u32[]{:S(2)}) collective-permute-start(bf16[512,256]{1,0:T(8,128)(2,1)S(1)} %z_other.3), channel_id=1, source_target_pairs={{0,4},{4,0},{1,5},{5,1},{2,6},{6,2},{3,7},{7,3},{8,12},{12,8},{9,1... | collective-permute-start | bytes 786440 | tf_op jit(solution)/shard_map/ppermute | solution.py:352
  52.6 6.6 %z_other.2 = bf16[512,256]{1,0:T(8,128)(2,1)S(1)} custom-call(s32[3]{0:T(128)S(1)} %pad_add_fusion.where, bf16[256,4096]{1,0:T(8,128)(2,1)S(1)} %copy-done.1, bf16[4096,2048]{1,0:T(8,128)(2,1)} %weight.11), custom_call_target="tpu_custom_call" | custom-call | flops 1073741824 | bytes 6291456 | tf_op jit(solution)/shard_map/z_other/pallas_call | solution.py:324
  61.9 2.2 %collective-permute-start.5 = (bf16[288,256]{1,0:T(8,128)(2,1)S(1)}, bf16[288,256]{1,0:T(8,128)(2,1)S(1)}, u32[]{:S(2)}, u32[]{:S(2)}) collective-permute-start(bf16[288,256]{1,0:T(8,128)(2,1)S(1)} %combine.2), channel_id=1, source_target_pairs={{0,16},{8,24},{16,0},{24,8},{1,17},{9,25},{17,1},{25,9},{2,18},{10... | collective-permute-start | bytes 442376 | tf_op jit(solution)/shard_map/ppermute | solution.py:352
  64.1 8.2 %z_own.1.z_mine = bf16[1024,256]{1,0:T(8,128)(2,1)S(1)} custom-call(s32[3]{0:T(128)S(1)} %pad_add_fusion.where, bf16[256,4096]{1,0:T(8,128)(2,1)S(1)} %copy-done.1, bf16[4096,2048]{1,0:T(8,128)(2,1)} %weight.11), custom_call_target="tpu_custom_call" | custom-call | flops 2147483648 | bytes 10485760 | tf_op jit(solution)/shard_map/z_own/pallas_call | solution.py:324
  76.0 1.6 %collective-permute-start.11 = (bf16[512,256]{1,0:T(8,128)(2,1)S(1)}, bf16[512,256]{1,0:T(8,128)(2,1)S(1)}, u32[]{:S(2)}, u32[]{:S(2)}) collective-permute-start(bf16[512,256]{1,0:T(8,128)(2,1)S(1)} %gate.3.refs_1_), channel_id=1, source_target_pairs={{0,4},{4,0},{1,5},{5,1},{2,6},{6,2},{3,7},{7,3},{8,12},{12,8},{9,1... | collective-permute-start | bytes 786440 | tf_op jit(solution)/shard_map/ppermute | solution.py:352
  79.6 3.8 %collective-permute-done.11.refs_3_ = bf16[512,256]{1,0:T(8,128)(2,1)S(1)} collective-permute-done((bf16[512,256]{1,0:T(8,128)(2,1)S(1)}, bf16[512,256]{1,0:T(8,128)(2,1)S(1)}, u32[]{:S(2)}, u32[]{:S(2)}) %collective-permute-start.11) | collective-permute-done | bytes 262176 | tf_op jit(solution)/shard_map/ppermute | solution.py:352
  83.4 2.8 %collective-permute-done.10.refs_2_ = bf16[512,256]{1,0:T(8,128)(2,1)S(1)} collective-permute-done((bf16[512,256]{1,0:T(8,128)(2,1)S(1)}, bf16[512,256]{1,0:T(8,128)(2,1)S(1)}, u32[]{:S(2)}, u32[]{:S(2)}) %collective-permute-start.10) | collective-permute-done | bytes 262176 | tf_op jit(solution)/shard_map/ppermute | solution.py:352
  86.2 6.2 %out_far.1 = (bf16[256,1024]{1,0:T(8,128)(2,1)S(1)}, bf16[256,1024]{1,0:T(8,128)(2,1)S(1)}) custom-call(s32[3]{0:T(128)S(1)} %pad_add_fusion.where, bf16[2048,4096]{1,0:T(8,128)(2,1)} %weight.13, bf16[512,256]{1,0:T(8,128)(2,1)S(1)} %gate.2.refs_0_, bf16[512,256]{1,0:T(8,128)(2,1)S(1)} %gate.3.refs_1_, bf16[512,256]{1,0:T(8,128)(2,1)S(1)} %collective-permute-done.10.refs_2_, ...), custom_call_target="tpu_custom_call" | custom-call | flops 2147483648 | bytes 8388608 | tf_op jit(solution)/shard_map/out_far/pallas_call | solution.py:324
  92.5 6.2 %out_near.1 = (bf16[256,1024]{1,0:T(8,128)(2,1)S(1)}, bf16[256,1024]{1,0:T(8,128)(2,1)S(1)}) custom-call(s32[3]{0:T(128)S(1)} %pad_add_fusion.where, bf16[2048,4096]{1,0:T(8,128)(2,1)} %weight.13, bf16[512,256]{1,0:T(8,128)(2,1)S(1)} %gate.2.refs_0_, bf16[512,256]{1,0:T(8,128)(2,1)S(1)} %gate.3.refs_1_, ...), custom_call_target="tpu_custom_call" | custom-call | flops 2147483648 | bytes 8388608 | tf_op jit(solution)/shard_map/out_near/pallas_call | solution.py:324
  99.4 1.6 %collective-permute-start.14 = (bf16[256,1024]{1,0:T(8,128)(2,1)S(1)}, bf16[256,1024]{1,0:T(8,128)(2,1)S(1)}, u32[]{:S(2)}, u32[]{:S(2)}) collective-permute-start(bf16[256,1024]{1,0:T(8,128)(2,1)S(1)} %add_convert_fusion.1), channel_id=1, source_target_pairs={{0,2},{1,3},{2,0},{3,1},{4,6},{5,7},{6,4},{7,5},{8,10},{9,11},{10,... | collective-permute-start | bytes 1572872 | tf_op jit(solution)/shard_map/ppermute | solution.py:352
  101.0 12.3 %collective-permute-done.14 = bf16[256,1024]{1,0:T(8,128)(2,1)S(1)} collective-permute-done((bf16[256,1024]{1,0:T(8,128)(2,1)S(1)}, bf16[256,1024]{1,0:T(8,128)(2,1)S(1)}, u32[]{:S(2)}, u32[]{:S(2)}) %collective-permute-start.14) | collective-permute-done | bytes 524320 | tf_op jit(solution)/shard_map/ppermute | solution.py:352
  (46 shorter events, 13.0 us)
Async XLA Ops:
  0.1 1.6 %copy-start = (bf16[256,4096]{1,0:T(8,128)(2,1)S(1)}, bf16[256,4096]{1,0:T(8,128)(2,1)}, u32[]{:S(2)}) copy-start(bf16[256,4096]{1,0:T(8,128)(2,1)} %tok.11) | copy-start | bytes 6291460
  1.7 1.6 %copy-start.2 = (bf16[4096,256]{1,0:T(8,128)(2,1)S(1)}, bf16[4096,256]{1,0:T(8,128)(2,1)}, u32[]{:S(2)}) copy-start(bf16[4096,256]{1,0:T(8,128)(2,1)} %w_bc.1) | copy-start | bytes 6291460
  11.4 26.8 %copy-start.4 = (f32[2048,4]{0,1:T(4,128)S(1)}, f32[2048,4]{0,1:T(4,128)}, u32[]{:S(2)}) copy-start(f32[2048,4]{0,1:T(4,128)} %param.20) | copy-start | bytes 98308
  11.4 26.8 %copy-start.6 = (f32[256,4]{0,1:T(4,128)S(1)}, f32[256,4]{0,1:T(4,128)}, u32[]{:S(2)}) copy-start(f32[256,4]{0,1:T(4,128)} %param.21) | copy-start | bytes 12292
  11.4 26.8 %copy-start.8 = (f32[32]{0:T(128)S(1)}, f32[32]{0:T(128)}, u32[]{:S(2)}) copy-start(f32[32]{0:T(128)} %param.17) | copy-start | bytes 388
  11.5 26.8 %copy-start.9 = (f32[32]{0:T(128)S(1)}, f32[32]{0:T(128)}, u32[]{:S(2)}) copy-start(f32[32]{0:T(128)} %param.18) | copy-start | bytes 388
  11.5 22.6 %collective-permute-start = (bf16[800,256]{1,0:T(8,128)(2,1)S(1)}, bf16[800,256]{1,0:T(8,128)(2,1)S(1)}, u32[]{:S(2)}, u32[]{:S(2)}) collective-permute-start(bf16[800,256]{1,0:T(8,128)(2,1)S(1)} %first.1.refs_0_.refs_1_.refs_2_), channel_id=1, source_target_pairs={{0,4},{4,0},{1,5},{5,1},{2,6},{6,2},{3,7},{7,3},{8,12},{12,8},{9,1... | collective-permute-start | bytes 1228808 | tf_op jit(solution)/shard_map/ppermute | solution.py:352
  21.1 23.3 %copy-start.1 = (bf16[256,4096]{1,0:T(8,128)(2,1)S(1)}, bf16[256,4096]{1,0:T(8,128)(2,1)}, u32[]{:S(2)}) copy-start(bf16[256,4096]{1,0:T(8,128)(2,1)} %tok.11) | copy-start | bytes 6291460
  21.1 19.3 %collective-permute-start.6 = (bf16[512,256]{1,0:T(8,128)(2,1)S(1)}, bf16[512,256]{1,0:T(8,128)(2,1)S(1)}, u32[]{:S(2)}, u32[]{:S(2)}) collective-permute-start(bf16[512,256]{1,0:T(8,128)(2,1)S(1)} %get-tuple-element.35), channel_id=1, source_target_pairs={{0,4},{4,0},{1,5},{5,1},{2,6},{6,2},{3,7},{7,3},{8,12},{12,8},{9,1... | collective-permute-start | bytes 786440 | tf_op jit(solution)/shard_map/ppermute | solution.py:352
  29.4 6.2 %collective-permute-start.2 = (bf16[80,256]{1,0:T(8,128)(2,1)S(1)}, bf16[80,256]{1,0:T(8,128)(2,1)S(1)}, u32[]{:S(2)}, u32[]{:S(2)}) collective-permute-start(bf16[80,256]{1,0:T(8,128)(2,1)S(1)} %get-tuple-element.27), channel_id=1, source_target_pairs={{0,8},{8,16},{16,24},{24,0},{1,9},{9,17},{17,25},{25,1},{2,10},{10... | collective-permute-start | bytes 122888 | tf_op jit(solution)/shard_map/ppermute | solution.py:440
  31.5 6.7 %collective-permute-start.1 = (bf16[80,256]{1,0:T(8,128)(2,1)S(1)}, bf16[80,256]{1,0:T(8,128)(2,1)S(1)}, u32[]{:S(2)}, u32[]{:S(2)}) collective-permute-start(bf16[80,256]{1,0:T(8,128)(2,1)S(1)} %get-tuple-element.26), channel_id=1, source_target_pairs={{0,12},{4,8},{8,20},{12,16},{16,28},{20,24},{24,4},{28,0},{1,13},{... | collective-permute-start | bytes 122888 | tf_op jit(solution)/shard_map/ppermute | solution.py:436
  42.3 17.5 %collective-permute-start.8 = (bf16[288,256]{1,0:T(8,128)(2,1)S(1)}, bf16[288,256]{1,0:T(8,128)(2,1)S(1)}, u32[]{:S(2)}, u32[]{:S(2)}) collective-permute-start(bf16[288,256]{1,0:T(8,128)(2,1)S(1)} %get-tuple-element.40.refs_0_), channel_id=1, source_target_pairs={{0,8},{8,0},{16,24},{24,16},{1,9},{9,1},{17,25},{25,17},{2,10},{10... | collective-permute-start | bytes 442376 | tf_op jit(solution)/shard_map/ppermute | solution.py:352
  42.4 18.9 %collective-permute-start.4 = (bf16[288,256]{1,0:T(8,128)(2,1)S(1)}, bf16[288,256]{1,0:T(8,128)(2,1)S(1)}, u32[]{:S(2)}, u32[]{:S(2)}) collective-permute-start(bf16[288,256]{1,0:T(8,128)(2,1)S(1)} %get-tuple-element.34.refs_0_), channel_id=1, source_target_pairs={{0,8},{8,0},{16,24},{24,16},{1,9},{9,1},{17,25},{25,17},{2,10},{10... | collective-permute-start | bytes 442376 | tf_op jit(solution)/shard_map/ppermute | solution.py:352
  51.0 21.2 %copy-start.7 = (f32[32]{0:T(128)S(1)}, f32[32]{0:T(128)}, u32[]{:S(2)}) copy-start(f32[32]{0:T(128)} %param.19) | copy-start | bytes 388
  51.0 23.6 %copy-start.5 = (f32[2048]{0:T(1024)S(1)}, f32[2048]{0:T(1024)}, u32[]{:S(2)}) copy-start(f32[2048]{0:T(1024)} %param.22) | copy-start | bytes 24580
  51.0 23.6 %collective-permute-start.7 = (bf16[512,256]{1,0:T(8,128)(2,1)S(1)}, bf16[512,256]{1,0:T(8,128)(2,1)S(1)}, u32[]{:S(2)}, u32[]{:S(2)}) collective-permute-start(bf16[512,256]{1,0:T(8,128)(2,1)S(1)} %z_other.3), channel_id=1, source_target_pairs={{0,4},{4,0},{1,5},{5,1},{2,6},{6,2},{3,7},{7,3},{8,12},{12,8},{9,1... | collective-permute-start | bytes 786440 | tf_op jit(solution)/shard_map/ppermute | solution.py:352
  59.2 18.4 %collective-permute-start.3 = (bf16[512,256]{1,0:T(8,128)(2,1)S(1)}, bf16[512,256]{1,0:T(8,128)(2,1)S(1)}, u32[]{:S(2)}, u32[]{:S(2)}) collective-permute-start(bf16[512,256]{1,0:T(8,128)(2,1)S(1)} %z_other.2), channel_id=1, source_target_pairs={{0,4},{4,0},{1,5},{5,1},{2,6},{6,2},{3,7},{7,3},{8,12},{12,8},{9,1... | collective-permute-start | bytes 786440 | tf_op jit(solution)/shard_map/ppermute | solution.py:352
  60.4 14.2 %collective-permute-start.9 = (bf16[288,256]{1,0:T(8,128)(2,1)S(1)}, bf16[288,256]{1,0:T(8,128)(2,1)S(1)}, u32[]{:S(2)}, u32[]{:S(2)}) collective-permute-start(bf16[288,256]{1,0:T(8,128)(2,1)S(1)} %combine.3), channel_id=1, source_target_pairs={{0,16},{8,24},{16,0},{24,8},{1,17},{9,25},{17,1},{25,9},{2,18},{10... | collective-permute-start | bytes 442376 | tf_op jit(solution)/shard_map/ppermute | solution.py:352
  61.9 15.7 %collective-permute-start.5 = (bf16[288,256]{1,0:T(8,128)(2,1)S(1)}, bf16[288,256]{1,0:T(8,128)(2,1)S(1)}, u32[]{:S(2)}, u32[]{:S(2)}) collective-permute-start(bf16[288,256]{1,0:T(8,128)(2,1)S(1)} %combine.2), channel_id=1, source_target_pairs={{0,16},{8,24},{16,0},{24,8},{1,17},{9,25},{17,1},{25,9},{2,18},{10... | collective-permute-start | bytes 442376 | tf_op jit(solution)/shard_map/ppermute | solution.py:352
  76.0 7.3 %collective-permute-start.11 = (bf16[512,256]{1,0:T(8,128)(2,1)S(1)}, bf16[512,256]{1,0:T(8,128)(2,1)S(1)}, u32[]{:S(2)}, u32[]{:S(2)}) collective-permute-start(bf16[512,256]{1,0:T(8,128)(2,1)S(1)} %gate.3.refs_1_), channel_id=1, source_target_pairs={{0,4},{4,0},{1,5},{5,1},{2,6},{6,2},{3,7},{7,3},{8,12},{12,8},{9,1... | collective-permute-start | bytes 786440 | tf_op jit(solution)/shard_map/ppermute | solution.py:352
  79.0 7.2 %collective-permute-start.10 = (bf16[512,256]{1,0:T(8,128)(2,1)S(1)}, bf16[512,256]{1,0:T(8,128)(2,1)S(1)}, u32[]{:S(2)}, u32[]{:S(2)}) collective-permute-start(bf16[512,256]{1,0:T(8,128)(2,1)S(1)} %gate.2.refs_0_), channel_id=1, source_target_pairs={{0,4},{4,0},{1,5},{5,1},{2,6},{6,2},{3,7},{7,3},{8,12},{12,8},{9,1... | collective-permute-start | bytes 786440 | tf_op jit(solution)/shard_map/ppermute | solution.py:352
  92.4 6.8 %collective-permute-start.13 = (bf16[256,1024]{1,0:T(8,128)(2,1)S(1)}, bf16[256,1024]{1,0:T(8,128)(2,1)S(1)}, u32[]{:S(2)}, u32[]{:S(2)}) collective-permute-start(bf16[256,1024]{1,0:T(8,128)(2,1)S(1)} %get-tuple-element.44), channel_id=1, source_target_pairs={{0,1},{1,0},{2,3},{3,2},{4,5},{5,4},{6,7},{7,6},{8,9},{9,8},{10,11... | collective-permute-start | bytes 1572872 | tf_op jit(solution)/shard_map/ppermute | solution.py:352
  98.6 2.4 %collective-permute-start.12 = (bf16[256,1024]{1,0:T(8,128)(2,1)S(1)}, bf16[256,1024]{1,0:T(8,128)(2,1)S(1)}, u32[]{:S(2)}, u32[]{:S(2)}) collective-permute-start(bf16[256,1024]{1,0:T(8,128)(2,1)S(1)} %get-tuple-element.42), channel_id=1, source_target_pairs={{0,1},{1,0},{2,3},{3,2},{4,5},{5,4},{6,7},{7,6},{8,9},{9,8},{10,11... | collective-permute-start | bytes 1572872 | tf_op jit(solution)/shard_map/ppermute | solution.py:352
  99.4 13.9 %collective-permute-start.14 = (bf16[256,1024]{1,0:T(8,128)(2,1)S(1)}, bf16[256,1024]{1,0:T(8,128)(2,1)S(1)}, u32[]{:S(2)}, u32[]{:S(2)}) collective-permute-start(bf16[256,1024]{1,0:T(8,128)(2,1)S(1)} %add_convert_fusion.1), channel_id=1, source_target_pairs={{0,2},{1,3},{2,0},{3,1},{4,6},{5,7},{6,4},{7,5},{8,10},{9,11},{10,... | collective-permute-start | bytes 1572872 | tf_op jit(solution)/shard_map/ppermute | solution.py:352
  (1 other events, 0.9 us)

commit v2 on v1

--- a/solution.py
+++ b/solution.py
@@ -10,7 +10,7 @@
 Q = 256
 EPS = 1e-05
 HALO = 16
-VMEM_LIMIT = 48 * 1024 * 1024
+MIB = 1024 * 1024
 f32 = jnp.float32
 bf16 = jnp.bfloat16
 highest_mode = lax.Precision.HIGHEST
@@ -84,73 +84,172 @@
     return enter, state, decay
 
 
-def first_kernel(where, tok, w_x, w_bc, w_dt, msg, acc_x, acc_bc, acc_dt):
-    step = pl.program_id(0)
+def copies(pairs, sems):
+    started = []
+    for i, (source, target) in enumerate(pairs):
+        now = pltpu.make_async_copy(source, target, sems.at[i])
+        now.start()
+        started.append(now)
+    return started
+
+
+def product(tok, held, waits, acc, kb):
+    for i in range(tok.shape[1] // kb):
+        for wait in waits[i]:
+            wait.wait()
+        deep = slice(i * kb, (i + 1) * kb)
+        for low in range(0, acc.shape[1], 256):
+            cols = slice(low, min(low + 256, acc.shape[1]))
+            part = mm(tok[:, deep], held[deep, cols])
+            if i == 0:
+                acc[:, cols] = part
+            else:
+                acc[:, cols] += part
+
+
+def place():
+    return lax.axis_index("row"), lax.axis_index("col"), lax.axis_index("ctx")
+
+
+def first_kernel(tok, w_x, w_bc, w_dt, msg, edge, held_tok, held_x, held_bc, held_dt, acc_x, acc_bc, acc_dt, sems, *, chunks, kb):
     toks, lanes = acc_bc.shape
-
-    @pl.when(step == 0)
-    def _():
-        acc_x[...] = jnp.zeros_like(acc_x)
-        acc_bc[...] = jnp.zeros_like(acc_bc)
-        acc_dt[...] = jnp.zeros_like(acc_dt)
-
-    now = tok[...]
-    acc_x[...] += mm(now, w_x[...])
-    acc_bc[...] += mm(now, w_bc[...])
-    acc_dt[...] += mm_nt(w_dt[...], now)
-
-    @pl.when(step == pl.num_programs(0) - 1)
-    def _():
-        heads = acc_dt.shape[0]
-        msg[:toks, :] = acc_bc[...].astype(bf16)
-        msg[toks : toks + heads, :] = acc_dt[...].astype(bf16)
-        for j in range(acc_x.shape[1] // lanes):
-            low = toks + heads + j * toks
-            msg[low : low + toks, :] = acc_x[:, j * lanes : (j + 1) * lanes].astype(bf16)
-
-
-def product_kernel(where, tok, weight, *refs, edges):
-    step = pl.program_id(0)
-    out, acc = refs[edges or 0], refs[-1]
-    toks = tok.shape[0]
-    lanes = out.shape[1]
-
-    @pl.when(step == 0)
-    def _():
-        acc[...] = jnp.zeros_like(acc)
-
-    acc[...] += mm(tok[...], weight[...])
-
-    @pl.when(step == pl.num_programs(0) - 1)
-    def _():
-        for j in range(acc.shape[1] // lanes):
-            out[j * toks : (j + 1) * toks, :] = acc[:, j * lanes : (j + 1) * lanes].astype(bf16)
-        if edges is not None:
-            edge = refs[edges + 1]
-            for j in range(edges):
-                edge[j * HALO : (j + 1) * HALO, :] = refs[j][...]
-            for j in range(acc.shape[1] // lanes):
-                low = (edges + j) * HALO
-                edge[low : low + HALO, :] = acc[
-                    toks - HALO :, j * lanes : (j + 1) * lanes
-                ].astype(bf16)
+    width = acc_x.shape[1]
+    low = pl.multiple_of((1 - place()[0]) * chunks * width, width)
+    parts = tok.shape[1] // kb
+    pairs = []
+    for i in range(parts):
+        deep = pl.ds(i * kb, kb)
+        pairs += [
+            (tok.at[:, deep], held_tok.at[:, deep]),
+            (w_x.at[deep, pl.ds(low, width)], held_x.at[deep, :]),
+            (w_bc.at[deep, :], held_bc.at[deep, :]),
+            (w_dt.at[:, deep], held_dt.at[:, deep]),
+        ]
+    started = copies(pairs, sems)
+    for i in range(parts):
+        for wait in started[4 * i : 4 * i + 4]:
+            wait.wait()
+        deep = slice(i * kb, (i + 1) * kb)
+        now = held_tok[:, deep]
+        for acc, part in (
+            (acc_x, mm(now, held_x[deep, :])),
+            (acc_bc, mm(now, held_bc[deep, :])),
+            (acc_dt, mm_nt(held_dt[:, deep], now)),
+        ):
+            if i == 0:
+                acc[...] = part
+            else:
+                acc[...] += part
+    heads = acc_dt.shape[0]
+    msg[:toks, :] = acc_bc[...].astype(bf16)
+    msg[toks : toks + heads, :] = acc_dt[...].astype(bf16)
+    edge[:HALO, :] = acc_bc[toks - HALO :, :].astype(bf16)
+    for j in range(width // lanes):
+        low = toks + heads + j * toks
+        cols = slice(j * lanes, (j + 1) * lanes)
+        msg[low : low + toks, :] = acc_x[:, cols].astype(bf16)
+        edge[(1 + j) * HALO : (2 + j) * HALO, :] = acc_x[toks - HALO :, cols].astype(bf16)
+
+
+def second_kernel(tok, w_x, edge_in, msg, mine, edge_other, edge_own, held_tok, held, acc, sems, *, chunks, kb):
+    toks, width = acc.shape
+    lanes = msg.shape[1]
+    row = place()[0]
+    half = chunks * (msg.shape[0] // toks) * lanes
+    first = width - half
+    low_other = pl.multiple_of((2 - row) * half - first, lanes)
+    low_own = pl.multiple_of(row * half, lanes)
+    parts = tok.shape[1] // kb
+    pairs = []
+    for i in range(parts):
+        deep = pl.ds(i * kb, kb)
+        pairs += [
+            (tok.at[:, deep], held_tok.at[:, deep]),
+            (w_x.at[deep, pl.ds(low_other, first)], held.at[deep, pl.ds(0, first)]),
+            (w_x.at[deep, pl.ds(low_own, half)], held.at[deep, pl.ds(first, half)]),
+        ]
+    started = copies(pairs, sems)
+    product(held_tok, held, [started[3 * i : 3 * i + 3] for i in range(parts)], acc, kb)
+    per = msg.shape[0] // toks
+    base = edge_in.shape[0]
+    edge_other[:base, :] = edge_in[...]
+    edge_own[:HALO, :] = edge_in[:HALO, :]
+    for j in range(width // lanes):
+        now = acc[:, j * lanes : (j + 1) * lanes].astype(bf16)
+        if j < per:
+            msg[j * toks : (j + 1) * toks, :] = now
+            edge_other[base + j * HALO : base + (j + 1) * HALO, :] = now[toks - HALO :, :]
+        else:
+            i = j - per
+            mine[i * toks : (i + 1) * toks, :] = now
+            edge_own[(i + 1) * HALO : (i + 2) * HALO, :] = now[toks - HALO :, :]
+
+
+def gate_product_kernel(tok, weight, *refs, kb):
+    *outs, tok_out, held, acc, sems = refs
+    toks, width = acc.shape
+    lanes = outs[0].shape[1]
+    low = pl.multiple_of((1 - place()[0]) * width, width)
+    parts = tok.shape[1] // kb
+    pairs = []
+    for i in range(parts):
+        deep = pl.ds(i * kb, kb)
+        pairs += [
+            (tok.at[:, deep], tok_out.at[:, deep]),
+            (weight.at[deep, pl.ds(low, width)], held.at[deep, :]),
+        ]
+    started = copies(pairs, sems)
+    product(tok_out, held, [started[2 * i : 2 * i + 2] for i in range(parts)], acc, kb)
+    per = width // lanes // len(outs)
+    for j in range(width // lanes):
+        at_row = j % per * toks
+        outs[j // per][at_row : at_row + toks, :] = acc[:, j * lanes : (j + 1) * lanes].astype(bf16)
+
+
+def middle_kernel(tok, weight, w_out, scores, skip, *refs, chunks, kb, head_dim):
+    scans, refs = [refs[4 * c : 4 * c + 4] for c in range(chunks)], refs[4 * chunks :]
+    inners, refs = refs[:chunks], refs[chunks:]
+    mine, w_own, held, acc, sems = refs
+    toks, width = acc.shape
+    lanes = mine.shape[1]
+    where = place()
+    low = pl.multiple_of(where[0] * width, width)
+    parts = tok.shape[1] // kb
+    pairs = [
+        (weight.at[pl.ds(i * kb, kb), pl.ds(low, width)], held.at[pl.ds(i * kb, kb), :])
+        for i in range(parts)
+    ]
+    pairs += [
+        (w_out.at[pl.ds(low + i * lanes, lanes), :], w_own.at[pl.ds(i * lanes, lanes), :])
+        for i in range(width // lanes)
+    ]
+    started = copies(pairs, sems)
+    heads = width // head_dim
+    for c in range(chunks):
+        within(
+            where, scores, *scans[c], skip, inners[c], head_dim=head_dim,
+            first_of=c * heads // chunks, local_heads=heads,
+        )
+    product(tok, held, [[now] for now in started[:parts]], acc, kb)
+    for j in range(width // lanes):
+        mine[j * toks : (j + 1) * toks, :] = acc[:, j * lanes : (j + 1) * lanes].astype(bf16)
+    for now in started[parts:]:
+        now.wait()
 
 
 def state_kernel(
-    where, *refs, first, chunk, chunks, head_dim, state_dim, toks, lanes
+    *refs, first, chunk, chunks, head_dim, state_dim, toks, lanes
 ):
     refs = list(refs)
-    if first:
-        bc_mine, bc_theirs = refs.pop(0), refs.pop(0)
-    else:
+    if not first:
         bc_in = refs.pop(0)
-    dt_mine, dt_theirs, x_mine, x_theirs, edge_a, edge_b, taps_x, taps_bc, bias, decay = refs[:10]
+    mine, theirs, x_mine, x_theirs, edge_a, edge_b, taps_x, taps_bc, bias, decay = refs[:10]
     refs = refs[10:]
     if first:
         bc_out, scores = refs.pop(0), refs.pop(0)
     msg, scaled, conv_out, cum_out, cum_t_out, ext = refs
-    row, here = where[0], where[2]
-    blocks = x_mine.shape[0] // toks
+    row, _, here = place()
+    blocks = x_mine.shape[0] // toks // chunks
     heads = blocks * lanes // head_dim
     local_heads = heads * chunks
     inside = jnp.where(here > 0, 1.0, 0.0)
@@ -161,7 +260,7 @@
 
     if first:
         ext[:HALO, :] = halo(0)
-        ext[HALO:, :] = total(bc_mine[...], bc_theirs[...])
+        ext[HALO:, :] = total(mine[:toks, :], theirs[:toks, :])
         bc_now = silu(conv(ext, taps_bc[...], toks)).astype(bf16)
         bc_out[...] = bc_now
         b_now = bc_now[:, :state_dim]
@@ -172,8 +271,8 @@
     else:
         b_now = bc_in[:, :state_dim]
 
-    low = pl.multiple_of(row * local_heads, local_heads)
-    dt_sum = total(dt_mine[pl.ds(low, local_heads), :], dt_theirs[pl.ds(low, local_heads), :])
+    low = pl.multiple_of(toks + row * local_heads, local_heads)
+    dt_sum = total(mine[pl.ds(low, local_heads), :], theirs[pl.ds(low, local_heads), :])
     dt_sum = dt_sum[chunk * heads : (chunk + 1) * heads]
     first_head = row * local_heads + chunk * heads
     dt_now = softplus(dt_sum + pick(bias[...], first_head, heads))
@@ -194,13 +293,16 @@
     tail_wide = spread(dt_now * jnp.exp(last - cum), head_dim)
     through = spread(jnp.exp(jnp.broadcast_to(last, (heads, HALO))), head_dim)
     rows = state_dim + HALO
+    x_low = x_theirs.shape[0] - blocks * toks
+    taps_low = (row * chunks + chunk) * blocks * lanes
     for j in range(blocks):
         ext[:HALO, :] = halo(1 + chunk * blocks + j)
         ext[HALO:, :] = total(
-            x_mine[j * toks : (j + 1) * toks, :], x_theirs[j * toks : (j + 1) * toks, :]
+            x_mine[(chunk * blocks + j) * toks : (chunk * blocks + j + 1) * toks, :],
+            x_theirs[x_low + j * toks : x_low + (j + 1) * toks, :],
         )
         cols = slice(j * lanes, (j + 1) * lanes)
-        x_now = silu(conv(ext, taps_x[:, cols], toks))
+        x_now = silu(conv(ext, taps_x[:, pl.ds(pl.multiple_of(taps_low + j * lanes, lanes), lanes)], toks))
         conv_out[:, cols] = x_now.astype(bf16)
         scaled[:, cols] = (x_now * dt_wide[:, cols]).astype(bf16)
         state = mm_tn(b_now, (x_now * tail_wide[:, cols]).astype(bf16))
@@ -208,17 +310,17 @@
         msg[j * rows + state_dim : (j + 1) * rows, :] = through[:, cols].astype(bf16)
 
 
-def combine_kernel(where, *refs, state_dim, lanes):
+def combine_kernel(*refs, state_dim, lanes):
     *messages, out = refs
     rows = state_dim + HALO
     for j in range(out.shape[0] // rows):
         now = [m[j * rows : (j + 1) * rows, :] for m in messages]
-        _, state, decay = prefix(now, where[2], state_dim)
+        _, state, decay = prefix(now, place()[2], state_dim)
         out[j * rows : j * rows + state_dim, :] = state.astype(bf16)
         out[j * rows + state_dim : (j + 1) * rows, :] = jnp.broadcast_to(decay, (HALO, lanes)).astype(bf16)
 
 
-def inner_kernel(where, scores, scaled, conv_out, cum, cum_t, skip, out, *, head_dim, first_of, local_heads):
+def within(where, scores, scaled, conv_out, cum, cum_t, skip, out, *, head_dim, first_of, local_heads):
     toks, channels = scaled.shape
     pair = 2 * head_dim
     half = toks // 2
@@ -247,9 +349,12 @@
         out[half:, cols] = low + skips * conv_out[half:, cols].astype(f32)
 
 
-def gate_kernel(where, inner, bc, cum, z_mine, z_theirs, gain, *refs, head_dim, state_dim, lanes):
-    *messages, out = refs
+def gate_kernel(inner, bc, cum, z_mine, z_theirs, gain, *refs, messages, chunk, chunks, head_dim, state_dim, lanes):
+    messages, outs = refs[:messages], refs[messages:]
     toks = inner.shape[0]
+    part_toks = toks // len(outs)
+    row, _, here = place()
+    gain_low = (row * chunks + chunk) * inner.shape[1]
     rows = state_dim + HALO
     grown = spread(jnp.exp(cum[...]), head_dim)
     c_now = bc[:, state_dim:]
@@ -261,10 +366,11 @@
     mean_of = jnp.where(same, 1.0 / head_dim, 0.0).astype(bf16)
     for j in range(inner.shape[1] // lanes):
         now = [m[j * rows : (j + 1) * rows, :] for m in messages]
-        enter, _, _ = prefix(now, where[2], state_dim)
+        enter, _, _ = prefix(now, here, state_dim)
         cols = slice(j * lanes, (j + 1) * lanes)
         scanned = inner[:, cols] + grown[:, cols] * mm(c_now, enter.astype(bf16))
-        z_now = total(z_mine[j * toks : (j + 1) * toks, :], z_theirs[j * toks : (j + 1) * toks, :])
+        z_low = (chunk * inner.shape[1] // lanes + j) * toks
+        z_now = total(z_mine[z_low : z_low + toks, :], z_theirs[j * toks : (j + 1) * toks, :])
         gated = scanned * silu(z_now)
         square = gated * gated
         for i in range(lanes // wide):
@@ -273,43 +379,69 @@
             rest = (part - high.astype(f32)).astype(bf16)
             mean = mm(high, mean_of) + mm(rest, mean_of)
             low = j * lanes + i * wide
-            out[j * toks : (j + 1) * toks, i * wide : (i + 1) * wide] = (
+            done = (
                 gated[:, i * wide : (i + 1) * wide]
                 * lax.rsqrt(mean + EPS)
-                * gain[:, low : low + wide]
+                * gain[:, pl.ds(pl.multiple_of(gain_low + low, wide), wide)]
             ).astype(bf16)
-
-
-def out_kernel(where, weight, *refs, half):
+            for t, out in enumerate(outs):
+                out[j * part_toks : (j + 1) * part_toks, i * wide : (i + 1) * wide] = done[
+                    t * part_toks : (t + 1) * part_toks
+                ]
+
+
+def own_kernel(weight, w_own, *refs, groups):
+    *normed, partial, rest, whole, sems = refs
+    toks, width = partial.shape
+    lanes = normed[0].shape[1]
+    half = rest.shape[0]
+    other = pl.multiple_of((1 - place()[0]) * half, half)
+    started = copies(
+        [
+            (weight.at[pl.ds(other + i * lanes, lanes), :], rest.at[pl.ds(i * lanes, lanes), :])
+            for i in range(half // lanes)
+        ],
+        sems,
+    )
+    low = 0
+    for parts in groups:
+        chunk = [normed.pop(0) for _ in range(parts)]
+        part_toks = toks // parts
+        for j in range(chunk[0].shape[0] // part_toks):
+            for t, part in enumerate(chunk):
+                whole[t * part_toks : (t + 1) * part_toks, low : low + lanes] = part[
+                    j * part_toks : (j + 1) * part_toks, :
+                ]
+            low += lanes
+    for low in range(0, width, 512):
+        cols = slice(low, min(low + 512, width))
+        partial[:, cols] = mm(whole[...], w_own[:, cols])
+    for now in started:
+        now.wait()
+
+
+def rest_kernel(partial, rest, *refs, part, parts, pair_of, groups):
     *normed, send, keep = refs
-    step = pl.program_id(0)
+    part_toks, piece = send.shape
     lanes = normed[0].shape[1]
-    toks = send.shape[0]
-    width = weight.shape[1]
-    per_send = send.shape[1] // width
-    acc = None
-    for side in range(2):
-        low = jnp.where(side == 0, where[0], 1 - where[0]) * half
-        at = 0
-        for chunk in normed[side * (len(normed) // 2) : (side + 1) * (len(normed) // 2)]:
-            for j in range(chunk.shape[0] // toks):
-                rows = pl.ds(pl.multiple_of(low + at, lanes), lanes)
-                part = mm(chunk[j * toks : (j + 1) * toks, :], weight[rows, :])
-                acc = part if acc is None else acc + part
-                at += lanes
-    done = acc.astype(bf16)
-
-    @pl.when(step < per_send)
-    def _():
-        send[:, pl.ds(pl.multiple_of(step * width, width), width)] = done
-
-    @pl.when(step >= per_send)
-    def _():
-        keep[:, pl.ds(pl.multiple_of((step - per_send) * width, width), width)] = done
-
-
-def add_kernel(a, b, out):
-    out[...] = (a[...].astype(f32) + b[...].astype(f32)).astype(bf16)
+    toks = partial.shape[0]
+    rows = slice(part * part_toks, (part + 1) * part_toks)
+    step = min(512, piece)
+    where = place()
+    for target, core in ((send, 1 - where[1] % 2), (keep, where[1] % 2)):
+        base = (pair_of(where) * 2 + core) * piece
+        for low in range(0, piece, step):
+            cols = pl.ds(pl.multiple_of(base + low, step), step)
+            acc = partial[rows, cols]
+            block = 0
+            for chunk, pieces in zip(normed, groups):
+                held_toks = toks // pieces
+                first = part * part_toks if pieces == 1 else 0
+                for j in range(chunk.shape[0] // held_toks):
+                    now = chunk[j * held_toks + first : j * held_toks + first + part_toks, :]
+                    acc = acc + mm(now, rest[block * lanes : (block + 1) * lanes, cols])
+                    block += 1
+            target[:, low : low + step] = acc.astype(bf16)
 
 
 def sds(*shape, dtype=bf16):
@@ -320,31 +452,21 @@
     return pl.CostEstimate(flops=int(flops), bytes_accessed=int(size), transcendentals=0)
 
 
-def call(kernel, where, args, specs, outs, out_specs, scratch=(), grid=(1,), flops=0, size=0, name=None):
+def call(kernel, args, specs, outs, scratch=(), flops=0, size=0, name=None, mib=16):
     return pl.pallas_call(
         kernel,
-        grid_spec=pltpu.PrefetchScalarGridSpec(
-            num_scalar_prefetch=1,
-            grid=grid,
-            in_specs=specs,
-            out_specs=out_specs,
-            scratch_shapes=list(scratch),
-        ),
+        in_specs=specs or [IN_VMEM] * len(args),
+        out_specs=[IN_VMEM] * len(outs),
+        scratch_shapes=list(scratch),
         out_shape=outs,
-        compiler_params=pltpu.CompilerParams(
-            dimension_semantics=("arbitrary",) * len(grid), vmem_limit_bytes=VMEM_LIMIT
-        ),
+        compiler_params=pltpu.CompilerParams(vmem_limit_bytes=mib * MIB),
         cost_estimate=cost(flops, size),
         name=name,
-    )(where, *args)
-
-
-def whole(shape):
-    return pl.BlockSpec(shape, lambda i, w: (0,) * len(shape))
-
-
-def at(shape, index):
-    return pl.BlockSpec(shape, index)
+    )(*args)
+
+
+IN_VMEM = pl.BlockSpec(memory_space=pltpu.VMEM)
+IN_HBM = pl.BlockSpec(memory_space=pltpu.HBM)
 
 
 def swapped(shard, axis, by):
@@ -370,112 +492,83 @@
     chunk_heads = local_heads // chunks
     out_cols = proj_out.shape[1]
     ctx_size = lax.axis_size("ctx")
-    row, col, ctx = lax.axis_index("row"), lax.axis_index("col"), lax.axis_index("ctx")
-    where = jnp.stack([row, col, ctx]).astype(jnp.int32)
     conv_x_t, conv_bc_t, proj_dt_t = conv_x.T, conv_bc.T, proj_dt.T
     bias, decay, skip, gain = (v[None] for v in (dt_bias, decay_rate, skip_gain, norm_gain))
 
     kb = depth // 8
-    tok_spec = at((toks, kb), lambda k, w: (0, k))
-    msg_rows = toks + heads + blocks * toks
-    msg_first = call(
-        first_kernel,
-        where,
+    parts = depth // kb
+    edge_rows = (1 + chunks * blocks) * HALO
+    msg_first, edge_first = call(
+        functools.partial(first_kernel, chunks=chunks, kb=kb),
         (tokens, proj_x, proj_bc, proj_dt_t),
+        [IN_HBM] * 4,
+        [sds(toks + heads + blocks * toks, lanes), sds((1 + blocks) * HALO, lanes)],
         [
-            tok_spec,
-            at((kb, width), lambda k, w: (k, (1 - w[0]) * chunks)),
-            at((kb, lanes), lambda k, w: (k, 0)),
-            at((heads, kb), lambda k, w: (0, k)),
+            pltpu.VMEM((toks, depth), bf16),
+            pltpu.VMEM((depth, width), bf16),
+            pltpu.VMEM((depth, lanes), bf16),
+            pltpu.VMEM((heads, depth), bf16),
+            pltpu.VMEM((toks, width), f32),
+            pltpu.VMEM((toks, lanes), f32),
+            pltpu.VMEM((heads, toks), f32),
+            pltpu.SemaphoreType.DMA((4 * parts,)),
         ],
-        sds(msg_rows, lanes),
-        whole((msg_rows, lanes)),
-        [pltpu.VMEM((toks, width), f32), pltpu.VMEM((toks, lanes), f32), pltpu.VMEM((heads, toks), f32)],
-        grid=(depth // kb,),
         flops=2 * toks * depth * (width + lanes + heads),
         size=2 * depth * (toks + width + lanes + heads),
         name="first",
+        mib=60,
     )
     first_got = swapped(msg_first, "row", 1)
-
-    def product(weight, n_cols, col_of, edge_blocks, name):
-        edge_args = [msg_first] * len(edge_blocks)
-        edge_specs = [at((HALO, lanes), lambda k, w, e=e: (e, 0)) for e in edge_blocks]
-        out_rows = n_cols // lanes * toks
-        outs, out_specs = [sds(out_rows, lanes)], [whole((out_rows, lanes))]
-        edges = None
-        if edge_blocks:
-            edges = len(edge_blocks)
-            edge_rows = (edges + n_cols // lanes) * HALO
-            outs.append(sds(edge_rows, lanes))
-            out_specs.append(whole((edge_rows, lanes)))
-        return call(
-            functools.partial(product_kernel, edges=edges),
-            where,
-            (tokens, weight, *edge_args),
-            [tok_spec, at((kb, n_cols), lambda k, w: (k, col_of(w))), *edge_specs],
-            outs,
-            out_specs,
-            [pltpu.VMEM((toks, n_cols), f32)],
-            grid=(depth // kb,),
-            flops=2 * toks * depth * n_cols,
-            size=2 * depth * (toks + n_cols),
-            name=name,
-        )
-
-    def last_rows(low):
-        return (low + toks) // HALO - 1
-
-    bc_edge = last_rows(0)
-    x_edges = [last_rows(toks + heads + j * toks) for j in range(blocks)]
-    msg_second, edge_other = product(
-        proj_x, width, lambda w: (1 - w[0]) * chunks + 1, [bc_edge, *x_edges], "x_other"
+    msg_second, x_mine, edge_other, edge_own = call(
+        functools.partial(second_kernel, chunks=chunks, kb=kb),
+        (tokens, proj_x, edge_first),
+        [IN_HBM, IN_HBM, IN_VMEM],
+        [sds(blocks * toks, lanes), sds(chunks * blocks * toks, lanes), *[sds(edge_rows, lanes)] * 2],
+        [
+            pltpu.VMEM((toks, depth), bf16),
+            pltpu.VMEM((depth, width + half), bf16),
+            pltpu.VMEM((toks, width + half), f32),
+            pltpu.SemaphoreType.DMA((3 * parts,)),
+        ],
+        flops=2 * toks * depth * (width + half),
+        size=2 * depth * (toks + width + half),
+        name="second",
+        mib=52,
     )
     second_got = swapped(msg_second, "row", 1)
     down = [(i, (i + 1) % ctx_size) for i in range(ctx_size)]
     edge_a = lax.ppermute(
         edge_other, ("ctx", "row"), [(2 * i + s, 2 * j + 1 - s) for i, j in down for s in range(2)]
     )
-    x_mine, edge_own = product(proj_x, half, lambda w: w[0], [bc_edge], "x_own")
     edge_b = lax.ppermute(edge_own, "ctx", down)
-    z_send = [
-        product(proj_z, width, lambda w, c=c: (1 - w[0]) * chunks + c, [], "z_other")[0]
-        for c in range(chunks)
-    ]
+    *z_send, tok_held = call(
+        functools.partial(gate_product_kernel, kb=kb),
+        (tokens, proj_z),
+        [IN_HBM] * 2,
+        [*[sds(blocks * toks, lanes)] * chunks, sds(toks, depth)],
+        [
+            pltpu.VMEM((depth, half), bf16),
+            pltpu.VMEM((toks, half), f32),
+            pltpu.SemaphoreType.DMA((2 * parts,)),
+        ],
+        flops=2 * toks * depth * half,
+        size=2 * depth * (toks + half),
+        name="z_other",
+        mib=50,
+    )
     z_got = [swapped(z, "row", 1) for z in z_send]
-    z_mine = product(proj_z, half, lambda w: w[0], [], "z_own")[0]
-
-    edge_shape = edge_a.shape
+
     rows = state_dim + HALO
-    kernel_sizes = dict(head_dim=head_dim, state_dim=state_dim, lanes=lanes)
+    sizes = dict(head_dim=head_dim, state_dim=state_dim, lanes=lanes)
     states, scans = [], []
     bc_now = scores = None
     for c in range(chunks):
-        dt_at = at((heads, lanes), lambda k, w: (toks // heads, 0))
-        args, specs = [], []
-        outs, out_specs = [], []
-        if c == 0:
-            args += [msg_first, first_got]
-            specs += [at((toks, lanes), lambda k, w: (0, 0))] * 2
-            outs += [sds(toks, lanes), sds(toks, toks, dtype=f32)]
-            out_specs += [whole((toks, lanes)), whole((toks, toks))]
-        else:
-            args += [bc_now]
-            specs += [whole((toks, lanes))]
-        x_theirs = first_got[toks + heads :] if c == 0 else second_got
-        args += [msg_first, first_got, x_mine, x_theirs, edge_a, edge_b, conv_x_t, conv_bc_t, bias, decay]
-        specs += [
-            dt_at,
-            dt_at,
-            at((blocks * toks, lanes), lambda k, w, c=c: (c, 0)),
-            whole((blocks * toks, lanes)),
-            whole(edge_shape),
-            whole(edge_shape),
-            at((taps, width), lambda k, w, c=c: (0, w[0] * chunks + c)),
-            whole((taps, lanes)),
-            whole((1, heads)),
-            whole((1, heads)),
+        args = [] if c == 0 else [bc_now]
+        args += [
+            msg_first, first_got, x_mine, first_got if c == 0 else second_got, edge_a, edge_b,
+            conv_x_t, conv_bc_t, bias, decay,
         ]
+        outs = [sds(toks, lanes), sds(toks, toks, dtype=f32)] if c == 0 else []
         outs += [
             sds(blocks * rows, lanes),
             sds(toks, width),
@@ -483,18 +576,20 @@
             sds(chunk_heads, toks, dtype=f32),
             sds(toks, chunk_heads, dtype=f32),
         ]
-        out_specs += [whole(o.shape) for o in outs[len(out_specs) :]]
         got = call(
             functools.partial(
-                state_kernel, first=c == 0, chunk=c, chunks=chunks, toks=toks, **kernel_sizes
+                state_kernel, first=c == 0, chunk=c, chunks=chunks, toks=toks, **sizes
             ),
-            where, args, specs, outs, out_specs,
+            args,
+            None,
+            outs,
             [pltpu.VMEM((HALO + toks, lanes), f32)],
-            flops=2 * toks * width * (state_dim + 64), size=2 * toks * width * 6, name="state",
+            flops=2 * toks * width * (state_dim + 64),
+            size=2 * toks * width * 6,
+            name="state",
         )
         if c == 0:
-            bc_now, scores = got[:2]
-            got = got[2:]
+            bc_now, scores, *got = got
         states.append(got[0])
         scans.append(got[1:])
 
@@ -505,86 +600,87 @@
         by = 1
         while by < ctx_size:
             if by > 1:
-                send = call(
+                (send,) = call(
                     functools.partial(combine_kernel, state_dim=state_dim, lanes=lanes),
-                    where, heard, [whole(send.shape)] * len(heard), sds(*send.shape), whole(send.shape),
+                    heard, None, [sds(*send.shape)],
                     flops=send.size * 6, size=send.size * 6, name="combine",
                 )
             heard.append(swapped(send, "ctx", by))
             by *= 2
         messages.append(heard)
 
-    inners = []
+    args = (tok_held, proj_z, proj_out, scores, skip, *[a for scan in scans for a in scan])
+    *inners, z_mine, w_own = call(
+        functools.partial(middle_kernel, chunks=chunks, kb=kb, head_dim=head_dim),
+        args,
+        [IN_VMEM, IN_HBM, IN_HBM, *[IN_VMEM] * (len(args) - 3)],
+        [*[sds(toks, width, dtype=f32)] * chunks, sds(chunks * blocks * toks, lanes), sds(half, out_cols)],
+        [
+            pltpu.VMEM((depth, half), bf16),
+            pltpu.VMEM((toks, half), f32),
+            pltpu.SemaphoreType.DMA((parts + half // lanes,)),
+        ],
+        flops=2 * toks * half * (depth + 2 * toks),
+        size=2 * depth * half + 2 * half * out_cols,
+        name="middle",
+        mib=38,
+    )
+
+    normed, normed_got = [], []
+    groups = [1] * (chunks - 1) + [2]
     for c in range(chunks):
-        scaled, conv_out, cum, cum_t = scans[c]
-        args = (scores, scaled, conv_out, cum, cum_t, skip)
-        inners.append(
-            call(
-                functools.partial(
-                    inner_kernel, head_dim=head_dim, first_of=c * chunk_heads, local_heads=local_heads
-                ),
-                where, args, [whole(a.shape) for a in args], sds(toks, width, dtype=f32),
-                whole((toks, width)), flops=chunk_heads * 2 * toks * toks * 2 * head_dim,
-                size=2 * toks * width * 5, name="inner",
-            )
-        )
-
-    normed, normed_got = [], []
-    for c in range(chunks):
-        cum = scans[c][2]
-        args = (inners[c], bc_now, cum, z_mine, z_got[c], gain, *messages[c])
         now = call(
-            functools.partial(gate_kernel, **kernel_sizes),
-            where,
-            args,
-            [
-                whole((toks, width)),
-                whole((toks, lanes)),
-                whole(cum.shape),
-                at((blocks * toks, lanes), lambda k, w, c=c: (c, 0)),
-                whole((blocks * toks, lanes)),
-                at((1, width), lambda k, w, c=c: (0, w[0] * chunks + c)),
-                *[whole(m.shape) for m in messages[c]],
-            ],
-            sds(blocks * toks, lanes),
-            whole((blocks * toks, lanes)),
-            flops=2 * toks * width * (state_dim + 4 * head_dim), size=2 * toks * width * 6, name="gate",
+            functools.partial(gate_kernel, messages=len(messages[c]), chunk=c, chunks=chunks, **sizes),
+            (inners[c], bc_now, scans[c][2], z_mine, z_got[c], gain, *messages[c]),
+            None,
+            [sds(blocks * toks // groups[c], lanes)] * groups[c],
+            flops=2 * toks * width * (state_dim + 4 * head_dim),
+            size=2 * toks * width * 6,
+            name="gate",
         )
         normed.append(now)
-        normed_got.append(swapped(now, "row", 1))
+        normed_got.append([swapped(part, "row", 1) for part in now])
 
     piece = out_cols // lax.axis_size("col")
-    tile = piece // 2
-    per = piece // tile
-
-    def out_half(pair_of, name):
-        def weight_at(n, w):
-            core = jnp.where(n < per, 1 - w[1] % 2, w[1] % 2)
-            return (0, (pair_of(w) * 2 + core) * per + n % per)
-
-        args = (proj_out, *normed, *normed_got)
+    args = (proj_out, w_own, *[part for now in normed for part in now])
+    partial, rest = call(
+        functools.partial(own_kernel, groups=groups),
+        args,
+        [IN_HBM, *[IN_VMEM] * (len(args) - 1)],
+        [sds(toks, out_cols, dtype=f32), sds(half, out_cols)],
+        [pltpu.VMEM((toks, half), bf16), pltpu.SemaphoreType.DMA((half // lanes,))],
+        flops=2 * toks * half * out_cols,
+        size=2 * half * out_cols,
+        name="out_own",
+        mib=26,
+    )
+
+    def out_rest(part, parts, pair_of, name):
+        args = (partial, rest, *[now[part] if len(now) > 1 else now[0] for now in normed_got])
         return call(
-            functools.partial(out_kernel, half=half),
-            where,
+            functools.partial(
+                rest_kernel, part=part, parts=parts, pair_of=pair_of,
+                groups=[len(now) if parts > 1 else 1 for now in normed_got],
+            ),
             args,
-            [at((proj_out.shape[0], tile), weight_at), *[whole(a.shape) for a in args[1:]]],
-            [sds(toks, piece)] * 2,
-            [whole((toks, piece))] * 2,
-            grid=(2 * per,),
-            flops=2 * toks * proj_out.shape[0] * 2 * piece,
-            size=2 * proj_out.shape[0] * 2 * piece,
+            None,
+            [sds(toks // parts, piece)] * 2,
+            flops=2 * toks // parts * half * 2 * piece,
+            size=half * 2 * piece,
             name=name,
         )
 
     def added(a, b):
         return (a.astype(f32) + b.astype(f32)).astype(bf16)
 
-    far_send, far_keep = out_half(lambda w: 1 - w[1] // 2, "out_far")
-    far = added(far_keep, swapped(far_send, "col", 1))
-    far_got = swapped(far, "col", 2)
-    near_send, near_keep = out_half(lambda w: w[1] // 2, "out_near")
-    near = near_keep.astype(f32) + swapped(near_send, "col", 1).astype(f32)
-    return (near + far_got.astype(f32)).astype(bf16)
+    parts = groups[-1]
+    far = [out_rest(part, parts, lambda w: 1 - w[1] // 2, "out_far") for part in range(parts)]
+    far = [added(keep, swapped(send, "col", 1)) for send, keep in far]
+    far_got = [swapped(now, "col", 2) for now in far]
+    near = [out_rest(part, parts, lambda w: w[1] // 2, "out_near") for part in range(parts)]
+    near_keep, near_send = (jnp.concatenate([now[i] for now in near]) for i in (1, 0))
+    total_near = near_keep.astype(f32) + swapped(near_send, "col", 1).astype(f32)
+    return (total_near + jnp.concatenate(far_got).astype(f32)).astype(bf16)
 
 
 def shifted(shard, axis, by):

time: 115 us -> 80.6 us (0.70)
  Pallas kernels: 66.1 us -> 36.3 us
  local copies, waits for them, and re-layouts: 4.19 us -> 0.77 us
  waiting for transfers between devices: 23.1 us -> 20.3 us
  starting transfers between devices: 19.4 us -> 21.1 us
    pallas_call x16 -> x15, Pallas kernels: 66.1 us -> 36.3 us  [call(): pl.pallas_call(kernel, in_specs=specs or [IN_VMEM] * len(args), out_specs...]
    unnamed x20 -> x16, local copies, waits for them, and re-layouts: 4.18 us -> 0.77 us
    ppermute x13 -> x16, waiting for transfers between devices: 18.9 us -> 16.1 us  [swapped(): return lax.ppermute(shard, axis, [(i, i ^ by) for i in range(devices)])]
    ppermute x13 -> x16, starting transfers between devices: 14.8 us -> 16.5 us  [swapped(): return lax.ppermute(shard, axis, [(i, i ^ by) for i in range(devices)])]
  transfers between devices with their start and end apart: 15 -> 18, of which waited for: 5 -> 7; matrix products, arithmetic and copies ran while one was open for 0% -> 0% of each run, Pallas kernels for 44% -> 37%
where the time goes in v2:
time: 80.6 us; the launch traced here: 79.9 us
  Pallas kernels  36.3 us (45%)
  starting transfers between devices  21.1 us (26%)
  waiting for transfers between devices  20.3 us (25%)
  other arithmetic  1.22 us (2%)
    pallas_call x15, Pallas kernels, call(): pl.pallas_call(kernel, in_specs=specs or [IN_VMEM] * len(args), out_specs...  36.3 us
    ppermute x16, starting transfers between devices, swapped(): return lax.ppermute(shard, axis, [(i, i ^ by) for i in range(devices)])  16.5 us
    ppermute x16, waiting for transfers between devices, swapped(): return lax.ppermute(shard, axis, [(i, i ^ by) for i in range(devices)])  16.1 us
    ppermute x1, starting transfers between devices, fast(): lax.ppermute(edge_other, ('ctx', 'row'), [(2 * i + s, 2 * j + 1 - s) for...  3.02 us
    ppermute x1, waiting for transfers between devices, fast(): lax.ppermute(edge_other, ('ctx', 'row'), [(2 * i + s, 2 * j + 1 - s) for...  2.76 us
  transfers between devices with their start and end apart: 18, of which 7 were waited for; matrix products, arithmetic and copies ran while one was open for 0% of the time, Pallas kernels for 37%

profile of v2, /device:TPU:0, one launch (start us, length us, event | category | flops | bytes accessed | tf_op | source)
XLA Modules:
  0.0 79.9 jit_solution(7036976254927632908)
XLA Ops:
  0.0 5.0 %first.1 = (bf16[800,256]{1,0:T(8,128)(2,1)}, bf16[48,256]{1,0:T(8,128)(2,1)}) custom-call(bf16[256,4096]{1,0:T(8,128)(2,1)} %tok.5, bf16[4096,2048]{1,0:T(8,128)(2,1)} %w_x.3, bf16[4096,256]{1,0:T(8,128)(2,1)} %w_bc.1, bf16[32,4096]{1,0:T(8,128)(2,1)} %bitcast.18), custom_call_target="tpu_custom_call" | custom-call | flops 1677721600 | bytes 8650752 | tf_op jit(solution)/shard_map/first/pallas_call | solution.py:456
  5.0 3.0 %collective-permute-start = (bf16[800,256]{1,0:T(8,128)(2,1)}, bf16[800,256]{1,0:T(8,128)(2,1)S(1)}, u32[]{:S(2)}, u32[]{:S(2)}) collective-permute-start(bf16[800,256]{1,0:T(8,128)(2,1)} %get-tuple-element.43.refs_0_.refs_1_), channel_id=1, source_target_pairs={{0,4},{4,0},{1,5},{5,1},{2,6},{6,2},{3,7},{7,3},{8,12},{12,8},{9,1... | collective-permute-start | bytes 1228808 | tf_op jit(solution)/shard_map/ppermute | solution.py:474
  8.8 6.1 %second.1 = (bf16[512,256]{1,0:T(8,128)(2,1)S(1)}, bf16[1024,256]{1,0:T(8,128)(2,1)S(1)}, bf16[80,256]{1,0:T(8,128)(2,1)S(1)}, bf16[80,256]{1,0:T(8,128)(2,1)S(1)}) custom-call(bf16[256,4096]{1,0:T(8,128)(2,1)} %tok.5, bf16[4096,2048]{1,0:T(8,128)(2,1)} %w_x.3, bf16[48,256]{1,0:T(8,128)(2,1)S(1)} %copy-done.3), custom_call_target="tpu_custom_call" | custom-call | flops 3221225472 | bytes 14680064 | tf_op jit(solution)/shard_map/second/pallas_call | solution.py:456
  15.0 3.0 %collective-permute-start.1 = (bf16[80,256]{1,0:T(8,128)(2,1)S(1)}, bf16[80,256]{1,0:T(8,128)(2,1)S(1)}, u32[]{:S(2)}, u32[]{:S(2)}) collective-permute-start(bf16[80,256]{1,0:T(8,128)(2,1)S(1)} %get-tuple-element.46), channel_id=1, source_target_pairs={{0,12},{4,8},{8,20},{12,16},{16,28},{20,24},{24,4},{28,0},{1,13},{... | collective-permute-start | bytes 122888 | tf_op jit(solution)/shard_map/ppermute | solution.py:540
  18.0 1.6 %collective-permute-start.2 = (bf16[80,256]{1,0:T(8,128)(2,1)S(1)}, bf16[80,256]{1,0:T(8,128)(2,1)S(1)}, u32[]{:S(2)}, u32[]{:S(2)}) collective-permute-start(bf16[80,256]{1,0:T(8,128)(2,1)S(1)} %get-tuple-element.47), channel_id=1, source_target_pairs={{0,8},{8,16},{16,24},{24,0},{1,9},{9,17},{17,25},{25,1},{2,10},{10... | collective-permute-start | bytes 122888 | tf_op jit(solution)/shard_map/ppermute | solution.py:543
  19.6 2.8 %collective-permute-done.1.refs_4_.refs_5_ = bf16[80,256]{1,0:T(8,128)(2,1)S(1)} collective-permute-done((bf16[80,256]{1,0:T(8,128)(2,1)S(1)}, bf16[80,256]{1,0:T(8,128)(2,1)S(1)}, u32[]{:S(2)}, u32[]{:S(2)}) %collective-permute-start.1) | collective-permute-done | bytes 40992 | tf_op jit(solution)/shard_map/ppermute | solution.py:540
  22.4 1.5 %collective-permute-done.2.refs_5_.refs_6_ = bf16[80,256]{1,0:T(8,128)(2,1)S(1)} collective-permute-done((bf16[80,256]{1,0:T(8,128)(2,1)S(1)}, bf16[80,256]{1,0:T(8,128)(2,1)S(1)}, u32[]{:S(2)}, u32[]{:S(2)}) %collective-permute-start.2) | collective-permute-done | bytes 40992 | tf_op jit(solution)/shard_map/ppermute | solution.py:543
  23.9 1.6 %state.2 = (bf16[256,256]{1,0:T(8,128)(2,1)S(1)}, f32[256,256]{1,0:T(8,128)S(1)}, bf16[288,256]{1,0:T(8,128)(2,1)S(1)}, bf16[256,512]{1,0:T(8,128)(2,1)S(1)}, bf...) custom-call(bf16[800,256]{1,0:T(8,128)(2,1)S(1)} %copy-done, ...), custom_call_target="tpu_custom_call" | custom-call | flops 50331648 | bytes 1572864 | tf_op jit(solution)/shard_map/state/pallas_call | solution.py:456
  25.4 1.4 %state.3 = (bf16[288,256]{1,0:T(8,128)(2,1)S(1)}, bf16[256,512]{1,0:T(8,128)(2,1)S(1)}, bf16[256,512]{1,0:T(8,128)(2,1)S(1)}, f32[8,256]{1,0:T(8,128)S(1)}, f32[256,8]{1,0:T(8,128)S(1)}) custom-call(bf16[256,256]{1,0:T(8,128)(2,1)S(1)} %get-tuple-element.53.refs_0_.bc, bf16[800,256]{1,0:T(8,128)(2,1)S(1)} %copy-done, ...), custom_call_target="tpu_custom_call" | custom-call | flops 50331648 | bytes 1572864 | tf_op jit(solution)/shard_map/state/pallas_call | solution.py:456
  27.5 1.4 %collective-permute-start.5 = (bf16[288,256]{1,0:T(8,128)(2,1)S(1)}, bf16[288,256]{1,0:T(8,128)(2,1)S(1)}, u32[]{:S(2)}, u32[]{:S(2)}) collective-permute-start(bf16[288,256]{1,0:T(8,128)(2,1)S(1)} %get-tuple-element.63.refs_0_), channel_id=1, source_target_pairs={{0,8},{8,0},{16,24},{24,16},{1,9},{9,1},{17,25},{25,17},{2,10},{10... | collective-permute-start | bytes 442376 | tf_op jit(solution)/shard_map/ppermute | solution.py:474
  28.9 4.6 %z_other.1 = (bf16[512,256]{1,0:T(8,128)(2,1)S(1)}, bf16[512,256]{1,0:T(8,128)(2,1)S(1)}, bf16[256,4096]{1,0:T(8,128)(2,1)S(1)}) custom-call(bf16[256,4096]{1,0:T(8,128)(2,1)} %tok.5, bf16[4096,2048]{1,0:T(8,128)(2,1)} %weight.4), custom_call_target="tpu_custom_call" | custom-call | flops 2147483648 | bytes 10485760 | tf_op jit(solution)/shard_map/z_other/pallas_call | solution.py:456
  34.1 1.5 %collective-permute-start.7 = (bf16[512,256]{1,0:T(8,128)(2,1)S(1)}, bf16[512,256]{1,0:T(8,128)(2,1)S(1)}, u32[]{:S(2)}, u32[]{:S(2)}) collective-permute-start(bf16[512,256]{1,0:T(8,128)(2,1)S(1)} %get-tuple-element.65), channel_id=1, source_target_pairs={{0,4},{4,0},{1,5},{5,1},{2,6},{6,2},{3,7},{7,3},{8,12},{12,8},{9,1... | collective-permute-start | bytes 786440 | tf_op jit(solution)/shard_map/ppermute | solution.py:474
  35.7 1.7 %collective-permute-start.9 = (bf16[288,256]{1,0:T(8,128)(2,1)S(1)}, bf16[288,256]{1,0:T(8,128)(2,1)S(1)}, u32[]{:S(2)}, u32[]{:S(2)}) collective-permute-start(bf16[288,256]{1,0:T(8,128)(2,1)S(1)} %combine.3), channel_id=1, source_target_pairs={{0,16},{8,24},{16,0},{24,8},{1,17},{9,25},{17,1},{25,9},{2,18},{10... | collective-permute-start | bytes 442376 | tf_op jit(solution)/shard_map/ppermute | solution.py:474
  37.5 1.4 %collective-permute-start.6 = (bf16[288,256]{1,0:T(8,128)(2,1)S(1)}, bf16[288,256]{1,0:T(8,128)(2,1)S(1)}, u32[]{:S(2)}, u32[]{:S(2)}) collective-permute-start(bf16[288,256]{1,0:T(8,128)(2,1)S(1)} %combine.2), channel_id=1, source_target_pairs={{0,16},{8,24},{16,0},{24,8},{1,17},{9,25},{17,1},{25,9},{2,18},{10... | collective-permute-start | bytes 442376 | tf_op jit(solution)/shard_map/ppermute | solution.py:474
  38.9 7.1 %middle.1 = (f32[256,512]{1,0:T(8,128)S(1)}, f32[256,512]{1,0:T(8,128)S(1)}, bf16[1024,256]{1,0:T(8,128)(2,1)S(1)}, bf16[1024,4096]{1,0:T(8,128)(2,1)S(1)}) custom-call(bf16[256,4096]{1,0:T(8,128)(2,1)S(1)} %get-tuple-element.42.tok, bf16[4096,2048]{1,0:T(8,128)(2,1)} %weight.4, bf16[2048,4096]{1,0:T(8,128)(2,1)} %weight.5, ...), custom_call_target="tpu_custom_call" | custom-call | flops 2415919104 | bytes 16777216 | tf_op jit(solution)/shard_map/middle/pallas_call | solution.py:456
  45.9 3.1 %collective-permute-done.6.refs_2_ = bf16[288,256]{1,0:T(8,128)(2,1)S(1)} collective-permute-done((bf16[288,256]{1,0:T(8,128)(2,1)S(1)}, bf16[288,256]{1,0:T(8,128)(2,1)S(1)}, u32[]{:S(2)}, u32[]{:S(2)}) %collective-permute-start.6) | collective-permute-done | bytes 147488 | tf_op jit(solution)/shard_map/ppermute | solution.py:474
  49.9 1.3 %collective-permute-start.10 = (bf16[512,256]{1,0:T(8,128)(2,1)S(1)}, bf16[512,256]{1,0:T(8,128)(2,1)S(1)}, u32[]{:S(2)}, u32[]{:S(2)}) collective-permute-start(bf16[512,256]{1,0:T(8,128)(2,1)S(1)} %gate.2.refs_0_), channel_id=1, source_target_pairs={{0,4},{4,0},{1,5},{5,1},{2,6},{6,2},{3,7},{7,3},{8,12},{12,8},{9,1... | collective-permute-start | bytes 786440 | tf_op jit(solution)/shard_map/ppermute | solution.py:474
  52.0 0.9 %collective-permute-start.11 = (bf16[256,256]{1,0:T(8,128)(2,1)S(1)}, bf16[256,256]{1,0:T(8,128)(2,1)S(1)}, u32[]{:S(2)}, u32[]{:S(2)}) collective-permute-start(bf16[256,256]{1,0:T(8,128)(2,1)S(1)} %get-tuple-element.67.refs_1_), channel_id=1, source_target_pairs={{0,4},{4,0},{1,5},{5,1},{2,6},{6,2},{3,7},{7,3},{8,12},{12,8},{9,1... | collective-permute-start | bytes 393224 | tf_op jit(solution)/shard_map/ppermute | solution.py:474
  52.9 1.2 %collective-permute-start.12 = (bf16[256,256]{1,0:T(8,128)(2,1)S(1)}, bf16[256,256]{1,0:T(8,128)(2,1)S(1)}, u32[]{:S(2)}, u32[]{:S(2)}) collective-permute-start(bf16[256,256]{1,0:T(8,128)(2,1)S(1)} %get-tuple-element.68.refs_2_), channel_id=1, source_target_pairs={{0,4},{4,0},{1,5},{5,1},{2,6},{6,2},{3,7},{7,3},{8,12},{12,8},{9,1... | collective-permute-start | bytes 393224 | tf_op jit(solution)/shard_map/ppermute | solution.py:474
  54.1 5.6 %out_own.1 = (f32[256,4096]{1,0:T(8,128)S(1)}, bf16[1024,4096]{1,0:T(8,128)(2,1)S(1)}) custom-call(bf16[2048,4096]{1,0:T(8,128)(2,1)} %weight.5, bf16[1024,4096]{1,0:T(8,128)(2,1)S(1)} %get-tuple-element.59.w_own, bf16[512,256]{1,0:T(8,128)(2,1)S(1)} %gate.2.refs_0_, bf16[256,256]{1,0:T(8,128)(2,1)S(1)} %get-tuple-element.67.refs_1_, ...), custom_call_target="tpu_custom_call" | custom-call | flops 2147483648 | bytes 8388608 | tf_op jit(solution)/shard_map/out_own/pallas_call | solution.py:456
  64.9 1.7 %collective-permute-start.15 = (bf16[128,1024]{1,0:T(8,128)(2,1)S(1)}, bf16[128,1024]{1,0:T(8,128)(2,1)S(1)}, u32[]{:S(2)}, u32[]{:S(2)}) collective-permute-start(bf16[128,1024]{1,0:T(8,128)(2,1)S(1)} %add_convert_fusion.2), channel_id=1, source_target_pairs={{0,2},{1,3},{2,0},{3,1},{4,6},{5,7},{6,4},{7,5},{8,10},{9,11},{10,... | collective-permute-start | bytes 786440 | tf_op jit(solution)/shard_map/ppermute | solution.py:474
  67.2 7.0 %collective-permute-done.15 = bf16[128,1024]{1,0:T(8,128)(2,1)S(1)} collective-permute-done((bf16[128,1024]{1,0:T(8,128)(2,1)S(1)}, bf16[128,1024]{1,0:T(8,128)(2,1)S(1)}, u32[]{:S(2)}, u32[]{:S(2)}) %collective-permute-start.15) | collective-permute-done | bytes 262176 | tf_op jit(solution)/shard_map/ppermute | solution.py:474
  74.2 4.7 %collective-permute-done.17 = bf16[128,1024]{1,0:T(8,128)(2,1)S(1)} collective-permute-done((bf16[128,1024]{1,0:T(8,128)(2,1)S(1)}, bf16[128,1024]{1,0:T(8,128)(2,1)S(1)}, u32[]{:S(2)}, u32[]{:S(2)}) %collective-permute-start.17) | collective-permute-done | bytes 262176 | tf_op jit(solution)/shard_map/ppermute | solution.py:474
  78.9 1.1 %add_convert_fusion = bf16[256,1024]{1,0:T(8,128)(2,1)} fusion(bf16[256,1024]{1,0:T(8,128)(2,1)S(1)} %collective-permute-done.13, bf16[128,1024]{1,0:T(8,128)(2,1)S(1)} %get-tuple-element.72, bf16[128,1024]{1,0:T(8,128)(2,1)S(1)} %get-tuple-element.71, bf16[128,1024]{1,0:T(8,128)(2,1)S(1)} %collective-permute-done.17, ...), kind=kLoop, calls=%fused_computation | loop fusion | flops 3145728 | bytes 2097152 | tf_op jit(solution)/shard_map/convert_element_type | solution.py:683
  (47 shorter events, 9.6 us)
Async XLA Ops:
  5.0 18.8 %collective-permute-start = (bf16[800,256]{1,0:T(8,128)(2,1)}, bf16[800,256]{1,0:T(8,128)(2,1)S(1)}, u32[]{:S(2)}, u32[]{:S(2)}) collective-permute-start(bf16[800,256]{1,0:T(8,128)(2,1)} %get-tuple-element.43.refs_0_.refs_1_), channel_id=1, source_target_pairs={{0,4},{4,0},{1,5},{5,1},{2,6},{6,2},{3,7},{7,3},{8,12},{12,8},{9,1... | collective-permute-start | bytes 1228808 | tf_op jit(solution)/shard_map/ppermute | solution.py:474
  8.8 15.0 %copy-start = (bf16[800,256]{1,0:T(8,128)(2,1)S(1)}, bf16[800,256]{1,0:T(8,128)(2,1)}, u32[]{:S(2)}) copy-start(bf16[800,256]{1,0:T(8,128)(2,1)} %get-tuple-element.43.refs_0_.refs_1_) | copy-start | bytes 1228804
  8.8 15.0 %copy-start.1 = (f32[2048,4]{0,1:T(4,128)S(1)}, f32[2048,4]{0,1:T(4,128)}, u32[]{:S(2)}) copy-start(f32[2048,4]{0,1:T(4,128)} %param.20) | copy-start | bytes 98308
  8.8 15.0 %copy-start.4 = (f32[256,4]{0,1:T(4,128)S(1)}, f32[256,4]{0,1:T(4,128)}, u32[]{:S(2)}) copy-start(f32[256,4]{0,1:T(4,128)} %param.21) | copy-start | bytes 12292
  8.8 15.0 %copy-start.5 = (f32[32]{0:T(128)S(1)}, f32[32]{0:T(128)}, u32[]{:S(2)}) copy-start(f32[32]{0:T(128)} %param.17) | copy-start | bytes 388
  8.8 15.0 %copy-start.6 = (f32[32]{0:T(128)S(1)}, f32[32]{0:T(128)}, u32[]{:S(2)}) copy-start(f32[32]{0:T(128)} %param.18) | copy-start | bytes 388
  14.9 10.5 %collective-permute-start.3 = (bf16[512,256]{1,0:T(8,128)(2,1)S(1)}, bf16[512,256]{1,0:T(8,128)(2,1)S(1)}, u32[]{:S(2)}, u32[]{:S(2)}) collective-permute-start(bf16[512,256]{1,0:T(8,128)(2,1)S(1)} %get-tuple-element.54), channel_id=1, source_target_pairs={{0,4},{4,0},{1,5},{5,1},{2,6},{6,2},{3,7},{7,3},{8,12},{12,8},{9,1... | collective-permute-start | bytes 786440 | tf_op jit(solution)/shard_map/ppermute | solution.py:474
  15.0 7.4 %collective-permute-start.1 = (bf16[80,256]{1,0:T(8,128)(2,1)S(1)}, bf16[80,256]{1,0:T(8,128)(2,1)S(1)}, u32[]{:S(2)}, u32[]{:S(2)}) collective-permute-start(bf16[80,256]{1,0:T(8,128)(2,1)S(1)} %get-tuple-element.46), channel_id=1, source_target_pairs={{0,12},{4,8},{8,20},{12,16},{16,28},{20,24},{24,4},{28,0},{1,13},{... | collective-permute-start | bytes 122888 | tf_op jit(solution)/shard_map/ppermute | solution.py:540
  18.0 5.8 %collective-permute-start.2 = (bf16[80,256]{1,0:T(8,128)(2,1)S(1)}, bf16[80,256]{1,0:T(8,128)(2,1)S(1)}, u32[]{:S(2)}, u32[]{:S(2)}) collective-permute-start(bf16[80,256]{1,0:T(8,128)(2,1)S(1)} %get-tuple-element.47), channel_id=1, source_target_pairs={{0,8},{8,16},{16,24},{24,0},{1,9},{9,17},{17,25},{25,1},{2,10},{10... | collective-permute-start | bytes 122888 | tf_op jit(solution)/shard_map/ppermute | solution.py:543
  26.8 8.8 %collective-permute-start.8 = (bf16[288,256]{1,0:T(8,128)(2,1)S(1)}, bf16[288,256]{1,0:T(8,128)(2,1)S(1)}, u32[]{:S(2)}, u32[]{:S(2)}) collective-permute-start(bf16[288,256]{1,0:T(8,128)(2,1)S(1)} %get-tuple-element.66.refs_0_), channel_id=1, source_target_pairs={{0,8},{8,0},{16,24},{24,16},{1,9},{9,1},{17,25},{25,17},{2,10},{10... | collective-permute-start | bytes 442376 | tf_op jit(solution)/shard_map/ppermute | solution.py:474
  27.5 11.3 %copy-start.7 = (f32[32]{0:T(128)S(1)}, f32[32]{0:T(128)}, u32[]{:S(2)}) copy-start(f32[32]{0:T(128)} %param.19) | copy-start | bytes 388
  27.5 9.9 %collective-permute-start.5 = (bf16[288,256]{1,0:T(8,128)(2,1)S(1)}, bf16[288,256]{1,0:T(8,128)(2,1)S(1)}, u32[]{:S(2)}, u32[]{:S(2)}) collective-permute-start(bf16[288,256]{1,0:T(8,128)(2,1)S(1)} %get-tuple-element.63.refs_0_), channel_id=1, source_target_pairs={{0,8},{8,0},{16,24},{24,16},{1,9},{9,1},{17,25},{25,17},{2,10},{10... | collective-permute-start | bytes 442376 | tf_op jit(solution)/shard_map/ppermute | solution.py:474
  33.5 12.4 %collective-permute-start.4 = (bf16[512,256]{1,0:T(8,128)(2,1)S(1)}, bf16[512,256]{1,0:T(8,128)(2,1)S(1)}, u32[]{:S(2)}, u32[]{:S(2)}) collective-permute-start(bf16[512,256]{1,0:T(8,128)(2,1)S(1)} %get-tuple-element.62), channel_id=1, source_target_pairs={{0,4},{4,0},{1,5},{5,1},{2,6},{6,2},{3,7},{7,3},{8,12},{12,8},{9,1... | collective-permute-start | bytes 786440 | tf_op jit(solution)/shard_map/ppermute | solution.py:474
  34.1 17.1 %collective-permute-start.7 = (bf16[512,256]{1,0:T(8,128)(2,1)S(1)}, bf16[512,256]{1,0:T(8,128)(2,1)S(1)}, u32[]{:S(2)}, u32[]{:S(2)}) collective-permute-start(bf16[512,256]{1,0:T(8,128)(2,1)S(1)} %get-tuple-element.65), channel_id=1, source_target_pairs={{0,4},{4,0},{1,5},{5,1},{2,6},{6,2},{3,7},{7,3},{8,12},{12,8},{9,1... | collective-permute-start | bytes 786440 | tf_op jit(solution)/shard_map/ppermute | solution.py:474
  35.7 15.5 %collective-permute-start.9 = (bf16[288,256]{1,0:T(8,128)(2,1)S(1)}, bf16[288,256]{1,0:T(8,128)(2,1)S(1)}, u32[]{:S(2)}, u32[]{:S(2)}) collective-permute-start(bf16[288,256]{1,0:T(8,128)(2,1)S(1)} %combine.3), channel_id=1, source_target_pairs={{0,16},{8,24},{16,0},{24,8},{1,17},{9,25},{17,1},{25,9},{2,18},{10... | collective-permute-start | bytes 442376 | tf_op jit(solution)/shard_map/ppermute | solution.py:474
  37.5 11.6 %collective-permute-start.6 = (bf16[288,256]{1,0:T(8,128)(2,1)S(1)}, bf16[288,256]{1,0:T(8,128)(2,1)S(1)}, u32[]{:S(2)}, u32[]{:S(2)}) collective-permute-start(bf16[288,256]{1,0:T(8,128)(2,1)S(1)} %combine.2), channel_id=1, source_target_pairs={{0,16},{8,24},{16,0},{24,8},{1,17},{9,25},{17,1},{25,9},{2,18},{10... | collective-permute-start | bytes 442376 | tf_op jit(solution)/shard_map/ppermute | solution.py:474
  49.9 10.5 %collective-permute-start.10 = (bf16[512,256]{1,0:T(8,128)(2,1)S(1)}, bf16[512,256]{1,0:T(8,128)(2,1)S(1)}, u32[]{:S(2)}, u32[]{:S(2)}) collective-permute-start(bf16[512,256]{1,0:T(8,128)(2,1)S(1)} %gate.2.refs_0_), channel_id=1, source_target_pairs={{0,4},{4,0},{1,5},{5,1},{2,6},{6,2},{3,7},{7,3},{8,12},{12,8},{9,1... | collective-permute-start | bytes 786440 | tf_op jit(solution)/shard_map/ppermute | solution.py:474
  52.0 8.4 %collective-permute-start.11 = (bf16[256,256]{1,0:T(8,128)(2,1)S(1)}, bf16[256,256]{1,0:T(8,128)(2,1)S(1)}, u32[]{:S(2)}, u32[]{:S(2)}) collective-permute-start(bf16[256,256]{1,0:T(8,128)(2,1)S(1)} %get-tuple-element.67.refs_1_), channel_id=1, source_target_pairs={{0,4},{4,0},{1,5},{5,1},{2,6},{6,2},{3,7},{7,3},{8,12},{12,8},{9,1... | collective-permute-start | bytes 393224 | tf_op jit(solution)/shard_map/ppermute | solution.py:474
  52.9 8.9 %collective-permute-start.12 = (bf16[256,256]{1,0:T(8,128)(2,1)S(1)}, bf16[256,256]{1,0:T(8,128)(2,1)S(1)}, u32[]{:S(2)}, u32[]{:S(2)}) collective-permute-start(bf16[256,256]{1,0:T(8,128)(2,1)S(1)} %get-tuple-element.68.refs_2_), channel_id=1, source_target_pairs={{0,4},{4,0},{1,5},{5,1},{2,6},{6,2},{3,7},{7,3},{8,12},{12,8},{9,1... | collective-permute-start | bytes 393224 | tf_op jit(solution)/shard_map/ppermute | solution.py:474
  61.2 3.6 %collective-permute-start.14 = (bf16[128,1024]{1,0:T(8,128)(2,1)S(1)}, bf16[128,1024]{1,0:T(8,128)(2,1)S(1)}, u32[]{:S(2)}, u32[]{:S(2)}) collective-permute-start(bf16[128,1024]{1,0:T(8,128)(2,1)S(1)} %get-tuple-element.76), channel_id=1, source_target_pairs={{0,1},{1,0},{2,3},{3,2},{4,5},{5,4},{6,7},{7,6},{8,9},{9,8},{10,11... | collective-permute-start | bytes 786440 | tf_op jit(solution)/shard_map/ppermute | solution.py:474
  62.6 4.0 %collective-permute-start.16 = (bf16[128,1024]{1,0:T(8,128)(2,1)S(1)}, bf16[128,1024]{1,0:T(8,128)(2,1)S(1)}, u32[]{:S(2)}, u32[]{:S(2)}) collective-permute-start(bf16[128,1024]{1,0:T(8,128)(2,1)S(1)} %get-tuple-element.78), channel_id=1, source_target_pairs={{0,1},{1,0},{2,3},{3,2},{4,5},{5,4},{6,7},{7,6},{8,9},{9,8},{10,11... | collective-permute-start | bytes 786440 | tf_op jit(solution)/shard_map/ppermute | solution.py:474
  64.3 14.5 %collective-permute-start.13 = (bf16[256,1024]{1,0:T(8,128)(2,1)S(1)}, bf16[256,1024]{1,0:T(8,128)(2,1)S(1)}, u32[]{:S(2)}, u32[]{:S(2)}) collective-permute-start(bf16[256,1024]{1,0:T(8,128)(2,1)S(1)} %pad_maximum_fusion), channel_id=1, source_target_pairs={{0,1},{1,0},{2,3},{3,2},{4,5},{5,4},{6,7},{7,6},{8,9},{9,8},{10,11... | collective-permute-start | bytes 1572872 | tf_op jit(solution)/shard_map/ppermute | solution.py:474
  64.9 9.2 %collective-permute-start.15 = (bf16[128,1024]{1,0:T(8,128)(2,1)S(1)}, bf16[128,1024]{1,0:T(8,128)(2,1)S(1)}, u32[]{:S(2)}, u32[]{:S(2)}) collective-permute-start(bf16[128,1024]{1,0:T(8,128)(2,1)S(1)} %add_convert_fusion.2), channel_id=1, source_target_pairs={{0,2},{1,3},{2,0},{3,1},{4,6},{5,7},{6,4},{7,5},{8,10},{9,11},{10,... | collective-permute-start | bytes 786440 | tf_op jit(solution)/shard_map/ppermute | solution.py:474
  66.7 12.2 %collective-permute-start.17 = (bf16[128,1024]{1,0:T(8,128)(2,1)S(1)}, bf16[128,1024]{1,0:T(8,128)(2,1)S(1)}, u32[]{:S(2)}, u32[]{:S(2)}) collective-permute-start(bf16[128,1024]{1,0:T(8,128)(2,1)S(1)} %add_convert_fusion.1), channel_id=1, source_target_pairs={{0,2},{1,3},{2,0},{3,1},{4,6},{5,7},{6,4},{7,5},{8,10},{9,11},{10,... | collective-permute-start | bytes 786440 | tf_op jit(solution)/shard_map/ppermute | solution.py:474
  (2 other events, 11.0 us)

commit v3 on v2

--- a/solution.py
+++ b/solution.py
@@ -151,7 +151,7 @@
         edge[(1 + j) * HALO : (2 + j) * HALO, :] = acc_x[toks - HALO :, cols].astype(bf16)
 
 
-def second_kernel(tok, w_x, edge_in, msg, mine, edge_other, edge_own, held_tok, held, acc, sems, *, chunks, kb):
+def second_kernel(tok, w_x, edge_first, msg, mine, edge_other, edge_own, edge_in, held_tok, held, acc, sems, *, chunks, kb):
     toks, width = acc.shape
     lanes = msg.shape[1]
     row = place()[0]
@@ -168,8 +168,9 @@
             (w_x.at[deep, pl.ds(low_other, first)], held.at[deep, pl.ds(0, first)]),
             (w_x.at[deep, pl.ds(low_own, half)], held.at[deep, pl.ds(first, half)]),
         ]
-    started = copies(pairs, sems)
+    started = copies([*pairs, (edge_first, edge_in)], sems)
     product(held_tok, held, [started[3 * i : 3 * i + 3] for i in range(parts)], acc, kb)
+    started[-1].wait()
     per = msg.shape[0] // toks
     base = edge_in.shape[0]
     edge_other[:base, :] = edge_in[...]
@@ -206,30 +207,52 @@
         outs[j // per][at_row : at_row + toks, :] = acc[:, j * lanes : (j + 1) * lanes].astype(bf16)
 
 
-def middle_kernel(tok, weight, w_out, scores, skip, *refs, chunks, kb, head_dim):
+def rows_of(weight, target, low, lanes):
+    return [
+        (weight.at[pl.ds(low + i * lanes, lanes), :], target.at[pl.ds(i * lanes, lanes), :])
+        for i in range(target.shape[0] // lanes)
+    ]
+
+
+def rows_of(weight, target, low, lanes):
+    return [
+        (weight.at[pl.ds(low + i * lanes, lanes), :], target.at[pl.ds(i * lanes, lanes), :])
+        for i in range(target.shape[0] // lanes)
+    ]
+
+
+def inner_kernel(scores, skip, w_out, *refs, chunks, head_dim, lanes):
     scans, refs = [refs[4 * c : 4 * c + 4] for c in range(chunks)], refs[4 * chunks :]
-    inners, refs = refs[:chunks], refs[chunks:]
-    mine, w_own, held, acc, sems = refs
+    *outs, w_own, sems = refs
+    where = place()
+    half = w_own.shape[0]
+    started = copies(rows_of(w_out, w_own, pl.multiple_of(where[0] * half, half), lanes), sems)
+
+    @pl.when(where[0] >= 0)
+    def _():
+        heads = half // head_dim
+        for c in range(chunks):
+            within(
+                where, scores, *scans[c], skip, outs[c], head_dim=head_dim,
+                first_of=c * heads // chunks, local_heads=heads,
+            )
+
+    for now in started:
+        now.wait()
+
+
+def own_gate_kernel(tok, weight, w_out, mine, w_early, held, acc, sems, *, kb):
     toks, width = acc.shape
     lanes = mine.shape[1]
-    where = place()
-    low = pl.multiple_of(where[0] * width, width)
+    row = place()[0]
+    low = pl.multiple_of(row * width, width)
     parts = tok.shape[1] // kb
     pairs = [
         (weight.at[pl.ds(i * kb, kb), pl.ds(low, width)], held.at[pl.ds(i * kb, kb), :])
         for i in range(parts)
     ]
-    pairs += [
-        (w_out.at[pl.ds(low + i * lanes, lanes), :], w_own.at[pl.ds(i * lanes, lanes), :])
-        for i in range(width // lanes)
-    ]
+    pairs += rows_of(w_out, w_early, pl.multiple_of((1 - row) * width, width), lanes)
     started = copies(pairs, sems)
-    heads = width // head_dim
-    for c in range(chunks):
-        within(
-            where, scores, *scans[c], skip, inners[c], head_dim=head_dim,
-            first_of=c * heads // chunks, local_heads=heads,
-        )
     product(tok, held, [[now] for now in started[:parts]], acc, kb)
     for j in range(width // lanes):
         mine[j * toks : (j + 1) * toks, :] = acc[:, j * lanes : (j + 1) * lanes].astype(bf16)
@@ -349,10 +372,9 @@
         out[half:, cols] = low + skips * conv_out[half:, cols].astype(f32)
 
 
-def gate_kernel(inner, bc, cum, z_mine, z_theirs, gain, *refs, messages, chunk, chunks, head_dim, state_dim, lanes):
+def gate_kernel(inner, bc, cum, z_mine, z_theirs, gain, *refs, messages, bounds, chunk, chunks, head_dim, state_dim, lanes):
     messages, outs = refs[:messages], refs[messages:]
     toks = inner.shape[0]
-    part_toks = toks // len(outs)
     row, _, here = place()
     gain_low = (row * chunks + chunk) * inner.shape[1]
     rows = state_dim + HALO
@@ -370,7 +392,7 @@
         cols = slice(j * lanes, (j + 1) * lanes)
         scanned = inner[:, cols] + grown[:, cols] * mm(c_now, enter.astype(bf16))
         z_low = (chunk * inner.shape[1] // lanes + j) * toks
-        z_now = total(z_mine[z_low : z_low + toks, :], z_theirs[j * toks : (j + 1) * toks, :])
+        z_now = total(z_mine[z_low : z_low + toks, :], z_theirs[z_low : z_low + toks, :])
         gated = scanned * silu(z_now)
         square = gated * gated
         for i in range(lanes // wide):
@@ -384,64 +406,70 @@
                 * lax.rsqrt(mean + EPS)
                 * gain[:, pl.ds(pl.multiple_of(gain_low + low, wide), wide)]
             ).astype(bf16)
-            for t, out in enumerate(outs):
-                out[j * part_toks : (j + 1) * part_toks, i * wide : (i + 1) * wide] = done[
-                    t * part_toks : (t + 1) * part_toks
-                ]
-
-
-def own_kernel(weight, w_own, *refs, groups):
-    *normed, partial, rest, whole, sems = refs
-    toks, width = partial.shape
+            for (start, end), out in zip(bounds, outs):
+                size = end - start
+                out[j * size : (j + 1) * size, i * wide : (i + 1) * wide] = done[start:end]
+
+
+def own_kernel(weight, w_own, *refs, bounds):
+    *normed, partial, w_late, whole, sems = refs
     lanes = normed[0].shape[1]
-    half = rest.shape[0]
-    other = pl.multiple_of((1 - place()[0]) * half, half)
-    started = copies(
-        [
-            (weight.at[pl.ds(other + i * lanes, lanes), :], rest.at[pl.ds(i * lanes, lanes), :])
-            for i in range(half // lanes)
-        ],
-        sems,
-    )
+    row = place()[0]
+    late = pl.multiple_of((2 - row) * w_own.shape[0] - w_late.shape[0], lanes)
+    started = copies(rows_of(weight, w_late, late, lanes), sems)
+
+    @pl.when(row >= 0)
+    def _():
+        own_product(w_own, normed, partial, whole, bounds)
+
+    for now in started:
+        now.wait()
+
+
+def own_product(weight, normed, partial, whole, bounds):
+    width = partial.shape[1]
+    lanes = normed[0].shape[1]
     low = 0
-    for parts in groups:
-        chunk = [normed.pop(0) for _ in range(parts)]
-        part_toks = toks // parts
-        for j in range(chunk[0].shape[0] // part_toks):
-            for t, part in enumerate(chunk):
-                whole[t * part_toks : (t + 1) * part_toks, low : low + lanes] = part[
-                    j * part_toks : (j + 1) * part_toks, :
-                ]
+    for chunk in zip(*[iter(normed)] * len(bounds)):
+        blocks = chunk[0].shape[0] // (bounds[0][1] - bounds[0][0])
+        for j in range(blocks):
+            for (start, end), part in zip(bounds, chunk):
+                size = end - start
+                whole[start:end, low : low + lanes] = part[j * size : (j + 1) * size, :]
             low += lanes
     for low in range(0, width, 512):
         cols = slice(low, min(low + 512, width))
-        partial[:, cols] = mm(whole[...], w_own[:, cols])
-    for now in started:
-        now.wait()
-
-
-def rest_kernel(partial, rest, *refs, part, parts, pair_of, groups):
+        partial[:, cols] = mm(whole[...], weight[:, cols])
+
+
+def rest_kernel(partial, w_early, w_late, *refs, jobs):
     *normed, send, keep = refs
-    part_toks, piece = send.shape
     lanes = normed[0].shape[1]
-    toks = partial.shape[0]
-    rows = slice(part * part_toks, (part + 1) * part_toks)
+    piece = send.shape[1]
     step = min(512, piece)
-    where = place()
-    for target, core in ((send, 1 - where[1] % 2), (keep, where[1] % 2)):
-        base = (pair_of(where) * 2 + core) * piece
-        for low in range(0, piece, step):
-            cols = pl.ds(pl.multiple_of(base + low, step), step)
-            acc = partial[rows, cols]
-            block = 0
-            for chunk, pieces in zip(normed, groups):
-                held_toks = toks // pieces
-                first = part * part_toks if pieces == 1 else 0
-                for j in range(chunk.shape[0] // held_toks):
-                    now = chunk[j * held_toks + first : j * held_toks + first + part_toks, :]
-                    acc = acc + mm(now, rest[block * lanes : (block + 1) * lanes, cols])
-                    block += 1
-            target[:, low : low + step] = acc.astype(bf16)
+    _, col, _ = place()
+    at_row = 0
+    for i, (start, end, far, crossed) in enumerate(jobs):
+        size = end - start
+        pair = 1 - col // 2 if far else col // 2
+        kept = (col + crossed) % 2
+        for target, core in ((send, 1 - kept), (keep, kept)):
+            base = (pair * 2 + core) * piece
+            for low in range(0, piece, step):
+                cols = pl.ds(pl.multiple_of(base + low, step), step)
+                acc = partial[start:end, cols]
+                row = 0
+                for chunk in normed[i :: len(jobs)]:
+                    for j in range(chunk.shape[0] // size):
+                        first = row < w_early.shape[0]
+                        held = w_early if first else w_late
+                        held_row = row - (0 if first else w_early.shape[0])
+                        acc = acc + mm(
+                            chunk[j * size : (j + 1) * size, :], held[held_row : held_row + lanes, cols]
+                        )
+                        row += lanes
+                target[at_row : at_row + size, low : low + step] = acc.astype(bf16)
+        at_row += size
 
 
 def sds(*shape, dtype=bf16):
@@ -452,17 +480,22 @@
     return pl.CostEstimate(flops=int(flops), bytes_accessed=int(size), transcendentals=0)
 
 
-def call(kernel, args, specs, outs, scratch=(), flops=0, size=0, name=None, mib=16):
+def call(kernel, args, specs, outs, scratch=(), flops=0, size=0, name=None, mib=16, after=()):
+    used = len(args)
+
+    def body(*refs):
+        kernel(*refs[:used], *refs[used + len(after) :])
+
     return pl.pallas_call(
-        kernel,
-        in_specs=specs or [IN_VMEM] * len(args),
+        body,
+        in_specs=[*(specs or [IN_VMEM] * used), *[pl.BlockSpec(memory_space=pl.ANY)] * len(after)],
         out_specs=[IN_VMEM] * len(outs),
         scratch_shapes=list(scratch),
         out_shape=outs,
         compiler_params=pltpu.CompilerParams(vmem_limit_bytes=mib * MIB),
         cost_estimate=cost(flops, size),
         name=name,
-    )(*args)
+    )(*args, *after)
 
 
 IN_VMEM = pl.BlockSpec(memory_space=pltpu.VMEM)
@@ -516,19 +549,20 @@
         flops=2 * toks * depth * (width + lanes + heads),
         size=2 * depth * (toks + width + lanes + heads),
         name="first",
-        mib=60,
+        mib=53,
     )
     first_got = swapped(msg_first, "row", 1)
     msg_second, x_mine, edge_other, edge_own = call(
         functools.partial(second_kernel, chunks=chunks, kb=kb),
         (tokens, proj_x, edge_first),
-        [IN_HBM, IN_HBM, IN_VMEM],
+        [IN_HBM] * 3,
         [sds(blocks * toks, lanes), sds(chunks * blocks * toks, lanes), *[sds(edge_rows, lanes)] * 2],
         [
+            pltpu.VMEM(edge_first.shape, bf16),
             pltpu.VMEM((toks, depth), bf16),
             pltpu.VMEM((depth, width + half), bf16),
             pltpu.VMEM((toks, width + half), f32),
-            pltpu.SemaphoreType.DMA((3 * parts,)),
+            pltpu.SemaphoreType.DMA((3 * parts + 1,)),
         ],
         flops=2 * toks * depth * (width + half),
         size=2 * depth * (toks + width + half),
@@ -541,11 +575,11 @@
         edge_other, ("ctx", "row"), [(2 * i + s, 2 * j + 1 - s) for i, j in down for s in range(2)]
     )
     edge_b = lax.ppermute(edge_own, "ctx", down)
-    *z_send, tok_held = call(
+    z_send, tok_held = call(
         functools.partial(gate_product_kernel, kb=kb),
         (tokens, proj_z),
         [IN_HBM] * 2,
-        [*[sds(blocks * toks, lanes)] * chunks, sds(toks, depth)],
+        [sds(chunks * blocks * toks, lanes), sds(toks, depth)],
         [
             pltpu.VMEM((depth, half), bf16),
             pltpu.VMEM((toks, half), f32),
@@ -555,8 +589,8 @@
         size=2 * depth * (toks + half),
         name="z_other",
         mib=50,
-    )
-    z_got = [swapped(z, "row", 1) for z in z_send]
+        after=(edge_own,),
+    )
 
     rows = state_dim + HALO
     sizes = dict(head_dim=head_dim, state_dim=state_dim, lanes=lanes)
@@ -587,13 +621,16 @@
             flops=2 * toks * width * (state_dim + 64),
             size=2 * toks * width * 6,
             name="state",
+            after=(z_send,),
         )
         if c == 0:
             bc_now, scores, *got = got
         states.append(got[0])
         scans.append(got[1:])
 
-    messages = []
+    z_send, _ = lax.optimization_barrier((z_send, states))
+    z_got = swapped(z_send, "row", 1)
+    messages, sent = [], []
     for c in range(chunks):
         heard = [states[c]]
         send = states[c]
@@ -608,32 +645,49 @@
             heard.append(swapped(send, "ctx", by))
             by *= 2
         messages.append(heard)
-
-    args = (tok_held, proj_z, proj_out, scores, skip, *[a for scan in scans for a in scan])
-    *inners, z_mine, w_own = call(
-        functools.partial(middle_kernel, chunks=chunks, kb=kb, head_dim=head_dim),
+        sent.append(send)
+
+    args = (scores, skip, proj_out, *[a for scan in scans for a in scan])
+    *inners, w_own = call(
+        functools.partial(inner_kernel, chunks=chunks, head_dim=head_dim, lanes=lanes),
         args,
-        [IN_VMEM, IN_HBM, IN_HBM, *[IN_VMEM] * (len(args) - 3)],
-        [*[sds(toks, width, dtype=f32)] * chunks, sds(chunks * blocks * toks, lanes), sds(half, out_cols)],
+        [IN_VMEM, IN_VMEM, IN_HBM, *[IN_VMEM] * (len(args) - 3)],
+        [*[sds(toks, width, dtype=f32)] * chunks, sds(half, out_cols)],
+        [pltpu.SemaphoreType.DMA((half // lanes,))],
+        flops=4 * toks * toks * half,
+        size=4 * toks * half * 3 + 2 * half * out_cols,
+        name="inner",
+        mib=42,
+    )
+    early = half // 2
+    z_mine, w_early = call(
+        functools.partial(own_gate_kernel, kb=kb),
+        (tok_held, proj_z, proj_out),
+        [IN_VMEM, IN_HBM, IN_HBM],
+        [sds(chunks * blocks * toks, lanes), sds(early, out_cols)],
         [
             pltpu.VMEM((depth, half), bf16),
             pltpu.VMEM((toks, half), f32),
-            pltpu.SemaphoreType.DMA((parts + half // lanes,)),
+            pltpu.SemaphoreType.DMA((parts + early // lanes,)),
         ],
-        flops=2 * toks * half * (depth + 2 * toks),
-        size=2 * depth * half + 2 * half * out_cols,
-        name="middle",
-        mib=38,
+        flops=2 * toks * half * depth,
+        size=2 * depth * half + 2 * early * out_cols,
+        name="z_own",
+        mib=34,
+        after=(sent[-1], inners[-1]),
     )
 
     normed, normed_got = [], []
-    groups = [1] * (chunks - 1) + [2]
+    cut = toks * 8 // 16
+    bounds = ((0, cut), (cut, toks))
     for c in range(chunks):
         now = call(
-            functools.partial(gate_kernel, messages=len(messages[c]), chunk=c, chunks=chunks, **sizes),
-            (inners[c], bc_now, scans[c][2], z_mine, z_got[c], gain, *messages[c]),
+            functools.partial(
+                gate_kernel, messages=len(messages[c]), bounds=bounds, chunk=c, chunks=chunks, **sizes
+            ),
+            (inners[c], bc_now, scans[c][2], z_mine, z_got, gain, *messages[c]),
             None,
-            [sds(blocks * toks // groups[c], lanes)] * groups[c],
+            [sds(blocks * (end - start), lanes) for start, end in bounds],
             flops=2 * toks * width * (state_dim + 4 * head_dim),
             size=2 * toks * width * 6,
             name="gate",
@@ -642,45 +696,43 @@
         normed_got.append([swapped(part, "row", 1) for part in now])
 
     piece = out_cols // lax.axis_size("col")
-    args = (proj_out, w_own, *[part for now in normed for part in now])
-    partial, rest = call(
-        functools.partial(own_kernel, groups=groups),
-        args,
-        [IN_HBM, *[IN_VMEM] * (len(args) - 1)],
-        [sds(toks, out_cols, dtype=f32), sds(half, out_cols)],
-        [pltpu.VMEM((toks, half), bf16), pltpu.SemaphoreType.DMA((half // lanes,))],
+    partial, w_late = call(
+        functools.partial(own_kernel, bounds=bounds),
+        (proj_out, w_own, *[part for now in normed for part in now]),
+        [IN_HBM, *[IN_VMEM] * (1 + len(bounds) * chunks)],
+        [sds(toks, out_cols, dtype=f32), sds(half - early, out_cols)],
+        [pltpu.VMEM((toks, half), bf16), pltpu.SemaphoreType.DMA(((half - early) // lanes,))],
         flops=2 * toks * half * out_cols,
-        size=2 * half * out_cols,
+        size=2 * (2 * half - early) * out_cols,
         name="out_own",
         mib=26,
     )
 
-    def out_rest(part, parts, pair_of, name):
-        args = (partial, rest, *[now[part] if len(now) > 1 else now[0] for now in normed_got])
+    def out_rest(jobs, name, after=()):
+        args = (partial, w_early, w_late, *[now[part] for now in normed_got for part, *_ in jobs])
+        jobs = tuple((*bounds[part], far, crossed) for part, far, crossed in jobs)
         return call(
-            functools.partial(
-                rest_kernel, part=part, parts=parts, pair_of=pair_of,
-                groups=[len(now) if parts > 1 else 1 for now in normed_got],
-            ),
+            functools.partial(rest_kernel, jobs=jobs),
             args,
             None,
-            [sds(toks // parts, piece)] * 2,
-            flops=2 * toks // parts * half * 2 * piece,
-            size=half * 2 * piece,
+            [sds(sum(end - start for start, end, *_ in jobs), piece)] * 2,
             name=name,
+            after=after,
         )
 
     def added(a, b):
         return (a.astype(f32) + b.astype(f32)).astype(bf16)
 
-    parts = groups[-1]
-    far = [out_rest(part, parts, lambda w: 1 - w[1] // 2, "out_far") for part in range(parts)]
-    far = [added(keep, swapped(send, "col", 1)) for send, keep in far]
-    far_got = [swapped(now, "col", 2) for now in far]
-    near = [out_rest(part, parts, lambda w: w[1] // 2, "out_near") for part in range(parts)]
-    near_keep, near_send = (jnp.concatenate([now[i] for now in near]) for i in (1, 0))
-    total_near = near_keep.astype(f32) + swapped(near_send, "col", 1).astype(f32)
-    return (total_near + jnp.concatenate(far_got).astype(f32)).astype(bf16)
+    got_far, near, order = [], [], ()
+    for part in range(len(bounds)):
+        send, keep = out_rest(((part, True, 0),), "out_far", order)
+        far = added(keep, swapped(send, "col", 1))
+        got_far.append(swapped(far, "col", 2))
+        order = (keep,) if part == 0 else (far,)
+        send, keep = out_rest(((part, False, 0),), "out_near", order)
+        near.append(keep.astype(f32) + swapped(send, "col", 1).astype(f32))
+        order = (keep,)
+    return (jnp.concatenate(near) + jnp.concatenate(got_far).astype(f32)).astype(bf16)
 
 
 def shifted(shard, axis, by):

time: 80.6 us -> 75.3 us (0.934)
  waiting for transfers between devices: 20.3 us -> 16.6 us
  Pallas kernels: 36.3 us -> 33.5 us
  starting transfers between devices: 21.1 us -> 22.6 us
    pallas_call x15 -> x16, Pallas kernels: 36.3 us -> 33.5 us  [call(): pl.pallas_call(body, in_specs=[*(specs or [IN_VMEM] * used), *[pl.BlockSp...]
    ppermute x1, waiting for transfers between devices: 2.76 us -> 0.01 us  [fast(): lax.ppermute(edge_other, ('ctx', 'row'), [(2 * i + s, 2 * j + 1 - s) for...]
    ppermute x16 -> x17, starting transfers between devices: 16.5 us -> 18 us  [swapped(): return lax.ppermute(shard, axis, [(i, i ^ by) for i in range(devices)])]
    ppermute x1, waiting for transfers between devices: 1.46 us -> 0.01 us  [fast(): edge_b = lax.ppermute(edge_own, 'ctx', down)]
    ppermute x16 -> x17, waiting for transfers between devices: 16.1 us -> 16.6 us  [swapped(): return lax.ppermute(shard, axis, [(i, i ^ by) for i in range(devices)])]
  transfers between devices with their start and end apart: 18 -> 19, of which waited for: 7 -> 8; matrix products, arithmetic and copies ran while one was open for 0% -> 0% of each run, Pallas kernels for 37% -> 36%
where the time goes in v3:
time: 75.3 us; the launch traced here: 75.2 us
  Pallas kernels  33.5 us (44%)
  starting transfers between devices  22.6 us (30%)
  waiting for transfers between devices  16.6 us (22%)
  other arithmetic  1.21 us (2%)
  local copies, waits for them, and re-layouts  0.97 us (1%)
    pallas_call x16, Pallas kernels, call(): pl.pallas_call(body, in_specs=[*(specs or [IN_VMEM] * used), *[pl.BlockSp...  33.5 us
    ppermute x17, starting transfers between devices, swapped(): return lax.ppermute(shard, axis, [(i, i ^ by) for i in range(devices)])  18 us
    ppermute x17, waiting for transfers between devices, swapped(): return lax.ppermute(shard, axis, [(i, i ^ by) for i in range(devices)])  16.6 us
    ppermute x1, starting transfers between devices, fast(): lax.ppermute(edge_other, ('ctx', 'row'), [(2 * i + s, 2 * j + 1 - s) for...  3.02 us
    ppermute x1, starting transfers between devices, fast(): edge_b = lax.ppermute(edge_own, 'ctx', down)  1.63 us
  transfers between devices with their start and end apart: 19, of which 8 were waited for; matrix products, arithmetic and copies ran while one was open for 0% of the time, Pallas kernels for 36%

profile of v3, /device:TPU:0, one launch (start us, length us, event | category | flops | bytes accessed | tf_op | source)
XLA Modules:
  0.0 75.2 jit_solution(5865934451011236153)
XLA Ops:
  0.0 0.9 %copy-done = bf16[4096,32]{0,1:T(8,128)(2,1)S(1)} copy-done((bf16[4096,32]{0,1:T(8,128)(2,1)S(1)}, bf16[4096,32]{0,1:T(8,128)(2,1)}, u32[]{:S(2)}) %copy-start) | copy-done | bytes 262168
  1.0 4.3 %first.1 = (bf16[800,256]{1,0:T(8,128)(2,1)S(1)}, bf16[48,256]{1,0:T(8,128)(2,1)S(1)}) custom-call(bf16[256,4096]{1,0:T(8,128)(2,1)} %refs_0_.6, bf16[4096,2048]{1,0:T(8,128)(2,1)} %refs_1_.5, bf16[4096,256]{1,0:T(8,128)(2,1)} %refs_2_.3, bf16[32,4096]{1,0:T(8,128)(2,1)S(1)} %bitcast.7), custom_call_target="tpu_custom_call" | custom-call | flops 1677721600 | bytes 8650752 | tf_op jit(solution)/shard_map/first/pallas_call | solution.py:489
  5.2 3.0 %collective-permute-start = (bf16[800,256]{1,0:T(8,128)(2,1)S(1)}, bf16[800,256]{1,0:T(8,128)(2,1)S(1)}, u32[]{:S(2)}, u32[]{:S(2)}) collective-permute-start(bf16[800,256]{1,0:T(8,128)(2,1)S(1)} %get-tuple-element.45.refs_0_.refs_1_), channel_id=1, source_target_pairs={{0,4},{4,0},{1,5},{5,1},{2,6},{6,2},{3,7},{7,3},{8,12},{12,8},{9,1... | collective-permute-start | bytes 1228808 | tf_op jit(solution)/shard_map/ppermute | solution.py:507
  8.2 6.1 %second.1 = (bf16[512,256]{1,0:T(8,128)(2,1)S(1)}, bf16[1024,256]{1,0:T(8,128)(2,1)S(1)}, bf16[80,256]{1,0:T(8,128)(2,1)S(1)}, bf16[80,256]{1,0:T(8,128)(2,1)S(1)}) custom-call(bf16[256,4096]{1,0:T(8,128)(2,1)} %refs_0_.6, bf16[4096,2048]{1,0:T(8,128)(2,1)} %refs_1_.5, bf16[48,256]{1,0:T(8,128)(2,1)S(1)} %get-tuple-element.46.refs_2_), custom_call_target="tpu_custom_call" | custom-call | flops 3221225472 | bytes 14680064 | tf_op jit(solution)/shard_map/second/pallas_call | solution.py:489
  14.5 3.0 %collective-permute-start.1 = (bf16[80,256]{1,0:T(8,128)(2,1)S(1)}, bf16[80,256]{1,0:T(8,128)(2,1)S(1)}, u32[]{:S(2)}, u32[]{:S(2)}) collective-permute-start(bf16[80,256]{1,0:T(8,128)(2,1)S(1)} %get-tuple-element.48), channel_id=1, source_target_pairs={{0,12},{4,8},{8,20},{12,16},{16,28},{20,24},{24,4},{28,0},{1,13},{... | collective-permute-start | bytes 122888 | tf_op jit(solution)/shard_map/ppermute | solution.py:574
  17.5 1.6 %collective-permute-start.2 = (bf16[80,256]{1,0:T(8,128)(2,1)S(1)}, bf16[80,256]{1,0:T(8,128)(2,1)S(1)}, u32[]{:S(2)}, u32[]{:S(2)}) collective-permute-start(bf16[80,256]{1,0:T(8,128)(2,1)S(1)} %get-tuple-element.49.refs_2_), channel_id=1, source_target_pairs={{0,8},{8,16},{16,24},{24,0},{1,9},{9,17},{17,25},{25,1},{2,10},{10... | collective-permute-start | bytes 122888 | tf_op jit(solution)/shard_map/ppermute | solution.py:577
  19.1 4.6 %z_other.1 = (bf16[1024,256]{1,0:T(8,128)(2,1)S(1)}, bf16[256,4096]{1,0:T(8,128)(2,1)S(1)}) custom-call(bf16[256,4096]{1,0:T(8,128)(2,1)} %refs_0_.6, bf16[4096,2048]{1,0:T(8,128)(2,1)} %refs_1_.7, bf16[80,256]{1,0:T(8,128)(2,1)S(1)} %get-tuple-element.49.refs_2_), custom_call_target="tpu_custom_call" | custom-call | flops 2147483648 | bytes 10485760 | tf_op jit(solution)/shard_map/z_other/pallas_call | solution.py:489
  23.8 1.6 %state.2 = (bf16[256,256]{1,0:T(8,128)(2,1)S(1)}, f32[256,256]{1,0:T(8,128)S(1)}, bf16[288,256]{1,0:T(8,128)(2,1)S(1)}, bf16[256,512]{1,0:T(8,128)(2,1)S(1)}, bf...) custom-call(bf16[800,256]{1,0:T(8,128)(2,1)S(1)} %get-tuple-element.45.refs_0_.refs_1_, ...), custom_call_target="tpu_custom_call" | custom-call | flops 50331648 | bytes 1572864 | tf_op jit(solution)/shard_map/state/pallas_call | solution.py:489
  25.4 1.4 %state.3 = (bf16[288,256]{1,0:T(8,128)(2,1)S(1)}, bf16[256,512]{1,0:T(8,128)(2,1)S(1)}, bf16[256,512]{1,0:T(8,128)(2,1)S(1)}, f32[8,256]{1,0:T(8,128)S(1)}, f32[256,8]{1,0:T(8,128)S(1)}) custom-call(bf16[256,256]{1,0:T(8,128)(2,1)S(1)} %get-tuple-element.56.refs_0_.refs_1_, bf16[800,256]{1,0:T(8,128)(2,1)S(1)} %get-tuple-element.45.refs_0_.refs_1_, ...), custom_call_target="tpu_custom_call" | custom-call | flops 50331648 | bytes 1572864 | tf_op jit(solution)/shard_map/state/pallas_call | solution.py:489
  27.4 1.6 %collective-permute-start.4 = (bf16[288,256]{1,0:T(8,128)(2,1)S(1)}, bf16[288,256]{1,0:T(8,128)(2,1)S(1)}, u32[]{:S(2)}, u32[]{:S(2)}) collective-permute-start(bf16[288,256]{1,0:T(8,128)(2,1)S(1)} %get-tuple-element.65.refs_0_.refs_6_), channel_id=1, source_target_pairs={{0,8},{8,0},{16,24},{24,16},{1,9},{9,1},{17,25},{25,17},{2,10},{10... | collective-permute-start | bytes 442376 | tf_op jit(solution)/shard_map/ppermute | solution.py:507
  29.4 3.5 %inner.1 = (f32[256,512]{1,0:T(8,128)S(1)}, f32[256,512]{1,0:T(8,128)S(1)}, bf16[1024,4096]{1,0:T(8,128)(2,1)S(1)}) custom-call(f32[256,256]{1,0:T(8,128)S(1)} %get-tuple-element.51.refs_0_, f32[1,32]{1,0:T(1,128)S(1)} %bitcast.18, bf16[2048,4096]{1,0:T(8,128)(2,1)} %refs_0_.7, bf16[256,512]{1,0:T(8,128)(2,1)S(1)} %get-tuple-element.52.refs_3_, ...), custom_call_target="tpu_custom_call" | custom-call | flops 268435456 | bytes 11534336 | tf_op jit(solution)/shard_map/inner/pallas_call | solution.py:489
  33.5 2.6 %collective-permute-start.8 = (bf16[288,256]{1,0:T(8,128)(2,1)S(1)}, bf16[288,256]{1,0:T(8,128)(2,1)S(1)}, u32[]{:S(2)}, u32[]{:S(2)}) collective-permute-start(bf16[288,256]{1,0:T(8,128)(2,1)S(1)} %combine.2.refs_3_), channel_id=1, source_target_pairs={{0,16},{8,24},{16,0},{24,8},{1,17},{9,25},{17,1},{25,9},{2,18},{10... | collective-permute-start | bytes 442376 | tf_op jit(solution)/shard_map/ppermute | solution.py:507
  36.3 2.6 %collective-permute-start.7 = (bf16[288,256]{1,0:T(8,128)(2,1)S(1)}, bf16[288,256]{1,0:T(8,128)(2,1)S(1)}, u32[]{:S(2)}, u32[]{:S(2)}) collective-permute-start(bf16[288,256]{1,0:T(8,128)(2,1)S(1)} %combine.3), channel_id=1, source_target_pairs={{0,16},{8,24},{16,0},{24,8},{1,17},{9,25},{17,1},{25,9},{2,18},{10... | collective-permute-start | bytes 442376 | tf_op jit(solution)/shard_map/ppermute | solution.py:507
  38.9 4.8 %z_own.1 = (bf16[1024,256]{1,0:T(8,128)(2,1)S(1)}, bf16[512,4096]{1,0:T(8,128)(2,1)S(1)}) custom-call(bf16[256,4096]{1,0:T(8,128)(2,1)S(1)} %get-tuple-element.64.refs_0_, bf16[4096,2048]{1,0:T(8,128)(2,1)} %refs_1_.7, bf16[2048,4096]{1,0:T(8,128)(2,1)} %refs_0_.7, bf16[288,256]{1,0:T(8,128)(2,1)S(1)} %combine.2.refs_3_, ...), custom_call_target="tpu_custom_call" | custom-call | flops 2147483648 | bytes 12582912 | tf_op jit(solution)/shard_map/z_own/pallas_call | solution.py:489
  43.7 2.2 %collective-permute-done.8.refs_8_ = bf16[288,256]{1,0:T(8,128)(2,1)S(1)} collective-permute-done((bf16[288,256]{1,0:T(8,128)(2,1)S(1)}, bf16[288,256]{1,0:T(8,128)(2,1)S(1)}, u32[]{:S(2)}, u32[]{:S(2)}) %collective-permute-start.8) | collective-permute-done | bytes 147488 | tf_op jit(solution)/shard_map/ppermute | solution.py:507
  46.8 1.2 %collective-permute-start.10 = (bf16[256,256]{1,0:T(8,128)(2,1)S(1)}, bf16[256,256]{1,0:T(8,128)(2,1)S(1)}, u32[]{:S(2)}, u32[]{:S(2)}) collective-permute-start(bf16[256,256]{1,0:T(8,128)(2,1)S(1)} %get-tuple-element.72.refs_4_), channel_id=1, source_target_pairs={{0,4},{4,0},{1,5},{5,1},{2,6},{6,2},{3,7},{7,3},{8,12},{12,8},{9,1... | collective-permute-start | bytes 393224 | tf_op jit(solution)/shard_map/ppermute | solution.py:507
  49.7 1.2 %collective-permute-start.9 = (bf16[256,256]{1,0:T(8,128)(2,1)S(1)}, bf16[256,256]{1,0:T(8,128)(2,1)S(1)}, u32[]{:S(2)}, u32[]{:S(2)}) collective-permute-start(bf16[256,256]{1,0:T(8,128)(2,1)S(1)} %get-tuple-element.70.refs_2_), channel_id=1, source_target_pairs={{0,4},{4,0},{1,5},{5,1},{2,6},{6,2},{3,7},{7,3},{8,12},{12,8},{9,1... | collective-permute-start | bytes 393224 | tf_op jit(solution)/shard_map/ppermute | solution.py:507
  51.8 2.4 %out_own.1 = (f32[256,4096]{1,0:T(8,128)S(1)}, bf16[512,4096]{1,0:T(8,128)(2,1)S(1)}) custom-call(bf16[2048,4096]{1,0:T(8,128)(2,1)} %refs_0_.7, bf16[1024,4096]{1,0:T(8,128)(2,1)S(1)} %get-tuple-element.62.refs_1_, bf16[256,256]{1,0:T(8,128)(2,1)S(1)} %get-tuple-element.70.refs_2_, bf16[256,256]{1,0:T(8,128)(2,1)S(1)} %get-tuple-element.71.refs_3_, ...), custom_call_target="tpu_custom_call" | custom-call | flops 2147483648 | bytes 12582912 | tf_op jit(solution)/shard_map/out_own/pallas_call | solution.py:489
  54.2 2.0 %collective-permute-done.9.refs_3_ = bf16[256,256]{1,0:T(8,128)(2,1)S(1)} collective-permute-done((bf16[256,256]{1,0:T(8,128)(2,1)S(1)}, bf16[256,256]{1,0:T(8,128)(2,1)S(1)}, u32[]{:S(2)}, u32[]{:S(2)}) %collective-permute-start.9) | collective-permute-done | bytes 131104 | tf_op jit(solution)/shard_map/ppermute | solution.py:507
  59.2 0.9 %collective-permute-done.14 = bf16[128,1024]{1,0:T(8,128)(2,1)S(1)} collective-permute-done((bf16[128,1024]{1,0:T(8,128)(2,1)S(1)}, bf16[128,1024]{1,0:T(8,128)(2,1)S(1)}, u32[]{:S(2)}, u32[]{:S(2)}) %collective-permute-start.14) | collective-permute-done | bytes 262176 | tf_op jit(solution)/shard_map/ppermute | solution.py:507
  60.2 1.6 %collective-permute-start.18 = (bf16[128,1024]{1,0:T(8,128)(2,1)S(1)}, bf16[128,1024]{1,0:T(8,128)(2,1)S(1)}, u32[]{:S(2)}, u32[]{:S(2)}) collective-permute-start(bf16[128,1024]{1,0:T(8,128)(2,1)S(1)} %add_convert_fusion.1.refs_5_), channel_id=1, source_target_pairs={{0,2},{1,3},{2,0},{3,1},{4,6},{5,7},{6,4},{7,5},{8,10},{9,11},{10,... | collective-permute-start | bytes 786440 | tf_op jit(solution)/shard_map/ppermute | solution.py:507
  64.2 5.2 %collective-permute-done.18 = bf16[128,1024]{1,0:T(8,128)(2,1)S(1)} collective-permute-done((bf16[128,1024]{1,0:T(8,128)(2,1)S(1)}, bf16[128,1024]{1,0:T(8,128)(2,1)S(1)}, u32[]{:S(2)}, u32[]{:S(2)}) %collective-permute-start.18) | collective-permute-done | bytes 262176 | tf_op jit(solution)/shard_map/ppermute | solution.py:507
  69.4 4.8 %collective-permute-done.17 = bf16[128,1024]{1,0:T(8,128)(2,1)S(1)} collective-permute-done((bf16[128,1024]{1,0:T(8,128)(2,1)S(1)}, bf16[128,1024]{1,0:T(8,128)(2,1)S(1)}, u32[]{:S(2)}, u32[]{:S(2)}) %collective-permute-start.17) | collective-permute-done | bytes 262176 | tf_op jit(solution)/shard_map/ppermute | solution.py:507
  74.2 1.0 %fusion = bf16[256,1024]{1,0:T(8,128)(2,1)} fusion(f32[128,1024]{1,0:T(8,128)S(1)} %convert_add_fusion, f32[128,1024]{1,0:T(8,128)S(1)} %convert_add_fusion.1, bf16[128,1024]{1,0:T(8,128)(2,1)S(1)} %collective-permute-done.18, bf16[128,1024]{1,0:T(8,128)(2,1)S(1)} %collective-permute-done.17), kind=kLoop, calls=%fused_computation.1 | loop fusion | flops 1835008 | bytes 2097152 | tf_op jit(solution)/shard_map/convert_element_type | solution.py:735
  (49 shorter events, 10.8 us)
Async XLA Ops:
  5.2 18.5 %collective-permute-start = (bf16[800,256]{1,0:T(8,128)(2,1)S(1)}, bf16[800,256]{1,0:T(8,128)(2,1)S(1)}, u32[]{:S(2)}, u32[]{:S(2)}) collective-permute-start(bf16[800,256]{1,0:T(8,128)(2,1)S(1)} %get-tuple-element.45.refs_0_.refs_1_), channel_id=1, source_target_pairs={{0,4},{4,0},{1,5},{5,1},{2,6},{6,2},{3,7},{7,3},{8,12},{12,8},{9,1... | collective-permute-start | bytes 1228808 | tf_op jit(solution)/shard_map/ppermute | solution.py:507
  14.4 11.0 %collective-permute-start.3 = (bf16[512,256]{1,0:T(8,128)(2,1)S(1)}, bf16[512,256]{1,0:T(8,128)(2,1)S(1)}, u32[]{:S(2)}, u32[]{:S(2)}) collective-permute-start(bf16[512,256]{1,0:T(8,128)(2,1)S(1)} %get-tuple-element.57), channel_id=1, source_target_pairs={{0,4},{4,0},{1,5},{5,1},{2,6},{6,2},{3,7},{7,3},{8,12},{12,8},{9,1... | collective-permute-start | bytes 786440 | tf_op jit(solution)/shard_map/ppermute | solution.py:507
  14.5 9.3 %collective-permute-start.1 = (bf16[80,256]{1,0:T(8,128)(2,1)S(1)}, bf16[80,256]{1,0:T(8,128)(2,1)S(1)}, u32[]{:S(2)}, u32[]{:S(2)}) collective-permute-start(bf16[80,256]{1,0:T(8,128)(2,1)S(1)} %get-tuple-element.48), channel_id=1, source_target_pairs={{0,12},{4,8},{8,20},{12,16},{16,28},{20,24},{24,4},{28,0},{1,13},{... | collective-permute-start | bytes 122888 | tf_op jit(solution)/shard_map/ppermute | solution.py:574
  17.5 6.3 %copy-start.1 = (f32[2048,4]{0,1:T(4,128)S(1)}, f32[2048,4]{0,1:T(4,128)}, u32[]{:S(2)}) copy-start(f32[2048,4]{0,1:T(4,128)} %param.20) | copy-start | bytes 98308
  17.5 6.3 %copy-start.3 = (f32[256,4]{0,1:T(4,128)S(1)}, f32[256,4]{0,1:T(4,128)}, u32[]{:S(2)}) copy-start(f32[256,4]{0,1:T(4,128)} %param.21) | copy-start | bytes 12292
  17.5 6.3 %copy-start.4 = (f32[32]{0:T(128)S(1)}, f32[32]{0:T(128)}, u32[]{:S(2)}) copy-start(f32[32]{0:T(128)} %param.17) | copy-start | bytes 388
  17.5 6.3 %copy-start.5 = (f32[32]{0:T(128)S(1)}, f32[32]{0:T(128)}, u32[]{:S(2)}) copy-start(f32[32]{0:T(128)} %param.18) | copy-start | bytes 388
  17.5 6.3 %collective-permute-start.2 = (bf16[80,256]{1,0:T(8,128)(2,1)S(1)}, bf16[80,256]{1,0:T(8,128)(2,1)S(1)}, u32[]{:S(2)}, u32[]{:S(2)}) collective-permute-start(bf16[80,256]{1,0:T(8,128)(2,1)S(1)} %get-tuple-element.49.refs_2_), channel_id=1, source_target_pairs={{0,8},{8,16},{16,24},{24,0},{1,9},{9,17},{17,25},{25,1},{2,10},{10... | collective-permute-start | bytes 122888 | tf_op jit(solution)/shard_map/ppermute | solution.py:577
  26.8 19.1 %collective-permute-start.5 = (bf16[1024,256]{1,0:T(8,128)(2,1)S(1)}, bf16[1024,256]{1,0:T(8,128)(2,1)S(1)}, u32[]{:S(2)}, u32[]{:S(2)}) collective-permute-start(bf16[1024,256]{1,0:T(8,128)(2,1)S(1)} %get-tuple-element.69.refs_10_.refs_11_), channel_id=1, source_target_pairs={{0,4},{4,0},{1,5},{5,1},{2,6},{6,2},{3,7},{7,3},{8,12},{12,8},{9,1... | collective-permute-start | bytes 1572872 | tf_op jit(solution)/shard_map/ppermute | solution.py:507
  27.4 6.0 %collective-permute-start.4 = (bf16[288,256]{1,0:T(8,128)(2,1)S(1)}, bf16[288,256]{1,0:T(8,128)(2,1)S(1)}, u32[]{:S(2)}, u32[]{:S(2)}) collective-permute-start(bf16[288,256]{1,0:T(8,128)(2,1)S(1)} %get-tuple-element.65.refs_0_.refs_6_), channel_id=1, source_target_pairs={{0,8},{8,0},{16,24},{24,16},{1,9},{9,1},{17,25},{25,17},{2,10},{10... | collective-permute-start | bytes 442376 | tf_op jit(solution)/shard_map/ppermute | solution.py:507
  29.0 7.3 %collective-permute-start.6 = (bf16[288,256]{1,0:T(8,128)(2,1)S(1)}, bf16[288,256]{1,0:T(8,128)(2,1)S(1)}, u32[]{:S(2)}, u32[]{:S(2)}) collective-permute-start(bf16[288,256]{1,0:T(8,128)(2,1)S(1)} %get-tuple-element.68.refs_0_.refs_6_), channel_id=1, source_target_pairs={{0,8},{8,0},{16,24},{24,16},{1,9},{9,1},{17,25},{25,17},{2,10},{10... | collective-permute-start | bytes 442376 | tf_op jit(solution)/shard_map/ppermute | solution.py:507
  33.5 12.5 %collective-permute-start.8 = (bf16[288,256]{1,0:T(8,128)(2,1)S(1)}, bf16[288,256]{1,0:T(8,128)(2,1)S(1)}, u32[]{:S(2)}, u32[]{:S(2)}) collective-permute-start(bf16[288,256]{1,0:T(8,128)(2,1)S(1)} %combine.2.refs_3_), channel_id=1, source_target_pairs={{0,16},{8,24},{16,0},{24,8},{1,17},{9,25},{17,1},{25,9},{2,18},{10... | collective-permute-start | bytes 442376 | tf_op jit(solution)/shard_map/ppermute | solution.py:507
  36.3 12.5 %collective-permute-start.7 = (bf16[288,256]{1,0:T(8,128)(2,1)S(1)}, bf16[288,256]{1,0:T(8,128)(2,1)S(1)}, u32[]{:S(2)}, u32[]{:S(2)}) collective-permute-start(bf16[288,256]{1,0:T(8,128)(2,1)S(1)} %combine.3), channel_id=1, source_target_pairs={{0,16},{8,24},{16,0},{24,8},{1,17},{9,25},{17,1},{25,9},{2,18},{10... | collective-permute-start | bytes 442376 | tf_op jit(solution)/shard_map/ppermute | solution.py:507
  38.9 7.0 %copy-start.2 = (f32[2048]{0:T(1024)S(1)}, f32[2048]{0:T(1024)}, u32[]{:S(2)}) copy-start(f32[2048]{0:T(1024)} %param.22) | copy-start | bytes 24580
  46.8 7.4 %collective-permute-start.10 = (bf16[256,256]{1,0:T(8,128)(2,1)S(1)}, bf16[256,256]{1,0:T(8,128)(2,1)S(1)}, u32[]{:S(2)}, u32[]{:S(2)}) collective-permute-start(bf16[256,256]{1,0:T(8,128)(2,1)S(1)} %get-tuple-element.72.refs_4_), channel_id=1, source_target_pairs={{0,4},{4,0},{1,5},{5,1},{2,6},{6,2},{3,7},{7,3},{8,12},{12,8},{9,1... | collective-permute-start | bytes 393224 | tf_op jit(solution)/shard_map/ppermute | solution.py:507
  48.0 9.7 %collective-permute-start.13 = (bf16[256,256]{1,0:T(8,128)(2,1)S(1)}, bf16[256,256]{1,0:T(8,128)(2,1)S(1)}, u32[]{:S(2)}, u32[]{:S(2)}) collective-permute-start(bf16[256,256]{1,0:T(8,128)(2,1)S(1)} %get-tuple-element.73.refs_5_), channel_id=1, source_target_pairs={{0,4},{4,0},{1,5},{5,1},{2,6},{6,2},{3,7},{7,3},{8,12},{12,8},{9,1... | collective-permute-start | bytes 393224 | tf_op jit(solution)/shard_map/ppermute | solution.py:507
  49.7 6.4 %collective-permute-start.9 = (bf16[256,256]{1,0:T(8,128)(2,1)S(1)}, bf16[256,256]{1,0:T(8,128)(2,1)S(1)}, u32[]{:S(2)}, u32[]{:S(2)}) collective-permute-start(bf16[256,256]{1,0:T(8,128)(2,1)S(1)} %get-tuple-element.70.refs_2_), channel_id=1, source_target_pairs={{0,4},{4,0},{1,5},{5,1},{2,6},{6,2},{3,7},{7,3},{8,12},{12,8},{9,1... | collective-permute-start | bytes 393224 | tf_op jit(solution)/shard_map/ppermute | solution.py:507
  50.9 6.8 %collective-permute-start.12 = (bf16[256,256]{1,0:T(8,128)(2,1)S(1)}, bf16[256,256]{1,0:T(8,128)(2,1)S(1)}, u32[]{:S(2)}, u32[]{:S(2)}) collective-permute-start(bf16[256,256]{1,0:T(8,128)(2,1)S(1)} %get-tuple-element.71.refs_3_), channel_id=1, source_target_pairs={{0,4},{4,0},{1,5},{5,1},{2,6},{6,2},{3,7},{7,3},{8,12},{12,8},{9,1... | collective-permute-start | bytes 393224 | tf_op jit(solution)/shard_map/ppermute | solution.py:507
  58.5 1.6 %collective-permute-start.14 = (bf16[128,1024]{1,0:T(8,128)(2,1)S(1)}, bf16[128,1024]{1,0:T(8,128)(2,1)S(1)}, u32[]{:S(2)}, u32[]{:S(2)}) collective-permute-start(bf16[128,1024]{1,0:T(8,128)(2,1)S(1)} %get-tuple-element.81), channel_id=1, source_target_pairs={{0,1},{1,0},{2,3},{3,2},{4,5},{5,4},{6,7},{7,6},{8,9},{9,8},{10,11... | collective-permute-start | bytes 786440 | tf_op jit(solution)/shard_map/ppermute | solution.py:507
  58.6 4.1 %collective-permute-start.16 = (bf16[128,1024]{1,0:T(8,128)(2,1)S(1)}, bf16[128,1024]{1,0:T(8,128)(2,1)S(1)}, u32[]{:S(2)}, u32[]{:S(2)}) collective-permute-start(bf16[128,1024]{1,0:T(8,128)(2,1)S(1)} %get-tuple-element.84), channel_id=1, source_target_pairs={{0,1},{1,0},{2,3},{3,2},{4,5},{5,4},{6,7},{7,6},{8,9},{9,8},{10,11... | collective-permute-start | bytes 786440 | tf_op jit(solution)/shard_map/ppermute | solution.py:507
  59.1 4.2 %collective-permute-start.11 = (bf16[128,1024]{1,0:T(8,128)(2,1)S(1)}, bf16[128,1024]{1,0:T(8,128)(2,1)S(1)}, u32[]{:S(2)}, u32[]{:S(2)}) collective-permute-start(bf16[128,1024]{1,0:T(8,128)(2,1)S(1)} %get-tuple-element.79), channel_id=1, source_target_pairs={{0,1},{1,0},{2,3},{3,2},{4,5},{5,4},{6,7},{7,6},{8,9},{9,8},{10,11... | collective-permute-start | bytes 786440 | tf_op jit(solution)/shard_map/ppermute | solution.py:507
  60.2 9.2 %collective-permute-start.18 = (bf16[128,1024]{1,0:T(8,128)(2,1)S(1)}, bf16[128,1024]{1,0:T(8,128)(2,1)S(1)}, u32[]{:S(2)}, u32[]{:S(2)}) collective-permute-start(bf16[128,1024]{1,0:T(8,128)(2,1)S(1)} %add_convert_fusion.1.refs_5_), channel_id=1, source_target_pairs={{0,2},{1,3},{2,0},{3,1},{4,6},{5,7},{6,4},{7,5},{8,10},{9,11},{10,... | collective-permute-start | bytes 786440 | tf_op jit(solution)/shard_map/ppermute | solution.py:507
  62.6 1.6 %collective-permute-start.15 = (bf16[128,1024]{1,0:T(8,128)(2,1)S(1)}, bf16[128,1024]{1,0:T(8,128)(2,1)S(1)}, u32[]{:S(2)}, u32[]{:S(2)}) collective-permute-start(bf16[128,1024]{1,0:T(8,128)(2,1)S(1)} %get-tuple-element.83), channel_id=1, source_target_pairs={{0,1},{1,0},{2,3},{3,2},{4,5},{5,4},{6,7},{7,6},{8,9},{9,8},{10,11... | collective-permute-start | bytes 786440 | tf_op jit(solution)/shard_map/ppermute | solution.py:507
  62.7 11.5 %collective-permute-start.17 = (bf16[128,1024]{1,0:T(8,128)(2,1)S(1)}, bf16[128,1024]{1,0:T(8,128)(2,1)S(1)}, u32[]{:S(2)}, u32[]{:S(2)}) collective-permute-start(bf16[128,1024]{1,0:T(8,128)(2,1)S(1)} %add_convert_fusion), channel_id=1, source_target_pairs={{0,2},{1,3},{2,0},{3,1},{4,6},{5,7},{6,4},{7,5},{8,10},{9,11},{10,... | collective-permute-start | bytes 786440 | tf_op jit(solution)/shard_map/ppermute | solution.py:507
  (2 other events, 6.6 us)

commit v4 on v3

--- a/solution.py
+++ b/solution.py
@@ -221,27 +221,15 @@
     ]
 
 
-def inner_kernel(scores, skip, w_out, *refs, chunks, head_dim, lanes):
-    scans, refs = [refs[4 * c : 4 * c + 4] for c in range(chunks)], refs[4 * chunks :]
-    *outs, w_own, sems = refs
-    where = place()
-    half = w_own.shape[0]
-    started = copies(rows_of(w_out, w_own, pl.multiple_of(where[0] * half, half), lanes), sems)
-
-    @pl.when(where[0] >= 0)
-    def _():
-        heads = half // head_dim
-        for c in range(chunks):
-            within(
-                where, scores, *scans[c], skip, outs[c], head_dim=head_dim,
-                first_of=c * heads // chunks, local_heads=heads,
-            )
-
-    for now in started:
-        now.wait()
-
-
-def own_gate_kernel(tok, weight, w_out, mine, w_early, held, acc, sems, *, kb):
+def inner_kernel(scores, skip, scaled, conv_out, cum, cum_t, out, *, chunk, chunks, head_dim):
+    heads = scaled.shape[1] // head_dim
+    within(
+        place(), scores, scaled, conv_out, cum, cum_t, skip, out,
+        head_dim=head_dim, first_of=chunk * heads, local_heads=chunks * heads,
+    )
+
+
+def own_gate_kernel(tok, weight, w_out, mine, w_own, held, acc, sems, *, kb):
     toks, width = acc.shape
     lanes = mine.shape[1]
     row = place()[0]
@@ -251,7 +239,7 @@
         (weight.at[pl.ds(i * kb, kb), pl.ds(low, width)], held.at[pl.ds(i * kb, kb), :])
         for i in range(parts)
     ]
-    pairs += rows_of(w_out, w_early, pl.multiple_of((1 - row) * width, width), lanes)
+    pairs += rows_of(w_out, w_own, pl.multiple_of(row * width, lanes), lanes)
     started = copies(pairs, sems)
     product(tok, held, [[now] for now in started[:parts]], acc, kb)
     for j in range(width // lanes):
@@ -392,7 +380,7 @@
         cols = slice(j * lanes, (j + 1) * lanes)
         scanned = inner[:, cols] + grown[:, cols] * mm(c_now, enter.astype(bf16))
         z_low = (chunk * inner.shape[1] // lanes + j) * toks
-        z_now = total(z_mine[z_low : z_low + toks, :], z_theirs[z_low : z_low + toks, :])
+        z_now = total(z_mine[z_low : z_low + toks, :], z_theirs[j * toks : (j + 1) * toks, :])
         gated = scanned * silu(z_now)
         square = gated * gated
         for i in range(lanes // wide):
@@ -411,76 +399,83 @@
                 out[j * size : (j + 1) * size, i * wide : (i + 1) * wide] = done[start:end]
 
 
-def own_kernel(weight, w_own, *refs, bounds):
-    *normed, partial, w_late, whole, sems = refs
+def own_kernel(weight, w_first, *refs, cuts):
+    *normed, partial, rest, w_last, whole, sems = refs
     lanes = normed[0].shape[1]
+    half = rest.shape[0]
     row = place()[0]
-    late = pl.multiple_of((2 - row) * w_own.shape[0] - w_late.shape[0], lanes)
-    started = copies(rows_of(weight, w_late, late, lanes), sems)
+    first = w_first.shape[0]
+    pairs = rows_of(weight, w_last, pl.multiple_of(row * half + first, lanes), lanes)
+    needed = len(pairs)
+    pairs += rows_of(weight, rest, pl.multiple_of((1 - row) * half, lanes), lanes)
+    started = copies(pairs, sems)
+    for now in started[:needed]:
+        now.wait()
 
     @pl.when(row >= 0)
     def _():
-        own_product(w_own, normed, partial, whole, bounds)
-
-    for now in started:
+        own_product(w_first, w_last, normed, partial, whole, cuts)
+
+    for now in started[needed:]:
         now.wait()
 
 
-def own_product(weight, normed, partial, whole, bounds):
+def own_product(w_first, w_last, normed, partial, whole, cuts):
+    cut_row = w_first.shape[0]
     width = partial.shape[1]
     lanes = normed[0].shape[1]
-    low = 0
-    for chunk in zip(*[iter(normed)] * len(bounds)):
-        blocks = chunk[0].shape[0] // (bounds[0][1] - bounds[0][0])
+    low = whole.shape[1]
+    for cut in cuts[::-1]:
+        parts, normed = normed[: len(cut)], normed[len(cut) :]
+        blocks = parts[0].shape[0] // (cut[0][1] - cut[0][0])
+        low -= blocks * lanes
         for j in range(blocks):
-            for (start, end), part in zip(bounds, chunk):
+            for (start, end), part in zip(cut, parts):
                 size = end - start
-                whole[start:end, low : low + lanes] = part[j * size : (j + 1) * size, :]
-            low += lanes
+                whole[start:end, low + j * lanes : low + (j + 1) * lanes] = part[j * size : (j + 1) * size, :]
     for low in range(0, width, 512):
         cols = slice(low, min(low + 512, width))
-        partial[:, cols] = mm(whole[...], weight[:, cols])
-
-
-def rest_kernel(partial, w_early, w_late, *refs, jobs):
+        partial[:, cols] = mm(whole[:, :cut_row], w_first[:, cols]) + mm(whole[:, cut_row:], w_last[:, cols])
+
+
+def rest_kernel(partial, rest, *refs, start, end, far):
     *normed, send, keep = refs
     lanes = normed[0].shape[1]
     piece = send.shape[1]
+    size = end - start
     step = min(512, piece)
+    blocks = rest.shape[0] // lanes // len(normed)
     _, col, _ = place()
-    at_row = 0
-    for i, (start, end, far, crossed) in enumerate(jobs):
-        size = end - start
-        pair = 1 - col // 2 if far else col // 2
-        kept = (col + crossed) % 2
-        for target, core in ((send, 1 - kept), (keep, kept)):
-            base = (pair * 2 + core) * piece
-            for low in range(0, piece, step):
-                cols = pl.ds(pl.multiple_of(base + low, step), step)
-                acc = partial[start:end, cols]
-                row = 0
-                for chunk in normed[i :: len(jobs)]:
-                    for j in range(chunk.shape[0] // size):
-                        first = row < w_early.shape[0]
-                        held = w_early if first else w_late
-                        held_row = row - (0 if first else w_early.shape[0])
-                        acc = acc + mm(
-                            chunk[j * size : (j + 1) * size, :], held[held_row : held_row + lanes, cols]
-                        )
-                        row += lanes
-                target[at_row : at_row + size, low : low + step] = acc.astype(bf16)
-        at_row += size
+    pair = 1 - col // 2 if far else col // 2
+    for target, core in ((send, 1 - col % 2), (keep, col % 2)):
+        base = (pair * 2 + core) * piece
+        for low in range(0, piece, step):
+            cols = pl.ds(pl.multiple_of(base + low, step), step)
+            acc = partial[start:end, cols]
+            row = 0
+            for chunk in normed[::-1]:
+                held_toks = chunk.shape[0] // blocks
+                first = start if held_toks > size else 0
+                for j in range(blocks):
+                    now = chunk[j * held_toks + first : j * held_toks + first + size, :]
+                    acc = acc + mm(now, rest[row : row + lanes, cols])
+                    row += lanes
+            target[:, low : low + step] = acc.astype(bf16)
+
+
+def final_kernel(*refs, bounds):
+    *parts, out = refs
+    for i, (start, end) in enumerate(bounds):
+        far, keep, got = parts[3 * i : 3 * i + 3]
+        total_now = far[...].astype(f32) + keep[...].astype(f32) + got[...].astype(f32)
+        out[start:end, :] = total_now.astype(bf16)
 
 
 def sds(*shape, dtype=bf16):
     return jax.ShapeDtypeStruct(shape, dtype)
 
 
-def cost(flops, size):
-    return pl.CostEstimate(flops=int(flops), bytes_accessed=int(size), transcendentals=0)
-
-
-def call(kernel, args, specs, outs, scratch=(), flops=0, size=0, name=None, mib=16, after=()):
+def call(kernel, args, specs, outs, scratch=(), name=None, mib=16, after=()):
     used = len(args)
 
     def body(*refs):
@@ -492,8 +487,8 @@
         out_specs=[IN_VMEM] * len(outs),
         scratch_shapes=list(scratch),
         out_shape=outs,
-        compiler_params=pltpu.CompilerParams(vmem_limit_bytes=mib * MIB),
-        cost_estimate=cost(flops, size),
+        compiler_params=pltpu.CompilerParams(vmem_limit_bytes=int(mib * MIB)),
+        cost_estimate=pl.CostEstimate(flops=0, bytes_accessed=0, transcendentals=0),
         name=name,
     )(*args, *after)
 
@@ -546,10 +541,8 @@
             pltpu.VMEM((heads, toks), f32),
             pltpu.SemaphoreType.DMA((4 * parts,)),
         ],
-        flops=2 * toks * depth * (width + lanes + heads),
-        size=2 * depth * (toks + width + lanes + heads),
         name="first",
-        mib=53,
+        mib=53.9,
     )
     first_got = swapped(msg_first, "row", 1)
     msg_second, x_mine, edge_other, edge_own = call(
@@ -564,8 +557,6 @@
             pltpu.VMEM((toks, width + half), f32),
             pltpu.SemaphoreType.DMA((3 * parts + 1,)),
         ],
-        flops=2 * toks * depth * (width + half),
-        size=2 * depth * (toks + width + half),
         name="second",
         mib=52,
     )
@@ -575,18 +566,16 @@
         edge_other, ("ctx", "row"), [(2 * i + s, 2 * j + 1 - s) for i, j in down for s in range(2)]
     )
     edge_b = lax.ppermute(edge_own, "ctx", down)
-    z_send, tok_held = call(
+    *z_send, tok_held = call(
         functools.partial(gate_product_kernel, kb=kb),
         (tokens, proj_z),
         [IN_HBM] * 2,
-        [sds(chunks * blocks * toks, lanes), sds(toks, depth)],
+        [*[sds(blocks * toks, lanes)] * chunks, sds(toks, depth)],
         [
             pltpu.VMEM((depth, half), bf16),
             pltpu.VMEM((toks, half), f32),
             pltpu.SemaphoreType.DMA((2 * parts,)),
         ],
-        flops=2 * toks * depth * half,
-        size=2 * depth * (toks + half),
         name="z_other",
         mib=50,
         after=(edge_own,),
@@ -618,10 +607,8 @@
             None,
             outs,
             [pltpu.VMEM((HALO + toks, lanes), f32)],
-            flops=2 * toks * width * (state_dim + 64),
-            size=2 * toks * width * 6,
             name="state",
-            after=(z_send,),
+            after=(z_send[0],),
         )
         if c == 0:
             bc_now, scores, *got = got
@@ -629,9 +616,22 @@
         scans.append(got[1:])
 
     z_send, _ = lax.optimization_barrier((z_send, states))
-    z_got = swapped(z_send, "row", 1)
-    messages, sent = [], []
+    z_got = [swapped(z, "row", 1) for z in z_send]
+    def inner_call(c):
+        (inner,) = call(
+            functools.partial(inner_kernel, chunk=c, chunks=chunks, head_dim=head_dim),
+            (scores, skip, *scans[c]),
+            None,
+            [sds(toks, width, dtype=f32)],
+            name="inner",
+            after=sent[:1],
+        )
+        return inner
+
+    messages, sent, inners = [], [], []
     for c in range(chunks):
+        if c == 1:
+            inners = [inner_call(i) for i in range(chunks)]
         heard = [states[c]]
         send = states[c]
         by = 1
@@ -639,28 +639,14 @@
             if by > 1:
                 (send,) = call(
                     functools.partial(combine_kernel, state_dim=state_dim, lanes=lanes),
-                    heard, None, [sds(*send.shape)],
-                    flops=send.size * 6, size=send.size * 6, name="combine",
+                    heard, None, [sds(*send.shape)], name="combine", after=(*sent, *inners),
                 )
             heard.append(swapped(send, "ctx", by))
             by *= 2
         messages.append(heard)
         sent.append(send)
-
-    args = (scores, skip, proj_out, *[a for scan in scans for a in scan])
-    *inners, w_own = call(
-        functools.partial(inner_kernel, chunks=chunks, head_dim=head_dim, lanes=lanes),
-        args,
-        [IN_VMEM, IN_VMEM, IN_HBM, *[IN_VMEM] * (len(args) - 3)],
-        [*[sds(toks, width, dtype=f32)] * chunks, sds(half, out_cols)],
-        [pltpu.SemaphoreType.DMA((half // lanes,))],
-        flops=4 * toks * toks * half,
-        size=4 * toks * half * 3 + 2 * half * out_cols,
-        name="inner",
-        mib=42,
-    )
     early = half // 2
-    z_mine, w_early = call(
+    z_mine, w_first = call(
         functools.partial(own_gate_kernel, kb=kb),
         (tok_held, proj_z, proj_out),
         [IN_VMEM, IN_HBM, IN_HBM],
@@ -670,69 +656,70 @@
             pltpu.VMEM((toks, half), f32),
             pltpu.SemaphoreType.DMA((parts + early // lanes,)),
         ],
-        flops=2 * toks * half * depth,
-        size=2 * depth * half + 2 * early * out_cols,
         name="z_own",
-        mib=34,
-        after=(sent[-1], inners[-1]),
+        mib=38,
+        after=(*sent, *inners),
     )
 
     normed, normed_got = [], []
-    cut = toks * 8 // 16
-    bounds = ((0, cut), (cut, toks))
+    bounds = ((0, toks // 2), (toks // 2, toks))
+    cuts = [((0, toks),)] * (chunks - 1) + [bounds]
     for c in range(chunks):
         now = call(
             functools.partial(
-                gate_kernel, messages=len(messages[c]), bounds=bounds, chunk=c, chunks=chunks, **sizes
+                gate_kernel, messages=len(messages[c]), bounds=cuts[c], chunk=c, chunks=chunks, **sizes
             ),
-            (inners[c], bc_now, scans[c][2], z_mine, z_got, gain, *messages[c]),
+            (inners[c], bc_now, scans[c][2], z_mine, z_got[c], gain, *messages[c]),
             None,
-            [sds(blocks * (end - start), lanes) for start, end in bounds],
-            flops=2 * toks * width * (state_dim + 4 * head_dim),
-            size=2 * toks * width * 6,
+            [sds(blocks * (end - start), lanes) for start, end in cuts[c]],
             name="gate",
         )
         normed.append(now)
         normed_got.append([swapped(part, "row", 1) for part in now])
 
     piece = out_cols // lax.axis_size("col")
-    partial, w_late = call(
-        functools.partial(own_kernel, bounds=bounds),
-        (proj_out, w_own, *[part for now in normed for part in now]),
-        [IN_HBM, *[IN_VMEM] * (1 + len(bounds) * chunks)],
-        [sds(toks, out_cols, dtype=f32), sds(half - early, out_cols)],
-        [pltpu.VMEM((toks, half), bf16), pltpu.SemaphoreType.DMA(((half - early) // lanes,))],
-        flops=2 * toks * half * out_cols,
-        size=2 * (2 * half - early) * out_cols,
+    partial, rest = call(
+        functools.partial(own_kernel, cuts=cuts),
+        (proj_out, w_first, *[part for now in normed[::-1] for part in now]),
+        [IN_HBM, *[IN_VMEM] * (1 + sum(len(cut) for cut in cuts))],
+        [sds(toks, out_cols, dtype=f32), sds(half, out_cols)],
+        [
+            pltpu.VMEM((half - early, out_cols), bf16),
+            pltpu.VMEM((toks, half), bf16),
+            pltpu.SemaphoreType.DMA(((2 * half - early) // lanes,)),
+        ],
         name="out_own",
-        mib=26,
-    )
-
-    def out_rest(jobs, name, after=()):
-        args = (partial, w_early, w_late, *[now[part] for now in normed_got for part, *_ in jobs])
-        jobs = tuple((*bounds[part], far, crossed) for part, far, crossed in jobs)
+        mib=34,
+    )
+
+    def out_rest(part, far, after):
+        start, end = bounds[part]
+        args = (partial, rest, *[now[min(part, len(now) - 1)] for now in normed_got[::-1]])
         return call(
-            functools.partial(rest_kernel, jobs=jobs),
+            functools.partial(rest_kernel, start=start, end=end, far=far),
             args,
             None,
-            [sds(sum(end - start for start, end, *_ in jobs), piece)] * 2,
-            name=name,
+            [sds(end - start, piece)] * 2,
+            name="out_far" if far else "out_near",
             after=after,
         )
 
     def added(a, b):
         return (a.astype(f32) + b.astype(f32)).astype(bf16)
 
-    got_far, near, order = [], [], ()
+    sends, sums, keep = [], [], None
     for part in range(len(bounds)):
-        send, keep = out_rest(((part, True, 0),), "out_far", order)
-        far = added(keep, swapped(send, "col", 1))
-        got_far.append(swapped(far, "col", 2))
-        order = (keep,) if part == 0 else (far,)
-        send, keep = out_rest(((part, False, 0),), "out_near", order)
-        near.append(keep.astype(f32) + swapped(send, "col", 1).astype(f32))
-        order = (keep,)
-    return (jnp.concatenate(near) + jnp.concatenate(got_far).astype(f32)).astype(bf16)
+        send, far_keep = out_rest(part, True, () if keep is None else (keep,))
+        sums.append(added(far_keep, swapped(send, "col", 1)))
+        send, keep = out_rest(part, False, (far_keep,))
+        sends.append((send, keep))
+    args = []
+    for far, (send, keep) in zip(sums, sends):
+        args += [swapped(far, "col", 2), keep, swapped(send, "col", 1)]
+    (out,) = call(
+        functools.partial(final_kernel, bounds=bounds), args, None, [sds(toks, piece)], name="final"
+    )
+    return out
 
 
 def shifted(shard, axis, by):

time: 75.3 us -> 73.5 us (0.976)
  starting transfers between devices: 22.6 us -> 20.1 us
  Pallas kernels: 33.5 us -> 35.4 us
  other arithmetic: 1.21 us -> 0.13 us
  local copies, waits for them, and re-layouts: 0.97 us -> 0.03 us
  waiting for transfers between devices: 16.6 us -> 17.4 us
    ppermute x17, starting transfers between devices: 18 us -> 15.3 us  [swapped(): return lax.ppermute(shard, axis, [(i, i ^ by) for i in range(devices)])]
    pallas_call x16 -> x18, Pallas kernels: 33.5 us -> 35.4 us  [call(): pl.pallas_call(body, in_specs=[*(specs or [IN_VMEM] * used), *[pl.BlockSp...]
    convert_element_type x1 -> x0, other arithmetic: 0.96 us -> none  [fast(): (jnp.concatenate(near) + jnp.concatenate(got_far).astype(f32)).astype(bf16)]
    unnamed x14, local copies, waits for them, and re-layouts: 0.97 us -> 0.03 us
    ppermute x17, waiting for transfers between devices: 16.6 us -> 17.4 us  [swapped(): return lax.ppermute(shard, axis, [(i, i ^ by) for i in range(devices)])]
  transfers between devices with their start and end apart: 19 -> 19, of which waited for: 8 -> 8; matrix products, arithmetic and copies ran while one was open for 0% -> 0% of each run, Pallas kernels for 36% -> 39%
where the time goes in v4:
time: 73.5 us; the launch traced here: 73.4 us
  Pallas kernels  35.4 us (48%)
  starting transfers between devices  20.1 us (27%)
  waiting for transfers between devices  17.4 us (24%)
    pallas_call x18, Pallas kernels, call(): pl.pallas_call(body, in_specs=[*(specs or [IN_VMEM] * used), *[pl.BlockSp...  35.4 us
    ppermute x17, waiting for transfers between devices, swapped(): return lax.ppermute(shard, axis, [(i, i ^ by) for i in range(devices)])  17.4 us
    ppermute x17, starting transfers between devices, swapped(): return lax.ppermute(shard, axis, [(i, i ^ by) for i in range(devices)])  15.3 us
    ppermute x1, starting transfers between devices, fast(): lax.ppermute(edge_other, ('ctx', 'row'), [(2 * i + s, 2 * j + 1 - s) for...  2.72 us
    ppermute x1, starting transfers between devices, fast(): edge_b = lax.ppermute(edge_own, 'ctx', down)  2.09 us
  transfers between devices with their start and end apart: 19, of which 8 were waited for; matrix products, arithmetic and copies ran while one was open for 0% of the time, Pallas kernels for 39%

profile of v4, /device:TPU:0, one launch (start us, length us, event | category | flops | bytes accessed | tf_op | source)
XLA Modules:
  0.0 73.4 jit_solution(10205810555449651750)
XLA Ops:
  0.0 5.0 %first.1 = (bf16[800,256]{1,0:T(8,128)(2,1)}, bf16[48,256]{1,0:T(8,128)(2,1)S(1)}) custom-call(bf16[256,4096]{1,0:T(8,128)(2,1)} %refs_0_.6, bf16[4096,2048]{1,0:T(8,128)(2,1)} %refs_1_.5, bf16[4096,256]{1,0:T(8,128)(2,1)} %refs_2_.2, bf16[32,4096]{1,0:T(8,128)(2,1)} %bitcast.19), custom_call_target="tpu_custom_call" | custom-call | tf_op jit(solution)/shard_map/first/pallas_call | solution.py:484
  5.0 3.0 %collective-permute-start = (bf16[800,256]{1,0:T(8,128)(2,1)}, bf16[800,256]{1,0:T(8,128)(2,1)S(1)}, u32[]{:S(2)}, u32[]{:S(2)}) collective-permute-start(bf16[800,256]{1,0:T(8,128)(2,1)} %get-tuple-element.45.refs_0_.refs_1_), channel_id=1, source_target_pairs={{0,4},{4,0},{1,5},{5,1},{2,6},{6,2},{3,7},{7,3},{8,12},{12,8},{9,1... | collective-permute-start | bytes 1228808 | tf_op jit(solution)/shard_map/ppermute | solution.py:502
  8.0 6.1 %second.1 = (bf16[512,256]{1,0:T(8,128)(2,1)S(1)}, bf16[1024,256]{1,0:T(8,128)(2,1)S(1)}, bf16[80,256]{1,0:T(8,128)(2,1)S(1)}, bf16[80,256]{1,0:T(8,128)(2,1)S(1)}) custom-call(bf16[256,4096]{1,0:T(8,128)(2,1)} %refs_0_.6, bf16[4096,2048]{1,0:T(8,128)(2,1)} %refs_1_.5, bf16[48,256]{1,0:T(8,128)(2,1)S(1)} %get-tuple-element.42.refs_2_), custom_call_target="tpu_custom_call" | custom-call | tf_op jit(solution)/shard_map/second/pallas_call | solution.py:484
  14.3 2.1 %collective-permute-start.2 = (bf16[80,256]{1,0:T(8,128)(2,1)S(1)}, bf16[80,256]{1,0:T(8,128)(2,1)S(1)}, u32[]{:S(2)}, u32[]{:S(2)}) collective-permute-start(bf16[80,256]{1,0:T(8,128)(2,1)S(1)} %get-tuple-element.43.refs_2_), channel_id=1, source_target_pairs={{0,8},{8,16},{16,24},{24,0},{1,9},{9,17},{17,25},{25,1},{2,10},{10... | collective-permute-start | bytes 122888 | tf_op jit(solution)/shard_map/ppermute | solution.py:568
  16.4 2.7 %collective-permute-start.1 = (bf16[80,256]{1,0:T(8,128)(2,1)S(1)}, bf16[80,256]{1,0:T(8,128)(2,1)S(1)}, u32[]{:S(2)}, u32[]{:S(2)}) collective-permute-start(bf16[80,256]{1,0:T(8,128)(2,1)S(1)} %get-tuple-element.47), channel_id=1, source_target_pairs={{0,12},{4,8},{8,20},{12,16},{16,28},{20,24},{24,4},{28,0},{1,13},{... | collective-permute-start | bytes 122888 | tf_op jit(solution)/shard_map/ppermute | solution.py:565
  19.1 4.6 %z_other.1 = (bf16[512,256]{1,0:T(8,128)(2,1)S(1)}, bf16[512,256]{1,0:T(8,128)(2,1)S(1)}, bf16[256,4096]{1,0:T(8,128)(2,1)S(1)}) custom-call(bf16[256,4096]{1,0:T(8,128)(2,1)} %refs_0_.6, bf16[4096,2048]{1,0:T(8,128)(2,1)} %refs_1_.7, bf16[80,256]{1,0:T(8,128)(2,1)S(1)} %get-tuple-element.43.refs_2_), custom_call_target="tpu_custom_call" | custom-call | tf_op jit(solution)/shard_map/z_other/pallas_call | solution.py:484
  23.8 1.6 %state.2 = (bf16[256,256]{1,0:T(8,128)(2,1)S(1)}, f32[256,256]{1,0:T(8,128)S(1)}, bf16[288,256]{1,0:T(8,128)(2,1)S(1)}, bf16[256,512]{1,0:T(8,128)(2,1)S(1)}, bf...) custom-call(bf16[800,256]{1,0:T(8,128)(2,1)S(1)} %copy-done, ...), custom_call_target="tpu_custom_call" | custom-call | tf_op jit(solution)/shard_map/state/pallas_call | solution.py:484
  25.4 1.7 %collective-permute-start.3 = (bf16[288,256]{1,0:T(8,128)(2,1)S(1)}, bf16[288,256]{1,0:T(8,128)(2,1)S(1)}, u32[]{:S(2)}, u32[]{:S(2)}) collective-permute-start(bf16[288,256]{1,0:T(8,128)(2,1)S(1)} %get-tuple-element.49.refs_0_.refs_6_), channel_id=1, source_target_pairs={{0,8},{8,0},{16,24},{24,16},{1,9},{9,1},{17,25},{25,17},{2,10},{10... | collective-permute-start | bytes 442376 | tf_op jit(solution)/shard_map/ppermute | solution.py:502
  27.1 1.4 %state.3 = (bf16[288,256]{1,0:T(8,128)(2,1)S(1)}, bf16[256,512]{1,0:T(8,128)(2,1)S(1)}, bf16[256,512]{1,0:T(8,128)(2,1)S(1)}, f32[8,256]{1,0:T(8,128)S(1)}, f32[256,8]{1,0:T(8,128)S(1)}) custom-call(bf16[256,256]{1,0:T(8,128)(2,1)S(1)} %get-tuple-element.50.refs_0_.refs_1_, bf16[800,256]{1,0:T(8,128)(2,1)S(1)} %copy-done, ...), custom_call_target="tpu_custom_call" | custom-call | tf_op jit(solution)/shard_map/state/pallas_call | solution.py:484
  29.0 1.0 %collective-permute-start.5 = (bf16[288,256]{1,0:T(8,128)(2,1)S(1)}, bf16[288,256]{1,0:T(8,128)(2,1)S(1)}, u32[]{:S(2)}, u32[]{:S(2)}) collective-permute-start(bf16[288,256]{1,0:T(8,128)(2,1)S(1)} %get-tuple-element.52.refs_0_.refs_6_), channel_id=1, source_target_pairs={{0,8},{8,0},{16,24},{24,16},{1,9},{9,1},{17,25},{25,17},{2,10},{10... | collective-permute-start | bytes 442376 | tf_op jit(solution)/shard_map/ppermute | solution.py:502
  30.1 1.4 %collective-permute-done.3.refs_1_.refs_7_ = bf16[288,256]{1,0:T(8,128)(2,1)S(1)} collective-permute-done((bf16[288,256]{1,0:T(8,128)(2,1)S(1)}, bf16[288,256]{1,0:T(8,128)(2,1)S(1)}, u32[]{:S(2)}, u32[]{:S(2)}) %collective-permute-start.3) | collective-permute-done | bytes 147488 | tf_op jit(solution)/shard_map/ppermute | solution.py:502
  31.5 1.0 %collective-permute-start.9 = (bf16[288,256]{1,0:T(8,128)(2,1)S(1)}, bf16[288,256]{1,0:T(8,128)(2,1)S(1)}, u32[]{:S(2)}, u32[]{:S(2)}) collective-permute-start(bf16[288,256]{1,0:T(8,128)(2,1)S(1)} %combine.2.refs_6_.refs_2_.refs_3_), channel_id=1, source_target_pairs={{0,16},{8,24},{16,0},{24,8},{1,17},{9,25},{17,1},{25,9},{2,18},{10... | collective-permute-start | bytes 442376 | tf_op jit(solution)/shard_map/ppermute | solution.py:502
  34.0 1.4 %collective-permute-done.5.refs_1_.refs_7_ = bf16[288,256]{1,0:T(8,128)(2,1)S(1)} collective-permute-done((bf16[288,256]{1,0:T(8,128)(2,1)S(1)}, bf16[288,256]{1,0:T(8,128)(2,1)S(1)}, u32[]{:S(2)}, u32[]{:S(2)}) %collective-permute-start.5) | collective-permute-done | bytes 147488 | tf_op jit(solution)/shard_map/ppermute | solution.py:502
  35.4 1.3 %collective-permute-start.7 = (bf16[288,256]{1,0:T(8,128)(2,1)S(1)}, bf16[288,256]{1,0:T(8,128)(2,1)S(1)}, u32[]{:S(2)}, u32[]{:S(2)}) collective-permute-start(bf16[288,256]{1,0:T(8,128)(2,1)S(1)} %combine.3.refs_4_), channel_id=1, source_target_pairs={{0,16},{8,24},{16,0},{24,8},{1,17},{9,25},{17,1},{25,9},{2,18},{10... | collective-permute-start | bytes 442376 | tf_op jit(solution)/shard_map/ppermute | solution.py:502
  36.7 4.8 %z_own.1 = (bf16[1024,256]{1,0:T(8,128)(2,1)S(1)}, bf16[512,4096]{1,0:T(8,128)(2,1)S(1)}) custom-call(bf16[256,4096]{1,0:T(8,128)(2,1)S(1)} %get-tuple-element.44.refs_0_, bf16[4096,2048]{1,0:T(8,128)(2,1)} %refs_1_.7, bf16[2048,4096]{1,0:T(8,128)(2,1)} %refs_0_.7, bf16[288,256]{1,0:T(8,128)(2,1)S(1)} %combine.2.refs_6_.refs_2_.refs_3_, ...), custom_call_target="tpu_custom_call" | custom-call | tf_op jit(solution)/shard_map/z_own/pallas_call | solution.py:484
  41.5 1.2 %collective-permute-done.9.refs_8_ = bf16[288,256]{1,0:T(8,128)(2,1)S(1)} collective-permute-done((bf16[288,256]{1,0:T(8,128)(2,1)S(1)}, bf16[288,256]{1,0:T(8,128)(2,1)S(1)}, u32[]{:S(2)}, u32[]{:S(2)}) %collective-permute-start.9) | collective-permute-done | bytes 147488 | tf_op jit(solution)/shard_map/ppermute | solution.py:502
  43.6 1.1 %collective-permute-start.11 = (bf16[512,256]{1,0:T(8,128)(2,1)S(1)}, bf16[512,256]{1,0:T(8,128)(2,1)S(1)}, u32[]{:S(2)}, u32[]{:S(2)}) collective-permute-start(bf16[512,256]{1,0:T(8,128)(2,1)S(1)} %gate.3.refs_4_), channel_id=1, source_target_pairs={{0,4},{4,0},{1,5},{5,1},{2,6},{6,2},{3,7},{7,3},{8,12},{12,8},{9,1... | collective-permute-start | bytes 786440 | tf_op jit(solution)/shard_map/ppermute | solution.py:502
  44.7 0.9 %collective-permute-done.7.refs_8_ = bf16[288,256]{1,0:T(8,128)(2,1)S(1)} collective-permute-done((bf16[288,256]{1,0:T(8,128)(2,1)S(1)}, bf16[288,256]{1,0:T(8,128)(2,1)S(1)}, u32[]{:S(2)}, u32[]{:S(2)}) %collective-permute-start.7) | collective-permute-done | bytes 147488 | tf_op jit(solution)/shard_map/ppermute | solution.py:502
  47.2 1.3 %collective-permute-start.15 = (bf16[256,256]{1,0:T(8,128)(2,1)S(1)}, bf16[256,256]{1,0:T(8,128)(2,1)S(1)}, u32[]{:S(2)}, u32[]{:S(2)}) collective-permute-start(bf16[256,256]{1,0:T(8,128)(2,1)S(1)} %get-tuple-element.67.refs_3_), channel_id=1, source_target_pairs={{0,4},{4,0},{1,5},{5,1},{2,6},{6,2},{3,7},{7,3},{8,12},{12,8},{9,1... | collective-permute-start | bytes 393224 | tf_op jit(solution)/shard_map/ppermute | solution.py:502
  48.5 4.8 %out_own.1 = (f32[256,4096]{1,0:T(8,128)S(1)}, bf16[1024,4096]{1,0:T(8,128)(2,1)S(1)}) custom-call(bf16[2048,4096]{1,0:T(8,128)(2,1)} %refs_0_.7, bf16[512,4096]{1,0:T(8,128)(2,1)S(1)} %get-tuple-element.62.refs_1_, bf16[256,256]{1,0:T(8,128)(2,1)S(1)} %get-tuple-element.66.refs_2_, bf16[256,256]{1,0:T(8,128)(2,1)S(1)} %get-tuple-element.67.refs_3_, ...), custom_call_target="tpu_custom_call" | custom-call | tf_op jit(solution)/shard_map/out_own/pallas_call | solution.py:484
  58.4 1.5 %collective-permute-start.17 = (bf16[128,1024]{1,0:T(8,128)(2,1)S(1)}, bf16[128,1024]{1,0:T(8,128)(2,1)S(1)}, u32[]{:S(2)}, u32[]{:S(2)}) collective-permute-start(bf16[128,1024]{1,0:T(8,128)(2,1)S(1)} %add_convert_fusion), channel_id=1, source_target_pairs={{0,2},{1,3},{2,0},{3,1},{4,6},{5,7},{6,4},{7,5},{8,10},{9,11},{10,... | collective-permute-start | bytes 786440 | tf_op jit(solution)/shard_map/ppermute | solution.py:502
  60.6 7.0 %collective-permute-done.17.refs_3_ = bf16[128,1024]{1,0:T(8,128)(2,1)S(1)} collective-permute-done((bf16[128,1024]{1,0:T(8,128)(2,1)S(1)}, bf16[128,1024]{1,0:T(8,128)(2,1)S(1)}, u32[]{:S(2)}, u32[]{:S(2)}) %collective-permute-start.17) | collective-permute-done | bytes 262176 | tf_op jit(solution)/shard_map/ppermute | solution.py:502
  67.6 4.7 %collective-permute-done.13.refs_0_ = bf16[128,1024]{1,0:T(8,128)(2,1)S(1)} collective-permute-done((bf16[128,1024]{1,0:T(8,128)(2,1)S(1)}, bf16[128,1024]{1,0:T(8,128)(2,1)S(1)}, u32[]{:S(2)}, u32[]{:S(2)}) %collective-permute-start.13) | collective-permute-done | bytes 262176 | tf_op jit(solution)/shard_map/ppermute | solution.py:502
  72.4 1.0 %final.1 = bf16[256,1024]{1,0:T(8,128)(2,1)} custom-call(bf16[128,1024]{1,0:T(8,128)(2,1)S(1)} %collective-permute-done.13.refs_0_, bf16[128,1024]{1,0:T(8,128)(2,1)S(1)} %get-tuple-element.73.refs_4_.refs_1_, bf16[128,1024]{1,0:T(8,128)(2,1)S(1)} %collective-permute-done.14.refs_2_, bf16[128,1024]{1,0:T(8,128)(2,1)S(1)} %collective-permute-done.17.refs_3_, ...), custom_call_target="tpu_custom_call" | custom-call | tf_op jit(solution)/shard_map/final/pallas_call | solution.py:484
  (48 shorter events, 10.5 us)
Async XLA Ops:
  5.0 18.7 %collective-permute-start = (bf16[800,256]{1,0:T(8,128)(2,1)}, bf16[800,256]{1,0:T(8,128)(2,1)S(1)}, u32[]{:S(2)}, u32[]{:S(2)}) collective-permute-start(bf16[800,256]{1,0:T(8,128)(2,1)} %get-tuple-element.45.refs_0_.refs_1_), channel_id=1, source_target_pairs={{0,4},{4,0},{1,5},{5,1},{2,6},{6,2},{3,7},{7,3},{8,12},{12,8},{9,1... | collective-permute-start | bytes 1228808 | tf_op jit(solution)/shard_map/ppermute | solution.py:502
  14.2 12.9 %collective-permute-start.4 = (bf16[512,256]{1,0:T(8,128)(2,1)S(1)}, bf16[512,256]{1,0:T(8,128)(2,1)S(1)}, u32[]{:S(2)}, u32[]{:S(2)}) collective-permute-start(bf16[512,256]{1,0:T(8,128)(2,1)S(1)} %get-tuple-element.51), channel_id=1, source_target_pairs={{0,4},{4,0},{1,5},{5,1},{2,6},{6,2},{3,7},{7,3},{8,12},{12,8},{9,1... | collective-permute-start | bytes 786440 | tf_op jit(solution)/shard_map/ppermute | solution.py:502
  14.3 9.5 %collective-permute-start.2 = (bf16[80,256]{1,0:T(8,128)(2,1)S(1)}, bf16[80,256]{1,0:T(8,128)(2,1)S(1)}, u32[]{:S(2)}, u32[]{:S(2)}) collective-permute-start(bf16[80,256]{1,0:T(8,128)(2,1)S(1)} %get-tuple-element.43.refs_2_), channel_id=1, source_target_pairs={{0,8},{8,16},{16,24},{24,0},{1,9},{9,17},{17,25},{25,1},{2,10},{10... | collective-permute-start | bytes 122888 | tf_op jit(solution)/shard_map/ppermute | solution.py:568
  16.4 7.4 %copy-start.1 = (f32[2048,4]{0,1:T(4,128)S(1)}, f32[2048,4]{0,1:T(4,128)}, u32[]{:S(2)}) copy-start(f32[2048,4]{0,1:T(4,128)} %param.20) | copy-start | bytes 98308
  16.4 7.4 %copy-start.3 = (f32[256,4]{0,1:T(4,128)S(1)}, f32[256,4]{0,1:T(4,128)}, u32[]{:S(2)}) copy-start(f32[256,4]{0,1:T(4,128)} %param.21) | copy-start | bytes 12292
  16.4 7.4 %copy-start.5 = (f32[32]{0:T(128)S(1)}, f32[32]{0:T(128)}, u32[]{:S(2)}) copy-start(f32[32]{0:T(128)} %param.17) | copy-start | bytes 388
  16.4 7.4 %copy-start.6 = (f32[32]{0:T(128)S(1)}, f32[32]{0:T(128)}, u32[]{:S(2)}) copy-start(f32[32]{0:T(128)} %param.18) | copy-start | bytes 388
  16.4 7.4 %collective-permute-start.1 = (bf16[80,256]{1,0:T(8,128)(2,1)S(1)}, bf16[80,256]{1,0:T(8,128)(2,1)S(1)}, u32[]{:S(2)}, u32[]{:S(2)}) collective-permute-start(bf16[80,256]{1,0:T(8,128)(2,1)S(1)} %get-tuple-element.47), channel_id=1, source_target_pairs={{0,12},{4,8},{8,20},{12,16},{16,28},{20,24},{24,4},{28,0},{1,13},{... | collective-permute-start | bytes 122888 | tf_op jit(solution)/shard_map/ppermute | solution.py:565
  23.7 9.0 %copy-start.4 = (f32[32]{0:T(128)S(1)}, f32[32]{0:T(128)}, u32[]{:S(2)}) copy-start(f32[32]{0:T(128)} %param.19) | copy-start | bytes 388
  25.4 6.1 %collective-permute-start.3 = (bf16[288,256]{1,0:T(8,128)(2,1)S(1)}, bf16[288,256]{1,0:T(8,128)(2,1)S(1)}, u32[]{:S(2)}, u32[]{:S(2)}) collective-permute-start(bf16[288,256]{1,0:T(8,128)(2,1)S(1)} %get-tuple-element.49.refs_0_.refs_6_), channel_id=1, source_target_pairs={{0,8},{8,0},{16,24},{24,16},{1,9},{9,1},{17,25},{25,17},{2,10},{10... | collective-permute-start | bytes 442376 | tf_op jit(solution)/shard_map/ppermute | solution.py:502
  28.4 13.1 %collective-permute-start.8 = (bf16[512,256]{1,0:T(8,128)(2,1)S(1)}, bf16[512,256]{1,0:T(8,128)(2,1)S(1)}, u32[]{:S(2)}, u32[]{:S(2)}) collective-permute-start(bf16[512,256]{1,0:T(8,128)(2,1)S(1)} %get-tuple-element.68.refs_10_.refs_11_), channel_id=1, source_target_pairs={{0,4},{4,0},{1,5},{5,1},{2,6},{6,2},{3,7},{7,3},{8,12},{12,8},{9,1... | collective-permute-start | bytes 786440 | tf_op jit(solution)/shard_map/ppermute | solution.py:502
  29.0 6.3 %collective-permute-start.5 = (bf16[288,256]{1,0:T(8,128)(2,1)S(1)}, bf16[288,256]{1,0:T(8,128)(2,1)S(1)}, u32[]{:S(2)}, u32[]{:S(2)}) collective-permute-start(bf16[288,256]{1,0:T(8,128)(2,1)S(1)} %get-tuple-element.52.refs_0_.refs_6_), channel_id=1, source_target_pairs={{0,8},{8,0},{16,24},{24,16},{1,9},{9,1},{17,25},{25,17},{2,10},{10... | collective-permute-start | bytes 442376 | tf_op jit(solution)/shard_map/ppermute | solution.py:502
  31.5 11.2 %collective-permute-start.9 = (bf16[288,256]{1,0:T(8,128)(2,1)S(1)}, bf16[288,256]{1,0:T(8,128)(2,1)S(1)}, u32[]{:S(2)}, u32[]{:S(2)}) collective-permute-start(bf16[288,256]{1,0:T(8,128)(2,1)S(1)} %combine.2.refs_6_.refs_2_.refs_3_), channel_id=1, source_target_pairs={{0,16},{8,24},{16,0},{24,8},{1,17},{9,25},{17,1},{25,9},{2,18},{10... | collective-permute-start | bytes 442376 | tf_op jit(solution)/shard_map/ppermute | solution.py:502
  32.6 12.1 %collective-permute-start.6 = (bf16[512,256]{1,0:T(8,128)(2,1)S(1)}, bf16[512,256]{1,0:T(8,128)(2,1)S(1)}, u32[]{:S(2)}, u32[]{:S(2)}) collective-permute-start(bf16[512,256]{1,0:T(8,128)(2,1)S(1)} %get-tuple-element.65), channel_id=1, source_target_pairs={{0,4},{4,0},{1,5},{5,1},{2,6},{6,2},{3,7},{7,3},{8,12},{12,8},{9,1... | collective-permute-start | bytes 786440 | tf_op jit(solution)/shard_map/ppermute | solution.py:502
  35.4 10.1 %collective-permute-start.7 = (bf16[288,256]{1,0:T(8,128)(2,1)S(1)}, bf16[288,256]{1,0:T(8,128)(2,1)S(1)}, u32[]{:S(2)}, u32[]{:S(2)}) collective-permute-start(bf16[288,256]{1,0:T(8,128)(2,1)S(1)} %combine.3.refs_4_), channel_id=1, source_target_pairs={{0,16},{8,24},{16,0},{24,8},{1,17},{9,25},{17,1},{25,9},{2,18},{10... | collective-permute-start | bytes 442376 | tf_op jit(solution)/shard_map/ppermute | solution.py:502
  43.6 10.4 %collective-permute-start.11 = (bf16[512,256]{1,0:T(8,128)(2,1)S(1)}, bf16[512,256]{1,0:T(8,128)(2,1)S(1)}, u32[]{:S(2)}, u32[]{:S(2)}) collective-permute-start(bf16[512,256]{1,0:T(8,128)(2,1)S(1)} %gate.3.refs_4_), channel_id=1, source_target_pairs={{0,4},{4,0},{1,5},{5,1},{2,6},{6,2},{3,7},{7,3},{8,12},{12,8},{9,1... | collective-permute-start | bytes 786440 | tf_op jit(solution)/shard_map/ppermute | solution.py:502
  46.4 7.6 %collective-permute-start.10 = (bf16[256,256]{1,0:T(8,128)(2,1)S(1)}, bf16[256,256]{1,0:T(8,128)(2,1)S(1)}, u32[]{:S(2)}, u32[]{:S(2)}) collective-permute-start(bf16[256,256]{1,0:T(8,128)(2,1)S(1)} %get-tuple-element.66.refs_2_), channel_id=1, source_target_pairs={{0,4},{4,0},{1,5},{5,1},{2,6},{6,2},{3,7},{7,3},{8,12},{12,8},{9,1... | collective-permute-start | bytes 393224 | tf_op jit(solution)/shard_map/ppermute | solution.py:502
  47.2 8.4 %collective-permute-start.15 = (bf16[256,256]{1,0:T(8,128)(2,1)S(1)}, bf16[256,256]{1,0:T(8,128)(2,1)S(1)}, u32[]{:S(2)}, u32[]{:S(2)}) collective-permute-start(bf16[256,256]{1,0:T(8,128)(2,1)S(1)} %get-tuple-element.67.refs_3_), channel_id=1, source_target_pairs={{0,4},{4,0},{1,5},{5,1},{2,6},{6,2},{3,7},{7,3},{8,12},{12,8},{9,1... | collective-permute-start | bytes 393224 | tf_op jit(solution)/shard_map/ppermute | solution.py:502
  56.4 1.9 %collective-permute-start.16 = (bf16[128,1024]{1,0:T(8,128)(2,1)S(1)}, bf16[128,1024]{1,0:T(8,128)(2,1)S(1)}, u32[]{:S(2)}, u32[]{:S(2)}) collective-permute-start(bf16[128,1024]{1,0:T(8,128)(2,1)S(1)} %get-tuple-element.76), channel_id=1, source_target_pairs={{0,1},{1,0},{2,3},{3,2},{4,5},{5,4},{6,7},{7,6},{8,9},{9,8},{10,11... | collective-permute-start | bytes 786440 | tf_op jit(solution)/shard_map/ppermute | solution.py:502
  56.5 3.4 %collective-permute-start.12 = (bf16[128,1024]{1,0:T(8,128)(2,1)S(1)}, bf16[128,1024]{1,0:T(8,128)(2,1)S(1)}, u32[]{:S(2)}, u32[]{:S(2)}) collective-permute-start(bf16[128,1024]{1,0:T(8,128)(2,1)S(1)} %get-tuple-element.72), channel_id=1, source_target_pairs={{0,1},{1,0},{2,3},{3,2},{4,5},{5,4},{6,7},{7,6},{8,9},{9,8},{10,11... | collective-permute-start | bytes 786440 | tf_op jit(solution)/shard_map/ppermute | solution.py:502
  57.7 2.9 %collective-permute-start.18 = (bf16[128,1024]{1,0:T(8,128)(2,1)S(1)}, bf16[128,1024]{1,0:T(8,128)(2,1)S(1)}, u32[]{:S(2)}, u32[]{:S(2)}) collective-permute-start(bf16[128,1024]{1,0:T(8,128)(2,1)S(1)} %get-tuple-element.78), channel_id=1, source_target_pairs={{0,1},{1,0},{2,3},{3,2},{4,5},{5,4},{6,7},{7,6},{8,9},{9,8},{10,11... | collective-permute-start | bytes 786440 | tf_op jit(solution)/shard_map/ppermute | solution.py:502
  57.9 2.7 %collective-permute-start.14 = (bf16[128,1024]{1,0:T(8,128)(2,1)S(1)}, bf16[128,1024]{1,0:T(8,128)(2,1)S(1)}, u32[]{:S(2)}, u32[]{:S(2)}) collective-permute-start(bf16[128,1024]{1,0:T(8,128)(2,1)S(1)} %get-tuple-element.74), channel_id=1, source_target_pairs={{0,1},{1,0},{2,3},{3,2},{4,5},{5,4},{6,7},{7,6},{8,9},{9,8},{10,11... | collective-permute-start | bytes 786440 | tf_op jit(solution)/shard_map/ppermute | solution.py:502
  58.4 9.2 %collective-permute-start.17 = (bf16[128,1024]{1,0:T(8,128)(2,1)S(1)}, bf16[128,1024]{1,0:T(8,128)(2,1)S(1)}, u32[]{:S(2)}, u32[]{:S(2)}) collective-permute-start(bf16[128,1024]{1,0:T(8,128)(2,1)S(1)} %add_convert_fusion), channel_id=1, source_target_pairs={{0,2},{1,3},{2,0},{3,1},{4,6},{5,7},{6,4},{7,5},{8,10},{9,11},{10,... | collective-permute-start | bytes 786440 | tf_op jit(solution)/shard_map/ppermute | solution.py:502
  60.0 12.4 %collective-permute-start.13 = (bf16[128,1024]{1,0:T(8,128)(2,1)S(1)}, bf16[128,1024]{1,0:T(8,128)(2,1)S(1)}, u32[]{:S(2)}, u32[]{:S(2)}) collective-permute-start(bf16[128,1024]{1,0:T(8,128)(2,1)S(1)} %add_convert_fusion.1), channel_id=1, source_target_pairs={{0,2},{1,3},{2,0},{3,1},{4,6},{5,7},{6,4},{7,5},{8,10},{9,11},{10,... | collective-permute-start | bytes 786440 | tf_op jit(solution)/shard_map/ppermute | solution.py:502
  (2 other events, 13.4 us)

commit v5 on v4

--- a/solution.py
+++ b/solution.py
@@ -67,15 +67,25 @@
     return running
 
 
-def prefix(messages, here, state_dim):
-    def parts(message):
-        return message[:state_dim].astype(f32), message[state_dim : state_dim + 1].astype(f32)
-
-    state, decay = parts(messages[0])
+def block_of(message, block, blocks, state_dim):
+    decays = message[blocks * state_dim :, :].astype(f32)
+    state = message[block * state_dim : (block + 1) * state_dim, :].astype(f32)
+    return state, decays[block : block + 1]
+
+
+def decay_rows(decays):
+    row = lax.broadcasted_iota(jnp.int32, (HALO, decays[0].shape[1]), 0)
+    rows = jnp.zeros((HALO, decays[0].shape[1]), f32)
+    for j, decay in enumerate(decays):
+        rows = jnp.where(row == j, decay, rows)
+    return rows.astype(bf16)
+
+
+def prefix(messages, here):
+    state, decay = messages[0]
     enter = jnp.zeros_like(state)
     reach = jnp.ones_like(decay)
-    for step, message in enumerate(messages[1:]):
-        their_state, their_decay = parts(message)
+    for step, (their_state, their_decay) in enumerate(messages[1:]):
         later = ((here >> step) & 1) == 1
         enter = jnp.where(later, enter + reach * their_state, enter)
         reach = jnp.where(later, reach * their_decay, reach)
@@ -303,7 +313,6 @@
     dt_wide = spread(dt_now, head_dim)
     tail_wide = spread(dt_now * jnp.exp(last - cum), head_dim)
     through = spread(jnp.exp(jnp.broadcast_to(last, (heads, HALO))), head_dim)
-    rows = state_dim + HALO
     x_low = x_theirs.shape[0] - blocks * toks
     taps_low = (row * chunks + chunk) * blocks * lanes
     for j in range(blocks):
@@ -317,18 +326,23 @@
         conv_out[:, cols] = x_now.astype(bf16)
         scaled[:, cols] = (x_now * dt_wide[:, cols]).astype(bf16)
         state = mm_tn(b_now, (x_now * tail_wide[:, cols]).astype(bf16))
-        msg[j * rows : j * rows + state_dim, :] = state.astype(bf16)
-        msg[j * rows + state_dim : (j + 1) * rows, :] = through[:, cols].astype(bf16)
-
-
-def combine_kernel(*refs, state_dim, lanes):
+        msg[j * state_dim : (j + 1) * state_dim, :] = state.astype(bf16)
+    msg[blocks * state_dim :, :] = decay_rows(
+        [through[:1, j * lanes : (j + 1) * lanes] for j in range(blocks)]
+    )
+
+
+def combine_kernel(*refs, state_dim):
     *messages, out = refs
-    rows = state_dim + HALO
-    for j in range(out.shape[0] // rows):
-        now = [m[j * rows : (j + 1) * rows, :] for m in messages]
-        _, state, decay = prefix(now, place()[2], state_dim)
-        out[j * rows : j * rows + state_dim, :] = state.astype(bf16)
-        out[j * rows + state_dim : (j + 1) * rows, :] = jnp.broadcast_to(decay, (HALO, lanes)).astype(bf16)
+    here = place()[2]
+    blocks = out.shape[0] // state_dim
+    decays = []
+    for j in range(blocks):
+        now = [block_of(m, j, blocks, state_dim) for m in messages]
+        _, state, decay = prefix(now, here)
+        out[j * state_dim : (j + 1) * state_dim, :] = state.astype(bf16)
+        decays.append(decay)
+    out[blocks * state_dim :, :] = decay_rows(decays)
 
 
 def within(where, scores, scaled, conv_out, cum, cum_t, skip, out, *, head_dim, first_of, local_heads):
@@ -365,7 +379,7 @@
     toks = inner.shape[0]
     row, _, here = place()
     gain_low = (row * chunks + chunk) * inner.shape[1]
-    rows = state_dim + HALO
+    blocks = inner.shape[1] // lanes
     grown = spread(jnp.exp(cum[...]), head_dim)
     c_now = bc[:, state_dim:]
     wide = 2 * head_dim
@@ -374,9 +388,8 @@
         lax.broadcasted_iota(jnp.int32, shape, 1) // head_dim
     )
     mean_of = jnp.where(same, 1.0 / head_dim, 0.0).astype(bf16)
-    for j in range(inner.shape[1] // lanes):
-        now = [m[j * rows : (j + 1) * rows, :] for m in messages]
-        enter, _, _ = prefix(now, here, state_dim)
+    for j in range(blocks):
+        enter, _, _ = prefix([block_of(m, j, blocks, state_dim) for m in messages], here)
         cols = slice(j * lanes, (j + 1) * lanes)
         scanned = inner[:, cols] + grown[:, cols] * mm(c_now, enter.astype(bf16))
         z_low = (chunk * inner.shape[1] // lanes + j) * toks
@@ -581,7 +594,6 @@
         after=(edge_own,),
     )
 
-    rows = state_dim + HALO
     sizes = dict(head_dim=head_dim, state_dim=state_dim, lanes=lanes)
     states, scans = [], []
     bc_now = scores = None
@@ -593,7 +605,7 @@
         ]
         outs = [sds(toks, lanes), sds(toks, toks, dtype=f32)] if c == 0 else []
         outs += [
-            sds(blocks * rows, lanes),
+            sds(blocks * state_dim + HALO, lanes),
             sds(toks, width),
             sds(toks, width),
             sds(chunk_heads, toks, dtype=f32),
@@ -638,7 +650,7 @@
         while by < ctx_size:
             if by > 1:
                 (send,) = call(
-                    functools.partial(combine_kernel, state_dim=state_dim, lanes=lanes),
+                    functools.partial(combine_kernel, state_dim=state_dim),
                     heard, None, [sds(*send.shape)], name="combine", after=(*sent, *inners),
                 )
             heard.append(swapped(send, "ctx", by))

time: 73.5 us -> 73.3 us (level)
  transfers between devices with their start and end apart: 19 -> 19, of which waited for: 8 -> 7; matrix products, arithmetic and copies ran while one was open for 0% -> 0% of each run, Pallas kernels for 39% -> 39%
where the time goes in v5:
time: 73.3 us; the launch traced here: 73.2 us
  Pallas kernels  35.4 us (48%)
  starting transfers between devices  20.2 us (28%)
  waiting for transfers between devices  17.2 us (23%)
    pallas_call x18, Pallas kernels, call(): pl.pallas_call(body, in_specs=[*(specs or [IN_VMEM] * used), *[pl.BlockSp...  35.4 us
    ppermute x17, waiting for transfers between devices, swapped(): return lax.ppermute(shard, axis, [(i, i ^ by) for i in range(devices)])  17.2 us
    ppermute x17, starting transfers between devices, swapped(): return lax.ppermute(shard, axis, [(i, i ^ by) for i in range(devices)])  15.4 us
    ppermute x1, starting transfers between devices, fast(): lax.ppermute(edge_other, ('ctx', 'row'), [(2 * i + s, 2 * j + 1 - s) for...  2.72 us
    ppermute x1, starting transfers between devices, fast(): edge_b = lax.ppermute(edge_own, 'ctx', down)  2.09 us
  transfers between devices with their start and end apart: 19, of which 7 were waited for; matrix products, arithmetic and copies ran while one was open for 0% of the time, Pallas kernels for 39%

profile of v5, /device:TPU:0, one launch (start us, length us, event | category | flops | bytes accessed | tf_op | source)
XLA Modules:
  0.0 73.2 jit_solution(9056506630418332659)
XLA Ops:
  0.0 5.0 %first.1 = (bf16[800,256]{1,0:T(8,128)(2,1)}, bf16[48,256]{1,0:T(8,128)(2,1)S(1)}) custom-call(bf16[256,4096]{1,0:T(8,128)(2,1)} %refs_0_.6, bf16[4096,2048]{1,0:T(8,128)(2,1)} %refs_1_.5, bf16[4096,256]{1,0:T(8,128)(2,1)} %refs_2_.2, bf16[32,4096]{1,0:T(8,128)(2,1)} %bitcast.19), custom_call_target="tpu_custom_call" | custom-call | tf_op jit(solution)/shard_map/first/pallas_call | solution.py:497
  5.0 3.0 %collective-permute-start = (bf16[800,256]{1,0:T(8,128)(2,1)}, bf16[800,256]{1,0:T(8,128)(2,1)S(1)}, u32[]{:S(2)}, u32[]{:S(2)}) collective-permute-start(bf16[800,256]{1,0:T(8,128)(2,1)} %get-tuple-element.45.refs_0_.refs_1_), channel_id=1, source_target_pairs={{0,4},{4,0},{1,5},{5,1},{2,6},{6,2},{3,7},{7,3},{8,12},{12,8},{9,1... | collective-permute-start | bytes 1228808 | tf_op jit(solution)/shard_map/ppermute | solution.py:515
  8.0 6.1 %second.1 = (bf16[512,256]{1,0:T(8,128)(2,1)S(1)}, bf16[1024,256]{1,0:T(8,128)(2,1)S(1)}, bf16[80,256]{1,0:T(8,128)(2,1)S(1)}, bf16[80,256]{1,0:T(8,128)(2,1)S(1)}) custom-call(bf16[256,4096]{1,0:T(8,128)(2,1)} %refs_0_.6, bf16[4096,2048]{1,0:T(8,128)(2,1)} %refs_1_.5, bf16[48,256]{1,0:T(8,128)(2,1)S(1)} %get-tuple-element.42.refs_2_), custom_call_target="tpu_custom_call" | custom-call | tf_op jit(solution)/shard_map/second/pallas_call | solution.py:497
  14.3 2.1 %collective-permute-start.2 = (bf16[80,256]{1,0:T(8,128)(2,1)S(1)}, bf16[80,256]{1,0:T(8,128)(2,1)S(1)}, u32[]{:S(2)}, u32[]{:S(2)}) collective-permute-start(bf16[80,256]{1,0:T(8,128)(2,1)S(1)} %get-tuple-element.43.refs_2_), channel_id=1, source_target_pairs={{0,8},{8,16},{16,24},{24,0},{1,9},{9,17},{17,25},{25,1},{2,10},{10... | collective-permute-start | bytes 122888 | tf_op jit(solution)/shard_map/ppermute | solution.py:581
  16.4 2.7 %collective-permute-start.1 = (bf16[80,256]{1,0:T(8,128)(2,1)S(1)}, bf16[80,256]{1,0:T(8,128)(2,1)S(1)}, u32[]{:S(2)}, u32[]{:S(2)}) collective-permute-start(bf16[80,256]{1,0:T(8,128)(2,1)S(1)} %get-tuple-element.47), channel_id=1, source_target_pairs={{0,12},{4,8},{8,20},{12,16},{16,28},{20,24},{24,4},{28,0},{1,13},{... | collective-permute-start | bytes 122888 | tf_op jit(solution)/shard_map/ppermute | solution.py:578
  19.1 4.6 %z_other.1 = (bf16[512,256]{1,0:T(8,128)(2,1)S(1)}, bf16[512,256]{1,0:T(8,128)(2,1)S(1)}, bf16[256,4096]{1,0:T(8,128)(2,1)S(1)}) custom-call(bf16[256,4096]{1,0:T(8,128)(2,1)} %refs_0_.6, bf16[4096,2048]{1,0:T(8,128)(2,1)} %refs_1_.7, bf16[80,256]{1,0:T(8,128)(2,1)S(1)} %get-tuple-element.43.refs_2_), custom_call_target="tpu_custom_call" | custom-call | tf_op jit(solution)/shard_map/z_other/pallas_call | solution.py:497
  23.8 1.6 %state.2 = (bf16[256,256]{1,0:T(8,128)(2,1)S(1)}, f32[256,256]{1,0:T(8,128)S(1)}, bf16[272,256]{1,0:T(8,128)(2,1)S(1)}, bf16[256,512]{1,0:T(8,128)(2,1)S(1)}, bf...) custom-call(bf16[800,256]{1,0:T(8,128)(2,1)S(1)} %copy-done, ...), custom_call_target="tpu_custom_call" | custom-call | tf_op jit(solution)/shard_map/state/pallas_call | solution.py:497
  25.4 1.7 %collective-permute-start.3 = (bf16[272,256]{1,0:T(8,128)(2,1)S(1)}, bf16[272,256]{1,0:T(8,128)(2,1)S(1)}, u32[]{:S(2)}, u32[]{:S(2)}) collective-permute-start(bf16[272,256]{1,0:T(8,128)(2,1)S(1)} %get-tuple-element.49.refs_0_.refs_6_), channel_id=1, source_target_pairs={{0,8},{8,0},{16,24},{24,16},{1,9},{9,1},{17,25},{25,17},{2,10},{10... | collective-permute-start | bytes 417800 | tf_op jit(solution)/shard_map/ppermute | solution.py:515
  27.1 1.4 %state.3 = (bf16[272,256]{1,0:T(8,128)(2,1)S(1)}, bf16[256,512]{1,0:T(8,128)(2,1)S(1)}, bf16[256,512]{1,0:T(8,128)(2,1)S(1)}, f32[8,256]{1,0:T(8,128)S(1)}, f32[256,8]{1,0:T(8,128)S(1)}) custom-call(bf16[256,256]{1,0:T(8,128)(2,1)S(1)} %get-tuple-element.50.refs_0_.refs_1_, bf16[800,256]{1,0:T(8,128)(2,1)S(1)} %copy-done, ...), custom_call_target="tpu_custom_call" | custom-call | tf_op jit(solution)/shard_map/state/pallas_call | solution.py:497
  29.0 1.0 %collective-permute-start.5 = (bf16[272,256]{1,0:T(8,128)(2,1)S(1)}, bf16[272,256]{1,0:T(8,128)(2,1)S(1)}, u32[]{:S(2)}, u32[]{:S(2)}) collective-permute-start(bf16[272,256]{1,0:T(8,128)(2,1)S(1)} %get-tuple-element.52.refs_0_.refs_6_), channel_id=1, source_target_pairs={{0,8},{8,0},{16,24},{24,16},{1,9},{9,1},{17,25},{25,17},{2,10},{10... | collective-permute-start | bytes 417800 | tf_op jit(solution)/shard_map/ppermute | solution.py:515
  30.1 1.2 %collective-permute-done.3.refs_1_.refs_7_ = bf16[272,256]{1,0:T(8,128)(2,1)S(1)} collective-permute-done((bf16[272,256]{1,0:T(8,128)(2,1)S(1)}, bf16[272,256]{1,0:T(8,128)(2,1)S(1)}, u32[]{:S(2)}, u32[]{:S(2)}) %collective-permute-start.3) | collective-permute-done | bytes 139296 | tf_op jit(solution)/shard_map/ppermute | solution.py:515
  31.3 1.0 %collective-permute-start.9 = (bf16[272,256]{1,0:T(8,128)(2,1)S(1)}, bf16[272,256]{1,0:T(8,128)(2,1)S(1)}, u32[]{:S(2)}, u32[]{:S(2)}) collective-permute-start(bf16[272,256]{1,0:T(8,128)(2,1)S(1)} %combine.2.refs_6_.refs_2_.refs_3_), channel_id=1, source_target_pairs={{0,16},{8,24},{16,0},{24,8},{1,17},{9,25},{17,1},{25,9},{2,18},{10... | collective-permute-start | bytes 417800 | tf_op jit(solution)/shard_map/ppermute | solution.py:515
  33.8 1.2 %collective-permute-done.5.refs_1_.refs_7_ = bf16[272,256]{1,0:T(8,128)(2,1)S(1)} collective-permute-done((bf16[272,256]{1,0:T(8,128)(2,1)S(1)}, bf16[272,256]{1,0:T(8,128)(2,1)S(1)}, u32[]{:S(2)}, u32[]{:S(2)}) %collective-permute-start.5) | collective-permute-done | bytes 139296 | tf_op jit(solution)/shard_map/ppermute | solution.py:515
  35.1 1.4 %collective-permute-start.7 = (bf16[272,256]{1,0:T(8,128)(2,1)S(1)}, bf16[272,256]{1,0:T(8,128)(2,1)S(1)}, u32[]{:S(2)}, u32[]{:S(2)}) collective-permute-start(bf16[272,256]{1,0:T(8,128)(2,1)S(1)} %combine.3.refs_4_), channel_id=1, source_target_pairs={{0,16},{8,24},{16,0},{24,8},{1,17},{9,25},{17,1},{25,9},{2,18},{10... | collective-permute-start | bytes 417800 | tf_op jit(solution)/shard_map/ppermute | solution.py:515
  36.5 4.8 %z_own.1 = (bf16[1024,256]{1,0:T(8,128)(2,1)S(1)}, bf16[512,4096]{1,0:T(8,128)(2,1)S(1)}) custom-call(bf16[256,4096]{1,0:T(8,128)(2,1)S(1)} %get-tuple-element.44.refs_0_, bf16[4096,2048]{1,0:T(8,128)(2,1)} %refs_1_.7, bf16[2048,4096]{1,0:T(8,128)(2,1)} %refs_0_.7, bf16[272,256]{1,0:T(8,128)(2,1)S(1)} %combine.2.refs_6_.refs_2_.refs_3_, ...), custom_call_target="tpu_custom_call" | custom-call | tf_op jit(solution)/shard_map/z_own/pallas_call | solution.py:497
  41.3 1.1 %collective-permute-done.9.refs_8_ = bf16[272,256]{1,0:T(8,128)(2,1)S(1)} collective-permute-done((bf16[272,256]{1,0:T(8,128)(2,1)S(1)}, bf16[272,256]{1,0:T(8,128)(2,1)S(1)}, u32[]{:S(2)}, u32[]{:S(2)}) %collective-permute-start.9) | collective-permute-done | bytes 139296 | tf_op jit(solution)/shard_map/ppermute | solution.py:515
  43.2 0.9 %collective-permute-start.11 = (bf16[512,256]{1,0:T(8,128)(2,1)S(1)}, bf16[512,256]{1,0:T(8,128)(2,1)S(1)}, u32[]{:S(2)}, u32[]{:S(2)}) collective-permute-start(bf16[512,256]{1,0:T(8,128)(2,1)S(1)} %gate.3.refs_4_), channel_id=1, source_target_pairs={{0,4},{4,0},{1,5},{5,1},{2,6},{6,2},{3,7},{7,3},{8,12},{12,8},{9,1... | collective-permute-start | bytes 786440 | tf_op jit(solution)/shard_map/ppermute | solution.py:515
  46.5 1.3 %collective-permute-start.15 = (bf16[256,256]{1,0:T(8,128)(2,1)S(1)}, bf16[256,256]{1,0:T(8,128)(2,1)S(1)}, u32[]{:S(2)}, u32[]{:S(2)}) collective-permute-start(bf16[256,256]{1,0:T(8,128)(2,1)S(1)} %get-tuple-element.67.refs_3_), channel_id=1, source_target_pairs={{0,4},{4,0},{1,5},{5,1},{2,6},{6,2},{3,7},{7,3},{8,12},{12,8},{9,1... | collective-permute-start | bytes 393224 | tf_op jit(solution)/shard_map/ppermute | solution.py:515
  47.8 4.8 %out_own.1 = (f32[256,4096]{1,0:T(8,128)S(1)}, bf16[1024,4096]{1,0:T(8,128)(2,1)S(1)}) custom-call(bf16[2048,4096]{1,0:T(8,128)(2,1)} %refs_0_.7, bf16[512,4096]{1,0:T(8,128)(2,1)S(1)} %get-tuple-element.62.refs_1_, bf16[256,256]{1,0:T(8,128)(2,1)S(1)} %get-tuple-element.66.refs_2_, bf16[256,256]{1,0:T(8,128)(2,1)S(1)} %get-tuple-element.67.refs_3_, ...), custom_call_target="tpu_custom_call" | custom-call | tf_op jit(solution)/shard_map/out_own/pallas_call | solution.py:497
  52.6 1.3 %collective-permute-done.10.refs_2_ = bf16[256,256]{1,0:T(8,128)(2,1)S(1)} collective-permute-done((bf16[256,256]{1,0:T(8,128)(2,1)S(1)}, bf16[256,256]{1,0:T(8,128)(2,1)S(1)}, u32[]{:S(2)}, u32[]{:S(2)}) %collective-permute-start.10) | collective-permute-done | bytes 131104 | tf_op jit(solution)/shard_map/ppermute | solution.py:515
  58.2 1.6 %collective-permute-start.17 = (bf16[128,1024]{1,0:T(8,128)(2,1)S(1)}, bf16[128,1024]{1,0:T(8,128)(2,1)S(1)}, u32[]{:S(2)}, u32[]{:S(2)}) collective-permute-start(bf16[128,1024]{1,0:T(8,128)(2,1)S(1)} %add_convert_fusion), channel_id=1, source_target_pairs={{0,2},{1,3},{2,0},{3,1},{4,6},{5,7},{6,4},{7,5},{8,10},{9,11},{10,... | collective-permute-start | bytes 786440 | tf_op jit(solution)/shard_map/ppermute | solution.py:515
  60.5 7.0 %collective-permute-done.17.refs_3_ = bf16[128,1024]{1,0:T(8,128)(2,1)S(1)} collective-permute-done((bf16[128,1024]{1,0:T(8,128)(2,1)S(1)}, bf16[128,1024]{1,0:T(8,128)(2,1)S(1)}, u32[]{:S(2)}, u32[]{:S(2)}) %collective-permute-start.17) | collective-permute-done | bytes 262176 | tf_op jit(solution)/shard_map/ppermute | solution.py:515
  67.5 4.7 %collective-permute-done.13.refs_0_ = bf16[128,1024]{1,0:T(8,128)(2,1)S(1)} collective-permute-done((bf16[128,1024]{1,0:T(8,128)(2,1)S(1)}, bf16[128,1024]{1,0:T(8,128)(2,1)S(1)}, u32[]{:S(2)}, u32[]{:S(2)}) %collective-permute-start.13) | collective-permute-done | bytes 262176 | tf_op jit(solution)/shard_map/ppermute | solution.py:515
  72.2 1.0 %final.1 = bf16[256,1024]{1,0:T(8,128)(2,1)} custom-call(bf16[128,1024]{1,0:T(8,128)(2,1)S(1)} %collective-permute-done.13.refs_0_, bf16[128,1024]{1,0:T(8,128)(2,1)S(1)} %get-tuple-element.73.refs_4_.refs_1_, bf16[128,1024]{1,0:T(8,128)(2,1)S(1)} %collective-permute-done.14.refs_2_, bf16[128,1024]{1,0:T(8,128)(2,1)S(1)} %collective-permute-done.17.refs_3_, ...), custom_call_target="tpu_custom_call" | custom-call | tf_op jit(solution)/shard_map/final/pallas_call | solution.py:497
  (48 shorter events, 10.4 us)
Async XLA Ops:
  5.0 18.7 %collective-permute-start = (bf16[800,256]{1,0:T(8,128)(2,1)}, bf16[800,256]{1,0:T(8,128)(2,1)S(1)}, u32[]{:S(2)}, u32[]{:S(2)}) collective-permute-start(bf16[800,256]{1,0:T(8,128)(2,1)} %get-tuple-element.45.refs_0_.refs_1_), channel_id=1, source_target_pairs={{0,4},{4,0},{1,5},{5,1},{2,6},{6,2},{3,7},{7,3},{8,12},{12,8},{9,1... | collective-permute-start | bytes 1228808 | tf_op jit(solution)/shard_map/ppermute | solution.py:515
  14.2 12.9 %collective-permute-start.4 = (bf16[512,256]{1,0:T(8,128)(2,1)S(1)}, bf16[512,256]{1,0:T(8,128)(2,1)S(1)}, u32[]{:S(2)}, u32[]{:S(2)}) collective-permute-start(bf16[512,256]{1,0:T(8,128)(2,1)S(1)} %get-tuple-element.51), channel_id=1, source_target_pairs={{0,4},{4,0},{1,5},{5,1},{2,6},{6,2},{3,7},{7,3},{8,12},{12,8},{9,1... | collective-permute-start | bytes 786440 | tf_op jit(solution)/shard_map/ppermute | solution.py:515
  14.3 9.5 %collective-permute-start.2 = (bf16[80,256]{1,0:T(8,128)(2,1)S(1)}, bf16[80,256]{1,0:T(8,128)(2,1)S(1)}, u32[]{:S(2)}, u32[]{:S(2)}) collective-permute-start(bf16[80,256]{1,0:T(8,128)(2,1)S(1)} %get-tuple-element.43.refs_2_), channel_id=1, source_target_pairs={{0,8},{8,16},{16,24},{24,0},{1,9},{9,17},{17,25},{25,1},{2,10},{10... | collective-permute-start | bytes 122888 | tf_op jit(solution)/shard_map/ppermute | solution.py:581
  16.4 7.4 %copy-start.1 = (f32[2048,4]{0,1:T(4,128)S(1)}, f32[2048,4]{0,1:T(4,128)}, u32[]{:S(2)}) copy-start(f32[2048,4]{0,1:T(4,128)} %param.20) | copy-start | bytes 98308
  16.4 7.4 %copy-start.3 = (f32[256,4]{0,1:T(4,128)S(1)}, f32[256,4]{0,1:T(4,128)}, u32[]{:S(2)}) copy-start(f32[256,4]{0,1:T(4,128)} %param.21) | copy-start | bytes 12292
  16.4 7.4 %copy-start.5 = (f32[32]{0:T(128)S(1)}, f32[32]{0:T(128)}, u32[]{:S(2)}) copy-start(f32[32]{0:T(128)} %param.17) | copy-start | bytes 388
  16.4 7.4 %copy-start.6 = (f32[32]{0:T(128)S(1)}, f32[32]{0:T(128)}, u32[]{:S(2)}) copy-start(f32[32]{0:T(128)} %param.18) | copy-start | bytes 388
  16.4 7.4 %collective-permute-start.1 = (bf16[80,256]{1,0:T(8,128)(2,1)S(1)}, bf16[80,256]{1,0:T(8,128)(2,1)S(1)}, u32[]{:S(2)}, u32[]{:S(2)}) collective-permute-start(bf16[80,256]{1,0:T(8,128)(2,1)S(1)} %get-tuple-element.47), channel_id=1, source_target_pairs={{0,12},{4,8},{8,20},{12,16},{16,28},{20,24},{24,4},{28,0},{1,13},{... | collective-permute-start | bytes 122888 | tf_op jit(solution)/shard_map/ppermute | solution.py:578
  23.7 8.9 %copy-start.4 = (f32[32]{0:T(128)S(1)}, f32[32]{0:T(128)}, u32[]{:S(2)}) copy-start(f32[32]{0:T(128)} %param.19) | copy-start | bytes 388
  25.4 5.9 %collective-permute-start.3 = (bf16[272,256]{1,0:T(8,128)(2,1)S(1)}, bf16[272,256]{1,0:T(8,128)(2,1)S(1)}, u32[]{:S(2)}, u32[]{:S(2)}) collective-permute-start(bf16[272,256]{1,0:T(8,128)(2,1)S(1)} %get-tuple-element.49.refs_0_.refs_6_), channel_id=1, source_target_pairs={{0,8},{8,0},{16,24},{24,16},{1,9},{9,1},{17,25},{25,17},{2,10},{10... | collective-permute-start | bytes 417800 | tf_op jit(solution)/shard_map/ppermute | solution.py:515
  28.4 12.8 %collective-permute-start.8 = (bf16[512,256]{1,0:T(8,128)(2,1)S(1)}, bf16[512,256]{1,0:T(8,128)(2,1)S(1)}, u32[]{:S(2)}, u32[]{:S(2)}) collective-permute-start(bf16[512,256]{1,0:T(8,128)(2,1)S(1)} %get-tuple-element.68.refs_10_.refs_11_), channel_id=1, source_target_pairs={{0,4},{4,0},{1,5},{5,1},{2,6},{6,2},{3,7},{7,3},{8,12},{12,8},{9,1... | collective-permute-start | bytes 786440 | tf_op jit(solution)/shard_map/ppermute | solution.py:515
  29.0 6.0 %collective-permute-start.5 = (bf16[272,256]{1,0:T(8,128)(2,1)S(1)}, bf16[272,256]{1,0:T(8,128)(2,1)S(1)}, u32[]{:S(2)}, u32[]{:S(2)}) collective-permute-start(bf16[272,256]{1,0:T(8,128)(2,1)S(1)} %get-tuple-element.52.refs_0_.refs_6_), channel_id=1, source_target_pairs={{0,8},{8,0},{16,24},{24,16},{1,9},{9,1},{17,25},{25,17},{2,10},{10... | collective-permute-start | bytes 417800 | tf_op jit(solution)/shard_map/ppermute | solution.py:515
  31.3 11.0 %collective-permute-start.9 = (bf16[272,256]{1,0:T(8,128)(2,1)S(1)}, bf16[272,256]{1,0:T(8,128)(2,1)S(1)}, u32[]{:S(2)}, u32[]{:S(2)}) collective-permute-start(bf16[272,256]{1,0:T(8,128)(2,1)S(1)} %combine.2.refs_6_.refs_2_.refs_3_), channel_id=1, source_target_pairs={{0,16},{8,24},{16,0},{24,8},{1,17},{9,25},{17,1},{25,9},{2,18},{10... | collective-permute-start | bytes 417800 | tf_op jit(solution)/shard_map/ppermute | solution.py:515
  32.4 11.8 %collective-permute-start.6 = (bf16[512,256]{1,0:T(8,128)(2,1)S(1)}, bf16[512,256]{1,0:T(8,128)(2,1)S(1)}, u32[]{:S(2)}, u32[]{:S(2)}) collective-permute-start(bf16[512,256]{1,0:T(8,128)(2,1)S(1)} %get-tuple-element.65), channel_id=1, source_target_pairs={{0,4},{4,0},{1,5},{5,1},{2,6},{6,2},{3,7},{7,3},{8,12},{12,8},{9,1... | collective-permute-start | bytes 786440 | tf_op jit(solution)/shard_map/ppermute | solution.py:515
  35.1 9.8 %collective-permute-start.7 = (bf16[272,256]{1,0:T(8,128)(2,1)S(1)}, bf16[272,256]{1,0:T(8,128)(2,1)S(1)}, u32[]{:S(2)}, u32[]{:S(2)}) collective-permute-start(bf16[272,256]{1,0:T(8,128)(2,1)S(1)} %combine.3.refs_4_), channel_id=1, source_target_pairs={{0,16},{8,24},{16,0},{24,8},{1,17},{9,25},{17,1},{25,9},{2,18},{10... | collective-permute-start | bytes 417800 | tf_op jit(solution)/shard_map/ppermute | solution.py:515
  43.2 10.7 %collective-permute-start.11 = (bf16[512,256]{1,0:T(8,128)(2,1)S(1)}, bf16[512,256]{1,0:T(8,128)(2,1)S(1)}, u32[]{:S(2)}, u32[]{:S(2)}) collective-permute-start(bf16[512,256]{1,0:T(8,128)(2,1)S(1)} %gate.3.refs_4_), channel_id=1, source_target_pairs={{0,4},{4,0},{1,5},{5,1},{2,6},{6,2},{3,7},{7,3},{8,12},{12,8},{9,1... | collective-permute-start | bytes 786440 | tf_op jit(solution)/shard_map/ppermute | solution.py:515
  45.7 8.2 %collective-permute-start.10 = (bf16[256,256]{1,0:T(8,128)(2,1)S(1)}, bf16[256,256]{1,0:T(8,128)(2,1)S(1)}, u32[]{:S(2)}, u32[]{:S(2)}) collective-permute-start(bf16[256,256]{1,0:T(8,128)(2,1)S(1)} %get-tuple-element.66.refs_2_), channel_id=1, source_target_pairs={{0,4},{4,0},{1,5},{5,1},{2,6},{6,2},{3,7},{7,3},{8,12},{12,8},{9,1... | collective-permute-start | bytes 393224 | tf_op jit(solution)/shard_map/ppermute | solution.py:515
  46.5 9.0 %collective-permute-start.15 = (bf16[256,256]{1,0:T(8,128)(2,1)S(1)}, bf16[256,256]{1,0:T(8,128)(2,1)S(1)}, u32[]{:S(2)}, u32[]{:S(2)}) collective-permute-start(bf16[256,256]{1,0:T(8,128)(2,1)S(1)} %get-tuple-element.67.refs_3_), channel_id=1, source_target_pairs={{0,4},{4,0},{1,5},{5,1},{2,6},{6,2},{3,7},{7,3},{8,12},{12,8},{9,1... | collective-permute-start | bytes 393224 | tf_op jit(solution)/shard_map/ppermute | solution.py:515
  56.2 1.9 %collective-permute-start.16 = (bf16[128,1024]{1,0:T(8,128)(2,1)S(1)}, bf16[128,1024]{1,0:T(8,128)(2,1)S(1)}, u32[]{:S(2)}, u32[]{:S(2)}) collective-permute-start(bf16[128,1024]{1,0:T(8,128)(2,1)S(1)} %get-tuple-element.76), channel_id=1, source_target_pairs={{0,1},{1,0},{2,3},{3,2},{4,5},{5,4},{6,7},{7,6},{8,9},{9,8},{10,11... | collective-permute-start | bytes 786440 | tf_op jit(solution)/shard_map/ppermute | solution.py:515
  56.3 3.5 %collective-permute-start.12 = (bf16[128,1024]{1,0:T(8,128)(2,1)S(1)}, bf16[128,1024]{1,0:T(8,128)(2,1)S(1)}, u32[]{:S(2)}, u32[]{:S(2)}) collective-permute-start(bf16[128,1024]{1,0:T(8,128)(2,1)S(1)} %get-tuple-element.72), channel_id=1, source_target_pairs={{0,1},{1,0},{2,3},{3,2},{4,5},{5,4},{6,7},{7,6},{8,9},{9,8},{10,11... | collective-permute-start | bytes 786440 | tf_op jit(solution)/shard_map/ppermute | solution.py:515
  57.6 2.9 %collective-permute-start.18 = (bf16[128,1024]{1,0:T(8,128)(2,1)S(1)}, bf16[128,1024]{1,0:T(8,128)(2,1)S(1)}, u32[]{:S(2)}, u32[]{:S(2)}) collective-permute-start(bf16[128,1024]{1,0:T(8,128)(2,1)S(1)} %get-tuple-element.78), channel_id=1, source_target_pairs={{0,1},{1,0},{2,3},{3,2},{4,5},{5,4},{6,7},{7,6},{8,9},{9,8},{10,11... | collective-permute-start | bytes 786440 | tf_op jit(solution)/shard_map/ppermute | solution.py:515
  57.7 2.7 %collective-permute-start.14 = (bf16[128,1024]{1,0:T(8,128)(2,1)S(1)}, bf16[128,1024]{1,0:T(8,128)(2,1)S(1)}, u32[]{:S(2)}, u32[]{:S(2)}) collective-permute-start(bf16[128,1024]{1,0:T(8,128)(2,1)S(1)} %get-tuple-element.74), channel_id=1, source_target_pairs={{0,1},{1,0},{2,3},{3,2},{4,5},{5,4},{6,7},{7,6},{8,9},{9,8},{10,11... | collective-permute-start | bytes 786440 | tf_op jit(solution)/shard_map/ppermute | solution.py:515
  58.2 9.2 %collective-permute-start.17 = (bf16[128,1024]{1,0:T(8,128)(2,1)S(1)}, bf16[128,1024]{1,0:T(8,128)(2,1)S(1)}, u32[]{:S(2)}, u32[]{:S(2)}) collective-permute-start(bf16[128,1024]{1,0:T(8,128)(2,1)S(1)} %add_convert_fusion), channel_id=1, source_target_pairs={{0,2},{1,3},{2,0},{3,1},{4,6},{5,7},{6,4},{7,5},{8,10},{9,11},{10,... | collective-permute-start | bytes 786440 | tf_op jit(solution)/shard_map/ppermute | solution.py:515
  59.9 12.3 %collective-permute-start.13 = (bf16[128,1024]{1,0:T(8,128)(2,1)S(1)}, bf16[128,1024]{1,0:T(8,128)(2,1)S(1)}, u32[]{:S(2)}, u32[]{:S(2)}) collective-permute-start(bf16[128,1024]{1,0:T(8,128)(2,1)S(1)} %add_convert_fusion.1), channel_id=1, source_target_pairs={{0,2},{1,3},{2,0},{3,1},{4,6},{5,7},{6,4},{7,5},{8,10},{9,11},{10,... | collective-permute-start | bytes 786440 | tf_op jit(solution)/shard_map/ppermute | solution.py:515
  (2 other events, 13.3 us)

commit v6 on v5

--- a/solution.py
+++ b/solution.py
@@ -231,10 +231,10 @@
     ]
 
 
-def inner_kernel(scores, skip, scaled, conv_out, cum, cum_t, out, *, chunk, chunks, head_dim):
-    heads = scaled.shape[1] // head_dim
+def inner_kernel(bc, skip, dt, conv_out, cum, cum_t, out, *, chunk, chunks, head_dim):
+    heads = conv_out.shape[1] // head_dim
     within(
-        place(), scores, scaled, conv_out, cum, cum_t, skip, out,
+        place(), bc, dt, conv_out, cum, cum_t, skip, out,
         head_dim=head_dim, first_of=chunk * heads, local_heads=chunks * heads,
     )
 
@@ -264,11 +264,11 @@
     refs = list(refs)
     if not first:
         bc_in = refs.pop(0)
-    mine, theirs, x_mine, x_theirs, edge_a, edge_b, taps_x, taps_bc, bias, decay = refs[:10]
+    mine, theirs, x_mine, x_theirs, edge_b, edge_a, taps_x, taps_bc, bias, decay = refs[:10]
     refs = refs[10:]
     if first:
-        bc_out, scores = refs.pop(0), refs.pop(0)
-    msg, scaled, conv_out, cum_out, cum_t_out, ext = refs
+        bc_out = refs.pop(0)
+    msg, dt_out, conv_out, cum_out, cum_t_out, ext = refs
     row, _, here = place()
     blocks = x_mine.shape[0] // toks // chunks
     heads = blocks * lanes // head_dim
@@ -285,10 +285,6 @@
         bc_now = silu(conv(ext, taps_bc[...], toks)).astype(bf16)
         bc_out[...] = bc_now
         b_now = bc_now[:, :state_dim]
-        products = mm_nt(bc_now[:, state_dim:], b_now)
-        shape = (toks, toks)
-        lower = lax.broadcasted_iota(jnp.int32, shape, 0) >= lax.broadcasted_iota(jnp.int32, shape, 1)
-        scores[...] = jnp.where(lower, products, 0.0)
     else:
         b_now = bc_in[:, :state_dim]
 
@@ -310,7 +306,7 @@
     last = cum[:, toks - 1 : toks]
     cum_out[...] = cum
     cum_t_out[...] = cum.T
-    dt_wide = spread(dt_now, head_dim)
+    dt_out[...] = dt_now
     tail_wide = spread(dt_now * jnp.exp(last - cum), head_dim)
     through = spread(jnp.exp(jnp.broadcast_to(last, (heads, HALO))), head_dim)
     x_low = x_theirs.shape[0] - blocks * toks
@@ -324,7 +320,6 @@
         cols = slice(j * lanes, (j + 1) * lanes)
         x_now = silu(conv(ext, taps_x[:, pl.ds(pl.multiple_of(taps_low + j * lanes, lanes), lanes)], toks))
         conv_out[:, cols] = x_now.astype(bf16)
-        scaled[:, cols] = (x_now * dt_wide[:, cols]).astype(bf16)
         state = mm_tn(b_now, (x_now * tail_wide[:, cols]).astype(bf16))
         msg[j * state_dim : (j + 1) * state_dim, :] = state.astype(bf16)
     msg[blocks * state_dim :, :] = decay_rows(
@@ -345,8 +340,13 @@
     out[blocks * state_dim :, :] = decay_rows(decays)
 
 
-def within(where, scores, scaled, conv_out, cum, cum_t, skip, out, *, head_dim, first_of, local_heads):
-    toks, channels = scaled.shape
+def within(where, bc, dt, conv_out, cum, cum_t, skip, out, *, head_dim, first_of, local_heads):
+    toks, channels = conv_out.shape
+    state_dim = bc.shape[1] // 2
+    shape = (toks, toks)
+    lower = lax.broadcasted_iota(jnp.int32, shape, 0) >= lax.broadcasted_iota(jnp.int32, shape, 1)
+    scores = jnp.where(lower, mm_nt(bc[:, state_dim:], bc[:, :state_dim]), 0.0)
+    dt_wide = spread(dt[...], head_dim)
     pair = 2 * head_dim
     half = toks // 2
     heads = channels // head_dim
@@ -356,7 +356,7 @@
     zero = jnp.zeros((toks, pair), bf16)
     for p in range(heads // 2):
         cols = slice(p * pair, (p + 1) * pair)
-        x_pair = scaled[:, cols]
+        x_pair = (conv_out[:, cols].astype(f32) * dt_wide[:, cols]).astype(bf16)
         top = None
         for side in range(2):
             h = 2 * p + side
@@ -596,17 +596,17 @@
 
     sizes = dict(head_dim=head_dim, state_dim=state_dim, lanes=lanes)
     states, scans = [], []
-    bc_now = scores = None
+    bc_now = None
     for c in range(chunks):
         args = [] if c == 0 else [bc_now]
         args += [
-            msg_first, first_got, x_mine, first_got if c == 0 else second_got, edge_a, edge_b,
+            msg_first, first_got, x_mine, first_got if c == 0 else second_got, edge_b, edge_a,
             conv_x_t, conv_bc_t, bias, decay,
         ]
-        outs = [sds(toks, lanes), sds(toks, toks, dtype=f32)] if c == 0 else []
+        outs = [sds(toks, lanes)] if c == 0 else []
         outs += [
             sds(blocks * state_dim + HALO, lanes),
-            sds(toks, width),
+            sds(chunk_heads, toks, dtype=f32),
             sds(toks, width),
             sds(chunk_heads, toks, dtype=f32),
             sds(toks, chunk_heads, dtype=f32),
@@ -623,7 +623,7 @@
             after=(z_send[0],),
         )
         if c == 0:
-            bc_now, scores, *got = got
+            bc_now, *got = got
         states.append(got[0])
         scans.append(got[1:])
 
@@ -632,7 +632,7 @@
     def inner_call(c):
         (inner,) = call(
             functools.partial(inner_kernel, chunk=c, chunks=chunks, head_dim=head_dim),
-            (scores, skip, *scans[c]),
+            (bc_now, skip, *scans[c]),
             None,
             [sds(toks, width, dtype=f32)],
             name="inner",
@@ -657,7 +657,7 @@
             by *= 2
         messages.append(heard)
         sent.append(send)
-    early = half // 2
+    early = half // 4
     z_mine, w_first = call(
         functools.partial(own_gate_kernel, kb=kb),
         (tok_held, proj_z, proj_out),

time: 73.3 us -> 73.2 us (level)
  no operation moved by 1% of the time
where the time goes in v6:
time: 73.2 us; the launch traced here: 73.1 us
  Pallas kernels  35.7 us (49%)
  starting transfers between devices  20.3 us (28%)
  waiting for transfers between devices  16.7 us (23%)
    pallas_call x18, Pallas kernels, call(): pl.pallas_call(body, in_specs=[*(specs or [IN_VMEM] * used), *[pl.BlockSp...  35.7 us
    ppermute x17, waiting for transfers between devices, swapped(): return lax.ppermute(shard, axis, [(i, i ^ by) for i in range(devices)])  16.7 us
    ppermute x17, starting transfers between devices, swapped(): return lax.ppermute(shard, axis, [(i, i ^ by) for i in range(devices)])  15.5 us
    ppermute x1, starting transfers between devices, fast(): lax.ppermute(edge_other, ('ctx', 'row'), [(2 * i + s, 2 * j + 1 - s) for...  2.72 us
    ppermute x1, starting transfers between devices, fast(): edge_b = lax.ppermute(edge_own, 'ctx', down)  2.09 us
  transfers between devices with their start and end apart: 19, of which 7 were waited for; matrix products, arithmetic and copies ran while one was open for 0% of the time, Pallas kernels for 39%

profile of v6, /device:TPU:0, one launch (start us, length us, event | category | flops | bytes accessed | tf_op | source)
XLA Modules:
  0.0 73.1 jit_solution(11566577142382571469)
XLA Ops:
  0.0 5.0 %first.1 = (bf16[800,256]{1,0:T(8,128)(2,1)}, bf16[48,256]{1,0:T(8,128)(2,1)S(1)}) custom-call(bf16[256,4096]{1,0:T(8,128)(2,1)} %refs_0_.6, bf16[4096,2048]{1,0:T(8,128)(2,1)} %refs_1_.5, bf16[4096,256]{1,0:T(8,128)(2,1)} %refs_2_.2, bf16[32,4096]{1,0:T(8,128)(2,1)} %bitcast.19), custom_call_target="tpu_custom_call" | custom-call | tf_op jit(solution)/shard_map/first/pallas_call | solution.py:497
  5.0 3.0 %collective-permute-start = (bf16[800,256]{1,0:T(8,128)(2,1)}, bf16[800,256]{1,0:T(8,128)(2,1)S(1)}, u32[]{:S(2)}, u32[]{:S(2)}) collective-permute-start(bf16[800,256]{1,0:T(8,128)(2,1)} %get-tuple-element.44.refs_0_.refs_1_), channel_id=1, source_target_pairs={{0,4},{4,0},{1,5},{5,1},{2,6},{6,2},{3,7},{7,3},{8,12},{12,8},{9,1... | collective-permute-start | bytes 1228808 | tf_op jit(solution)/shard_map/ppermute | solution.py:515
  8.0 6.1 %second.1 = (bf16[512,256]{1,0:T(8,128)(2,1)S(1)}, bf16[1024,256]{1,0:T(8,128)(2,1)S(1)}, bf16[80,256]{1,0:T(8,128)(2,1)S(1)}, bf16[80,256]{1,0:T(8,128)(2,1)S(1)}) custom-call(bf16[256,4096]{1,0:T(8,128)(2,1)} %refs_0_.6, bf16[4096,2048]{1,0:T(8,128)(2,1)} %refs_1_.5, bf16[48,256]{1,0:T(8,128)(2,1)S(1)} %get-tuple-element.41.refs_2_), custom_call_target="tpu_custom_call" | custom-call | tf_op jit(solution)/shard_map/second/pallas_call | solution.py:497
  14.3 2.1 %collective-permute-start.1 = (bf16[80,256]{1,0:T(8,128)(2,1)S(1)}, bf16[80,256]{1,0:T(8,128)(2,1)S(1)}, u32[]{:S(2)}, u32[]{:S(2)}) collective-permute-start(bf16[80,256]{1,0:T(8,128)(2,1)S(1)} %get-tuple-element.42.refs_2_), channel_id=1, source_target_pairs={{0,8},{8,16},{16,24},{24,0},{1,9},{9,17},{17,25},{25,1},{2,10},{10... | collective-permute-start | bytes 122888 | tf_op jit(solution)/shard_map/ppermute | solution.py:581
  16.4 2.7 %collective-permute-start.2 = (bf16[80,256]{1,0:T(8,128)(2,1)S(1)}, bf16[80,256]{1,0:T(8,128)(2,1)S(1)}, u32[]{:S(2)}, u32[]{:S(2)}) collective-permute-start(bf16[80,256]{1,0:T(8,128)(2,1)S(1)} %get-tuple-element.46), channel_id=1, source_target_pairs={{0,12},{4,8},{8,20},{12,16},{16,28},{20,24},{24,4},{28,0},{1,13},{... | collective-permute-start | bytes 122888 | tf_op jit(solution)/shard_map/ppermute | solution.py:578
  19.1 4.6 %z_other.1 = (bf16[512,256]{1,0:T(8,128)(2,1)S(1)}, bf16[512,256]{1,0:T(8,128)(2,1)S(1)}, bf16[256,4096]{1,0:T(8,128)(2,1)S(1)}) custom-call(bf16[256,4096]{1,0:T(8,128)(2,1)} %refs_0_.6, bf16[4096,2048]{1,0:T(8,128)(2,1)} %refs_1_.7, bf16[80,256]{1,0:T(8,128)(2,1)S(1)} %get-tuple-element.42.refs_2_), custom_call_target="tpu_custom_call" | custom-call | tf_op jit(solution)/shard_map/z_other/pallas_call | solution.py:497
  23.8 1.6 %state.2 = (bf16[256,256]{1,0:T(8,128)(2,1)S(1)}, bf16[272,256]{1,0:T(8,128)(2,1)S(1)}, f32[8,256]{1,0:T(8,128)S(1)}, bf16[256,512]{1,0:T(8,128)(2,1)S(1)}, f32[8,256]{1,0:T(8,128)S(1)}, /*index=5*/f32[256,8]{1,0:T(8,128)S(1)}) custom-call(bf16[800,256]{1,0:T(8,128)(2,1)S(1)} %copy-done, bf16[800,256]{1,0:T(8,128)(2,1)S(1)} %collective-permute-done.refs_1_.refs_3_.refs_2_, ...), custom_call_target="tpu_custom_call" | custom-call | tf_op jit(solution)/shard_map/state/pallas_call | solution.py:497
  25.4 1.7 %collective-permute-start.3 = (bf16[272,256]{1,0:T(8,128)(2,1)S(1)}, bf16[272,256]{1,0:T(8,128)(2,1)S(1)}, u32[]{:S(2)}, u32[]{:S(2)}) collective-permute-start(bf16[272,256]{1,0:T(8,128)(2,1)S(1)} %get-tuple-element.48.refs_0_.refs_6_), channel_id=1, source_target_pairs={{0,8},{8,0},{16,24},{24,16},{1,9},{9,1},{17,25},{25,17},{2,10},{10... | collective-permute-start | bytes 417800 | tf_op jit(solution)/shard_map/ppermute | solution.py:515
  27.0 1.4 %state.3 = (bf16[272,256]{1,0:T(8,128)(2,1)S(1)}, f32[8,256]{1,0:T(8,128)S(1)}, bf16[256,512]{1,0:T(8,128)(2,1)S(1)}, f32[8,256]{1,0:T(8,128)S(1)}, f32[256,8]{1,0:T(8,128)S(1)}) custom-call(bf16[256,256]{1,0:T(8,128)(2,1)S(1)} %get-tuple-element.49.refs_0_.refs_1_, bf16[800,256]{1,0:T(8,128)(2,1)S(1)} %copy-done, ...), custom_call_target="tpu_custom_call" | custom-call | tf_op jit(solution)/shard_map/state/pallas_call | solution.py:497
  29.1 1.0 %collective-permute-start.5 = (bf16[272,256]{1,0:T(8,128)(2,1)S(1)}, bf16[272,256]{1,0:T(8,128)(2,1)S(1)}, u32[]{:S(2)}, u32[]{:S(2)}) collective-permute-start(bf16[272,256]{1,0:T(8,128)(2,1)S(1)} %get-tuple-element.51.refs_0_.refs_6_), channel_id=1, source_target_pairs={{0,8},{8,0},{16,24},{24,16},{1,9},{9,1},{17,25},{25,17},{2,10},{10... | collective-permute-start | bytes 417800 | tf_op jit(solution)/shard_map/ppermute | solution.py:515
  30.1 1.1 %collective-permute-done.3.refs_1_.refs_7_ = bf16[272,256]{1,0:T(8,128)(2,1)S(1)} collective-permute-done((bf16[272,256]{1,0:T(8,128)(2,1)S(1)}, bf16[272,256]{1,0:T(8,128)(2,1)S(1)}, u32[]{:S(2)}, u32[]{:S(2)}) %collective-permute-start.3) | collective-permute-done | bytes 139296 | tf_op jit(solution)/shard_map/ppermute | solution.py:515
  31.3 1.0 %collective-permute-start.9 = (bf16[272,256]{1,0:T(8,128)(2,1)S(1)}, bf16[272,256]{1,0:T(8,128)(2,1)S(1)}, u32[]{:S(2)}, u32[]{:S(2)}) collective-permute-start(bf16[272,256]{1,0:T(8,128)(2,1)S(1)} %combine.2.refs_6_.refs_2_.refs_3_), channel_id=1, source_target_pairs={{0,16},{8,24},{16,0},{24,8},{1,17},{9,25},{17,1},{25,9},{2,18},{10... | collective-permute-start | bytes 417800 | tf_op jit(solution)/shard_map/ppermute | solution.py:515
  33.9 1.0 %collective-permute-done.5.refs_1_.refs_7_ = bf16[272,256]{1,0:T(8,128)(2,1)S(1)} collective-permute-done((bf16[272,256]{1,0:T(8,128)(2,1)S(1)}, bf16[272,256]{1,0:T(8,128)(2,1)S(1)}, u32[]{:S(2)}, u32[]{:S(2)}) %collective-permute-start.5) | collective-permute-done | bytes 139296 | tf_op jit(solution)/shard_map/ppermute | solution.py:515
  35.1 1.5 %collective-permute-start.7 = (bf16[272,256]{1,0:T(8,128)(2,1)S(1)}, bf16[272,256]{1,0:T(8,128)(2,1)S(1)}, u32[]{:S(2)}, u32[]{:S(2)}) collective-permute-start(bf16[272,256]{1,0:T(8,128)(2,1)S(1)} %combine.3.refs_4_), channel_id=1, source_target_pairs={{0,16},{8,24},{16,0},{24,8},{1,17},{9,25},{17,1},{25,9},{2,18},{10... | collective-permute-start | bytes 417800 | tf_op jit(solution)/shard_map/ppermute | solution.py:515
  36.6 4.2 %z_own.1 = (bf16[1024,256]{1,0:T(8,128)(2,1)S(1)}, bf16[256,4096]{1,0:T(8,128)(2,1)S(1)}) custom-call(bf16[256,4096]{1,0:T(8,128)(2,1)S(1)} %get-tuple-element.43.refs_0_, bf16[4096,2048]{1,0:T(8,128)(2,1)} %refs_1_.7, bf16[2048,4096]{1,0:T(8,128)(2,1)} %refs_0_.7, bf16[272,256]{1,0:T(8,128)(2,1)S(1)} %combine.2.refs_6_.refs_2_.refs_3_, ...), custom_call_target="tpu_custom_call" | custom-call | tf_op jit(solution)/shard_map/z_own/pallas_call | solution.py:497
  40.8 1.5 %collective-permute-done.9.refs_8_ = bf16[272,256]{1,0:T(8,128)(2,1)S(1)} collective-permute-done((bf16[272,256]{1,0:T(8,128)(2,1)S(1)}, bf16[272,256]{1,0:T(8,128)(2,1)S(1)}, u32[]{:S(2)}, u32[]{:S(2)}) %collective-permute-start.9) | collective-permute-done | bytes 139296 | tf_op jit(solution)/shard_map/ppermute | solution.py:515
  42.3 0.8 %gate.3.refs_4_ = bf16[512,256]{1,0:T(8,128)(2,1)S(1)} custom-call(f32[256,512]{1,0:T(8,128)S(1)} %inner.2.refs_3_.refs_5_.refs_0_, bf16[256,256]{1,0:T(8,128)(2,1)S(1)} %get-tuple-element.49.refs_0_.refs_1_, f32[8,256]{1,0:T(8,128)S(1)} %get-tuple-element.54.refs_4_.refs_2_, bf16[1024,256]{1,0:T(8,128)(2,1)S(1)} %get-tuple-element.61.refs_3_, ...), custom_call_target="tpu_custom_call" | custom-call | tf_op jit(solution)/shard_map/gate/pallas_call | solution.py:497
  43.1 0.9 %collective-permute-start.11 = (bf16[512,256]{1,0:T(8,128)(2,1)S(1)}, bf16[512,256]{1,0:T(8,128)(2,1)S(1)}, u32[]{:S(2)}, u32[]{:S(2)}) collective-permute-start(bf16[512,256]{1,0:T(8,128)(2,1)S(1)} %gate.3.refs_4_), channel_id=1, source_target_pairs={{0,4},{4,0},{1,5},{5,1},{2,6},{6,2},{3,7},{7,3},{8,12},{12,8},{9,1... | collective-permute-start | bytes 786440 | tf_op jit(solution)/shard_map/ppermute | solution.py:515
  46.4 1.3 %collective-permute-start.15 = (bf16[256,256]{1,0:T(8,128)(2,1)S(1)}, bf16[256,256]{1,0:T(8,128)(2,1)S(1)}, u32[]{:S(2)}, u32[]{:S(2)}) collective-permute-start(bf16[256,256]{1,0:T(8,128)(2,1)S(1)} %get-tuple-element.65.refs_3_), channel_id=1, source_target_pairs={{0,4},{4,0},{1,5},{5,1},{2,6},{6,2},{3,7},{7,3},{8,12},{12,8},{9,1... | collective-permute-start | bytes 393224 | tf_op jit(solution)/shard_map/ppermute | solution.py:515
  47.7 5.5 %out_own.1 = (f32[256,4096]{1,0:T(8,128)S(1)}, bf16[1024,4096]{1,0:T(8,128)(2,1)S(1)}) custom-call(bf16[2048,4096]{1,0:T(8,128)(2,1)} %refs_0_.7, bf16[256,4096]{1,0:T(8,128)(2,1)S(1)} %get-tuple-element.60.refs_1_, bf16[256,256]{1,0:T(8,128)(2,1)S(1)} %get-tuple-element.64.refs_2_, bf16[256,256]{1,0:T(8,128)(2,1)S(1)} %get-tuple-element.65.refs_3_, ...), custom_call_target="tpu_custom_call" | custom-call | tf_op jit(solution)/shard_map/out_own/pallas_call | solution.py:497
  58.1 1.6 %collective-permute-start.17 = (bf16[128,1024]{1,0:T(8,128)(2,1)S(1)}, bf16[128,1024]{1,0:T(8,128)(2,1)S(1)}, u32[]{:S(2)}, u32[]{:S(2)}) collective-permute-start(bf16[128,1024]{1,0:T(8,128)(2,1)S(1)} %add_convert_fusion), channel_id=1, source_target_pairs={{0,2},{1,3},{2,0},{3,1},{4,6},{5,7},{6,4},{7,5},{8,10},{9,11},{10,... | collective-permute-start | bytes 786440 | tf_op jit(solution)/shard_map/ppermute | solution.py:515
  60.4 7.0 %collective-permute-done.17.refs_3_ = bf16[128,1024]{1,0:T(8,128)(2,1)S(1)} collective-permute-done((bf16[128,1024]{1,0:T(8,128)(2,1)S(1)}, bf16[128,1024]{1,0:T(8,128)(2,1)S(1)}, u32[]{:S(2)}, u32[]{:S(2)}) %collective-permute-start.17) | collective-permute-done | bytes 262176 | tf_op jit(solution)/shard_map/ppermute | solution.py:515
  67.4 4.7 %collective-permute-done.13.refs_0_ = bf16[128,1024]{1,0:T(8,128)(2,1)S(1)} collective-permute-done((bf16[128,1024]{1,0:T(8,128)(2,1)S(1)}, bf16[128,1024]{1,0:T(8,128)(2,1)S(1)}, u32[]{:S(2)}, u32[]{:S(2)}) %collective-permute-start.13) | collective-permute-done | bytes 262176 | tf_op jit(solution)/shard_map/ppermute | solution.py:515
  72.1 1.0 %final.1 = bf16[256,1024]{1,0:T(8,128)(2,1)} custom-call(bf16[128,1024]{1,0:T(8,128)(2,1)S(1)} %collective-permute-done.13.refs_0_, bf16[128,1024]{1,0:T(8,128)(2,1)S(1)} %get-tuple-element.71.refs_4_.refs_1_, bf16[128,1024]{1,0:T(8,128)(2,1)S(1)} %collective-permute-done.14.refs_2_, bf16[128,1024]{1,0:T(8,128)(2,1)S(1)} %collective-permute-done.17.refs_3_, ...), custom_call_target="tpu_custom_call" | custom-call | tf_op jit(solution)/shard_map/final/pallas_call | solution.py:497
  (48 shorter events, 10.3 us)
Async XLA Ops:
  5.0 18.7 %collective-permute-start = (bf16[800,256]{1,0:T(8,128)(2,1)}, bf16[800,256]{1,0:T(8,128)(2,1)S(1)}, u32[]{:S(2)}, u32[]{:S(2)}) collective-permute-start(bf16[800,256]{1,0:T(8,128)(2,1)} %get-tuple-element.44.refs_0_.refs_1_), channel_id=1, source_target_pairs={{0,4},{4,0},{1,5},{5,1},{2,6},{6,2},{3,7},{7,3},{8,12},{12,8},{9,1... | collective-permute-start | bytes 1228808 | tf_op jit(solution)/shard_map/ppermute | solution.py:515
  14.2 12.9 %collective-permute-start.4 = (bf16[512,256]{1,0:T(8,128)(2,1)S(1)}, bf16[512,256]{1,0:T(8,128)(2,1)S(1)}, u32[]{:S(2)}, u32[]{:S(2)}) collective-permute-start(bf16[512,256]{1,0:T(8,128)(2,1)S(1)} %get-tuple-element.50), channel_id=1, source_target_pairs={{0,4},{4,0},{1,5},{5,1},{2,6},{6,2},{3,7},{7,3},{8,12},{12,8},{9,1... | collective-permute-start | bytes 786440 | tf_op jit(solution)/shard_map/ppermute | solution.py:515
  14.3 9.5 %collective-permute-start.1 = (bf16[80,256]{1,0:T(8,128)(2,1)S(1)}, bf16[80,256]{1,0:T(8,128)(2,1)S(1)}, u32[]{:S(2)}, u32[]{:S(2)}) collective-permute-start(bf16[80,256]{1,0:T(8,128)(2,1)S(1)} %get-tuple-element.42.refs_2_), channel_id=1, source_target_pairs={{0,8},{8,16},{16,24},{24,0},{1,9},{9,17},{17,25},{25,1},{2,10},{10... | collective-permute-start | bytes 122888 | tf_op jit(solution)/shard_map/ppermute | solution.py:581
  16.4 7.4 %copy-start.1 = (f32[2048,4]{0,1:T(4,128)S(1)}, f32[2048,4]{0,1:T(4,128)}, u32[]{:S(2)}) copy-start(f32[2048,4]{0,1:T(4,128)} %param.20) | copy-start | bytes 98308
  16.4 7.4 %copy-start.3 = (f32[256,4]{0,1:T(4,128)S(1)}, f32[256,4]{0,1:T(4,128)}, u32[]{:S(2)}) copy-start(f32[256,4]{0,1:T(4,128)} %param.21) | copy-start | bytes 12292
  16.4 7.4 %copy-start.5 = (f32[32]{0:T(128)S(1)}, f32[32]{0:T(128)}, u32[]{:S(2)}) copy-start(f32[32]{0:T(128)} %param.17) | copy-start | bytes 388
  16.4 7.4 %copy-start.6 = (f32[32]{0:T(128)S(1)}, f32[32]{0:T(128)}, u32[]{:S(2)}) copy-start(f32[32]{0:T(128)} %param.18) | copy-start | bytes 388
  16.4 7.4 %collective-permute-start.2 = (bf16[80,256]{1,0:T(8,128)(2,1)S(1)}, bf16[80,256]{1,0:T(8,128)(2,1)S(1)}, u32[]{:S(2)}, u32[]{:S(2)}) collective-permute-start(bf16[80,256]{1,0:T(8,128)(2,1)S(1)} %get-tuple-element.46), channel_id=1, source_target_pairs={{0,12},{4,8},{8,20},{12,16},{16,28},{20,24},{24,4},{28,0},{1,13},{... | collective-permute-start | bytes 122888 | tf_op jit(solution)/shard_map/ppermute | solution.py:578
  23.7 8.9 %copy-start.4 = (f32[32]{0:T(128)S(1)}, f32[32]{0:T(128)}, u32[]{:S(2)}) copy-start(f32[32]{0:T(128)} %param.19) | copy-start | bytes 388
  25.4 5.8 %collective-permute-start.3 = (bf16[272,256]{1,0:T(8,128)(2,1)S(1)}, bf16[272,256]{1,0:T(8,128)(2,1)S(1)}, u32[]{:S(2)}, u32[]{:S(2)}) collective-permute-start(bf16[272,256]{1,0:T(8,128)(2,1)S(1)} %get-tuple-element.48.refs_0_.refs_6_), channel_id=1, source_target_pairs={{0,8},{8,0},{16,24},{24,16},{1,9},{9,1},{17,25},{25,17},{2,10},{10... | collective-permute-start | bytes 417800 | tf_op jit(solution)/shard_map/ppermute | solution.py:515
  28.5 12.3 %collective-permute-start.8 = (bf16[512,256]{1,0:T(8,128)(2,1)S(1)}, bf16[512,256]{1,0:T(8,128)(2,1)S(1)}, u32[]{:S(2)}, u32[]{:S(2)}) collective-permute-start(bf16[512,256]{1,0:T(8,128)(2,1)S(1)} %get-tuple-element.66.refs_10_.refs_11_), channel_id=1, source_target_pairs={{0,4},{4,0},{1,5},{5,1},{2,6},{6,2},{3,7},{7,3},{8,12},{12,8},{9,1... | collective-permute-start | bytes 786440 | tf_op jit(solution)/shard_map/ppermute | solution.py:515
  29.1 5.9 %collective-permute-start.5 = (bf16[272,256]{1,0:T(8,128)(2,1)S(1)}, bf16[272,256]{1,0:T(8,128)(2,1)S(1)}, u32[]{:S(2)}, u32[]{:S(2)}) collective-permute-start(bf16[272,256]{1,0:T(8,128)(2,1)S(1)} %get-tuple-element.51.refs_0_.refs_6_), channel_id=1, source_target_pairs={{0,8},{8,0},{16,24},{24,16},{1,9},{9,1},{17,25},{25,17},{2,10},{10... | collective-permute-start | bytes 417800 | tf_op jit(solution)/shard_map/ppermute | solution.py:515
  31.3 11.0 %collective-permute-start.9 = (bf16[272,256]{1,0:T(8,128)(2,1)S(1)}, bf16[272,256]{1,0:T(8,128)(2,1)S(1)}, u32[]{:S(2)}, u32[]{:S(2)}) collective-permute-start(bf16[272,256]{1,0:T(8,128)(2,1)S(1)} %combine.2.refs_6_.refs_2_.refs_3_), channel_id=1, source_target_pairs={{0,16},{8,24},{16,0},{24,8},{1,17},{9,25},{17,1},{25,9},{2,18},{10... | collective-permute-start | bytes 417800 | tf_op jit(solution)/shard_map/ppermute | solution.py:515
  32.3 11.8 %collective-permute-start.6 = (bf16[512,256]{1,0:T(8,128)(2,1)S(1)}, bf16[512,256]{1,0:T(8,128)(2,1)S(1)}, u32[]{:S(2)}, u32[]{:S(2)}) collective-permute-start(bf16[512,256]{1,0:T(8,128)(2,1)S(1)} %get-tuple-element.63), channel_id=1, source_target_pairs={{0,4},{4,0},{1,5},{5,1},{2,6},{6,2},{3,7},{7,3},{8,12},{12,8},{9,1... | collective-permute-start | bytes 786440 | tf_op jit(solution)/shard_map/ppermute | solution.py:515
  35.1 9.7 %collective-permute-start.7 = (bf16[272,256]{1,0:T(8,128)(2,1)S(1)}, bf16[272,256]{1,0:T(8,128)(2,1)S(1)}, u32[]{:S(2)}, u32[]{:S(2)}) collective-permute-start(bf16[272,256]{1,0:T(8,128)(2,1)S(1)} %combine.3.refs_4_), channel_id=1, source_target_pairs={{0,16},{8,24},{16,0},{24,8},{1,17},{9,25},{17,1},{25,9},{2,18},{10... | collective-permute-start | bytes 417800 | tf_op jit(solution)/shard_map/ppermute | solution.py:515
  43.1 10.7 %collective-permute-start.11 = (bf16[512,256]{1,0:T(8,128)(2,1)S(1)}, bf16[512,256]{1,0:T(8,128)(2,1)S(1)}, u32[]{:S(2)}, u32[]{:S(2)}) collective-permute-start(bf16[512,256]{1,0:T(8,128)(2,1)S(1)} %gate.3.refs_4_), channel_id=1, source_target_pairs={{0,4},{4,0},{1,5},{5,1},{2,6},{6,2},{3,7},{7,3},{8,12},{12,8},{9,1... | collective-permute-start | bytes 786440 | tf_op jit(solution)/shard_map/ppermute | solution.py:515
  45.6 8.2 %collective-permute-start.10 = (bf16[256,256]{1,0:T(8,128)(2,1)S(1)}, bf16[256,256]{1,0:T(8,128)(2,1)S(1)}, u32[]{:S(2)}, u32[]{:S(2)}) collective-permute-start(bf16[256,256]{1,0:T(8,128)(2,1)S(1)} %get-tuple-element.64.refs_2_), channel_id=1, source_target_pairs={{0,4},{4,0},{1,5},{5,1},{2,6},{6,2},{3,7},{7,3},{8,12},{12,8},{9,1... | collective-permute-start | bytes 393224 | tf_op jit(solution)/shard_map/ppermute | solution.py:515
  46.4 8.9 %collective-permute-start.15 = (bf16[256,256]{1,0:T(8,128)(2,1)S(1)}, bf16[256,256]{1,0:T(8,128)(2,1)S(1)}, u32[]{:S(2)}, u32[]{:S(2)}) collective-permute-start(bf16[256,256]{1,0:T(8,128)(2,1)S(1)} %get-tuple-element.65.refs_3_), channel_id=1, source_target_pairs={{0,4},{4,0},{1,5},{5,1},{2,6},{6,2},{3,7},{7,3},{8,12},{12,8},{9,1... | collective-permute-start | bytes 393224 | tf_op jit(solution)/shard_map/ppermute | solution.py:515
  56.1 1.9 %collective-permute-start.16 = (bf16[128,1024]{1,0:T(8,128)(2,1)S(1)}, bf16[128,1024]{1,0:T(8,128)(2,1)S(1)}, u32[]{:S(2)}, u32[]{:S(2)}) collective-permute-start(bf16[128,1024]{1,0:T(8,128)(2,1)S(1)} %get-tuple-element.74), channel_id=1, source_target_pairs={{0,1},{1,0},{2,3},{3,2},{4,5},{5,4},{6,7},{7,6},{8,9},{9,8},{10,11... | collective-permute-start | bytes 786440 | tf_op jit(solution)/shard_map/ppermute | solution.py:515
  56.2 3.5 %collective-permute-start.12 = (bf16[128,1024]{1,0:T(8,128)(2,1)S(1)}, bf16[128,1024]{1,0:T(8,128)(2,1)S(1)}, u32[]{:S(2)}, u32[]{:S(2)}) collective-permute-start(bf16[128,1024]{1,0:T(8,128)(2,1)S(1)} %get-tuple-element.70), channel_id=1, source_target_pairs={{0,1},{1,0},{2,3},{3,2},{4,5},{5,4},{6,7},{7,6},{8,9},{9,8},{10,11... | collective-permute-start | bytes 786440 | tf_op jit(solution)/shard_map/ppermute | solution.py:515
  57.5 2.9 %collective-permute-start.18 = (bf16[128,1024]{1,0:T(8,128)(2,1)S(1)}, bf16[128,1024]{1,0:T(8,128)(2,1)S(1)}, u32[]{:S(2)}, u32[]{:S(2)}) collective-permute-start(bf16[128,1024]{1,0:T(8,128)(2,1)S(1)} %get-tuple-element.76), channel_id=1, source_target_pairs={{0,1},{1,0},{2,3},{3,2},{4,5},{5,4},{6,7},{7,6},{8,9},{9,8},{10,11... | collective-permute-start | bytes 786440 | tf_op jit(solution)/shard_map/ppermute | solution.py:515
  57.6 2.7 %collective-permute-start.14 = (bf16[128,1024]{1,0:T(8,128)(2,1)S(1)}, bf16[128,1024]{1,0:T(8,128)(2,1)S(1)}, u32[]{:S(2)}, u32[]{:S(2)}) collective-permute-start(bf16[128,1024]{1,0:T(8,128)(2,1)S(1)} %get-tuple-element.72), channel_id=1, source_target_pairs={{0,1},{1,0},{2,3},{3,2},{4,5},{5,4},{6,7},{7,6},{8,9},{9,8},{10,11... | collective-permute-start | bytes 786440 | tf_op jit(solution)/shard_map/ppermute | solution.py:515
  58.1 9.2 %collective-permute-start.17 = (bf16[128,1024]{1,0:T(8,128)(2,1)S(1)}, bf16[128,1024]{1,0:T(8,128)(2,1)S(1)}, u32[]{:S(2)}, u32[]{:S(2)}) collective-permute-start(bf16[128,1024]{1,0:T(8,128)(2,1)S(1)} %add_convert_fusion), channel_id=1, source_target_pairs={{0,2},{1,3},{2,0},{3,1},{4,6},{5,7},{6,4},{7,5},{8,10},{9,11},{10,... | collective-permute-start | bytes 786440 | tf_op jit(solution)/shard_map/ppermute | solution.py:515
  59.8 12.3 %collective-permute-start.13 = (bf16[128,1024]{1,0:T(8,128)(2,1)S(1)}, bf16[128,1024]{1,0:T(8,128)(2,1)S(1)}, u32[]{:S(2)}, u32[]{:S(2)}) collective-permute-start(bf16[128,1024]{1,0:T(8,128)(2,1)S(1)} %add_convert_fusion.1), channel_id=1, source_target_pairs={{0,2},{1,3},{2,0},{3,1},{4,6},{5,7},{6,4},{7,5},{8,10},{9,11},{10,... | collective-permute-start | bytes 786440 | tf_op jit(solution)/shard_map/ppermute | solution.py:515
  (2 other events, 13.1 us)
